TPU v7x, 128 devices: a whole 4x4x4 slice. The times are simulated.
128 devices in a mesh: section: 2 (over x_hi), dp: 16 (over y, x_lo, core), tensor: 4 (over z).
Axes of the slice: x: 4 (x_hi: 2, x_lo: 2; x = x_hi * 2 + x_lo), y: 4, z: 4, core: 2. Of those that a mesh axis runs over, the one named last changes fastest.
Arguments:
- inputs: bfloat16 [2, 8192, 768], P(None, 'dp'), may hold values from -6 to 6
- cotangent: bfloat16 [2, 8192, 768], P(None, 'dp'), may hold values from -6 to 6
- seq_lengths: int32 [2, 16, 4], P(None, 'dp'), may hold values from 0 to 512, as said below
- w_qkv: bfloat16 [2, 768, 3, 768], P('section', 'dp', None, 'tensor'), may hold values from -0.21875 to 0.21875
- b_qkv: float32 [2, 3, 768], P('section', None, 'tensor'), may hold values from -1.8 to 1.8
- w_attn_out: bfloat16 [2, 768, 768], P('section', 'tensor', 'dp'), may hold values from -0.625 to 0.625
- w_in: bfloat16 [2, 768, 3072], P('section', 'dp', 'tensor'), may hold values from -0.21875 to 0.21875
- b_in: float32 [2, 3072], P('section', 'tensor'), may hold values from -1.8 to 1.8
- w_out: bfloat16 [2, 3072, 768], P('section', 'tensor', 'dp'), may hold values from -0.109375 to 0.109375
- b_out: float32 [2, 768], P('section'), may hold values from -1.8 to 1.8
- norm_gains: float32 [2, 2, 768], P('section'), may hold values from 0.5 to 1.5
- norm_biases: float32 [2, 2, 768], P('section'), may hold values from -1.8 to 1.8
Outputs:
- section_out: bfloat16 [2, 2, 8192, 768], P('section', None, 'dp', 'tensor')
- input_grads: bfloat16 [2, 2, 8192, 768], P('section', None, 'dp', 'tensor')
- grad_w_qkv: float32 [2, 768, 3, 768], P('section', 'dp', None, 'tensor')
- grad_b_qkv: float32 [2, 3, 768], P('section', None, 'tensor')
- grad_w_attn_out: float32 [2, 768, 768], P('section', 'tensor', 'dp')
- grad_w_in: float32 [2, 768, 3072], P('section', 'dp', 'tensor')
- grad_b_in: float32 [2, 3072], P('section', 'tensor')
- grad_w_out: float32 [2, 3072, 768], P('section', 'tensor', 'dp')
- grad_b_out: float32 [2, 768], P('section')
- grad_norm_gains: float32 [2, 2, 768], P('section')
- grad_norm_biases: float32 [2, 2, 768], P('section')
Inputs may be any that keep to these rules, and one draw needn't show every extreme that they name: `seq_lengths`: sequence j of a slot takes ceil(length / 128) blocks, all sequences of a slot together at most 4 blocks; zero lengths (absent sequences) stand after all others; in every micro-batch one data group's slot holds a single sequence of 512 tokens.
All inputs are finite; a program needn't handle non-finite values.
Results may differ from a plain program's by a relative error of at most 0.023.
Values may be sent and summed in bfloat16 or wider, within the bound.
A program may use at most 128 MiB of HBM per device.

v0:
```python
import math

import jax
import jax.numpy as jnp
from jax import lax
from jax.sharding import PartitionSpec as P

HD = 64
ROT = 16
BLOCK = 128
SEQS = 4
SLOT = 512


EPSILON = 1e-05
MASKED = -1e30


def from_behind(shard, axis, by):
    peers = lax.axis_size(axis)
    pairs = [(i, i + by) for i in range(peers) if 0 <= i + by < peers]
    return lax.ppermute(shard, axis, pairs)


def layer_norm(values, gain, shift_term):
    average = jnp.mean(values, axis=-1, keepdims=True)
    centred = values - average
    spread = jnp.mean(centred * centred, axis=-1, keepdims=True)
    return centred * lax.rsqrt(spread + EPSILON) * gain + shift_term


def norm_terms(values, grad):
    average = jnp.mean(values, axis=-1, keepdims=True)
    centred = values - average
    spread = jnp.mean(centred * centred, axis=-1, keepdims=True)
    normal = centred * lax.rsqrt(spread + EPSILON)
    return (jnp.sum(grad * normal, axis=0), jnp.sum(grad, axis=0))


def gelu_exact(values):
    return jax.nn.gelu(values, approximate=False)


def arrange(lengths):
    blocks = (lengths + BLOCK - 1) // BLOCK
    block_ends = jnp.cumsum(blocks)
    places = jnp.arange(SLOT, dtype=jnp.int32)
    owners = jnp.sum((block_ends[None, :] <= (places // BLOCK)[:, None]).astype(jnp.int32), axis=1)
    starts = jnp.concatenate([jnp.zeros((1,), jnp.int32), block_ends]) * BLOCK
    limits = jnp.concatenate([lengths, jnp.zeros((1,), jnp.int32)])
    chosen = (owners[:, None] == jnp.arange(SEQS + 1, dtype=jnp.int32)[None, :]).astype(jnp.int32)
    offset = places - jnp.sum(chosen * starts[None, :], axis=1)
    seq_len = jnp.sum(chosen * limits[None, :], axis=1)
    allowed = (
        (owners[:, None] == owners[None, :])
        & (offset[None, :] <= offset[:, None])
        & ((offset[None, :] < seq_len[None, :]) | (places[:, None] == places[None, :]))
    )
    half_rot = ROT // 2
    inv_freq = 1.0 / 10000.0 ** (jnp.arange(half_rot, dtype=jnp.float32) * 2.0 / ROT)
    angles = offset.astype(jnp.float32)[:, None] * inv_freq[None, :]
    return (jnp.cos(angles), jnp.sin(angles), allowed)


def rotate(values, cosines, sines):
    half_rot = ROT // 2
    cos_rows = cosines[:, None, :]
    sin_rows = sines[:, None, :]
    first = values[..., :half_rot]
    second = values[..., half_rot:ROT]
    return jnp.concatenate(
        [
            first * cos_rows - second * sin_rows,
            second * cos_rows + first * sin_rows,
            values[..., ROT:],
        ],
        axis=-1,
    )


def body(
    inputs,
    cotangent,
    seq_lengths,
    w_qkv,
    b_qkv,
    w_attn_out,
    w_in,
    b_in,
    w_out,
    b_out,
    norm_gains,
    norm_biases,
):
    section_no = lax.axis_index("section")
    tensor_no = lax.axis_index("tensor")
    micro_count = inputs.shape[0]
    slot_len = inputs.shape[1]
    model_width = inputs.shape[2]
    out_cols = model_width // lax.axis_size("tensor")
    rows_share = slot_len // lax.axis_size("tensor")
    qkv_full, attn_full, in_full, out_full = (
        lax.all_gather(w_qkv[0], "dp", axis=0, tiled=True),
        lax.all_gather(w_attn_out[0], "dp", axis=1, tiled=True),
        lax.all_gather(w_in[0], "dp", axis=0, tiled=True),
        lax.all_gather(w_out[0], "dp", axis=1, tiled=True),
    )
    local_heads = qkv_full.shape[2] // HD
    qkv_mat = qkv_full.reshape(model_width, -1)
    qkv_bias = b_qkv[0].reshape(-1)
    in_bias = b_in[0]
    out_bias = b_out[0]
    gains = norm_gains[0]
    shifts = norm_biases[0]
    scale_factor = 1.0 / math.sqrt(HD)

    def row_slice(values):
        return lax.dynamic_slice_in_dim(values, tensor_no * rows_share, rows_share, 0)

    length_rows = seq_lengths[:, 0]
    received = jnp.zeros((slot_len, model_width), jnp.bfloat16)
    outputs_by_moment = []
    kept_by_moment = []
    for moment in range(micro_count + 1):
        own_rows = inputs[min(moment, micro_count - 1)]
        acts_in = jnp.where(section_no == 0, own_rows, received)
        micro_no = jnp.clip(moment - section_no, 0, micro_count - 1)
        lengths = lax.dynamic_index_in_dim(length_rows, micro_no, 0, keepdims=False)
        forward_acts = acts_in.astype(jnp.float32)
        forward_cosines, forward_sines, forward_allowed = arrange(lengths)
        forward_normed = layer_norm(forward_acts, gains[0], shifts[0]).astype(jnp.bfloat16)
        pre = (
            jnp.dot(forward_normed, qkv_mat, preferred_element_type=jnp.float32) + qkv_bias
        ).reshape(slot_len, 3, local_heads, HD)
        forward_query = rotate(pre[:, 0], forward_cosines, forward_sines).astype(jnp.bfloat16)
        forward_key_rot = rotate(pre[:, 1], forward_cosines, forward_sines).astype(jnp.bfloat16)
        forward_value = pre[:, 2].astype(jnp.bfloat16)
        forward_scores = (
            jnp.einsum(
                "qhd,khd->hqk", forward_query, forward_key_rot, preferred_element_type=jnp.float32
            )
            * scale_factor
        )
        masked = jnp.where(forward_allowed[None], forward_scores, MASKED)
        top_score = jnp.max(masked, axis=-1, keepdims=True)
        weights = jnp.where(forward_allowed[None], jnp.exp(masked - top_score), 0.0)
        totals = jnp.sum(weights, axis=-1, keepdims=True)
        forward_log_total = top_score + jnp.log(totals)
        probs = (weights / totals).astype(jnp.bfloat16)
        forward_mixed = (
            jnp.einsum("hqk,khd->qhd", probs, forward_value, preferred_element_type=jnp.float32)
            .reshape(slot_len, -1)
            .astype(jnp.bfloat16)
        )
        forward_normed_two = layer_norm(forward_acts, gains[1], shifts[1]).astype(jnp.bfloat16)
        forward_hidden = (
            jnp.dot(forward_normed_two, in_full, preferred_element_type=jnp.float32) + in_bias
        )
        forward_activated = gelu_exact(forward_hidden).astype(jnp.bfloat16)
        partial_sum = jnp.dot(
            forward_mixed, attn_full, preferred_element_type=jnp.float32
        ) + jnp.dot(forward_activated, out_full, preferred_element_type=jnp.float32)
        summed = lax.psum(partial_sum.astype(jnp.bfloat16), "tensor").astype(jnp.float32)
        result = acts_in.astype(jnp.float32) + summed + out_bias
        forward_kept = (
            acts_in,
            forward_normed,
            forward_query,
            forward_key_rot,
            forward_value,
            forward_log_total,
            forward_mixed,
            forward_normed_two,
            forward_hidden,
            forward_activated,
        )
        result, kept = (result, forward_kept)
        result_bf = result.astype(jnp.bfloat16)
        outputs_by_moment.append(result_bf)
        kept_by_moment.append(kept)
        if moment < micro_count:
            received = from_behind(result_bf, "section", 1)
    sent = jnp.zeros((slot_len, model_width), jnp.bfloat16)
    weight_sums = None
    vector_sums = None
    grads_by_moment = []
    for moment in range(micro_count + 1):
        micro_no = moment - 1 + section_no
        valid = (micro_no >= 0) & (micro_no < micro_count)
        index_no = jnp.clip(micro_no, 0, micro_count - 1)
        lengths = lax.dynamic_index_in_dim(length_rows, index_no, 0, keepdims=False)
        own_grad = cotangent[min(moment, micro_count - 1)]
        grad_in = jnp.where(section_no == 1, own_grad, sent)
        kept = jax.tree.map(
            lambda earlier, latter: jnp.where(section_no == 0, earlier, latter),
            kept_by_moment[max(moment - 1, 0)],
            kept_by_moment[min(moment + 1, micro_count)],
        )
        acts_bf, normed, query, key_rot, value, log_total, mixed, normed_two, hidden, activated = (
            kept
        )
        acts = acts_bf.astype(jnp.float32)
        grad_f = grad_in.astype(jnp.float32)
        cosines, sines, allowed = arrange(lengths)
        g_out_bias = jnp.sum(grad_f, axis=0)
        g_attn = jnp.dot(mixed.T, grad_in, preferred_element_type=jnp.float32)
        grad_mixed = (
            jnp.dot(grad_in, attn_full.T, preferred_element_type=jnp.float32)
            .astype(jnp.bfloat16)
            .reshape(slot_len, local_heads, HD)
        )
        g_out = jnp.dot(activated.T, grad_in, preferred_element_type=jnp.float32)
        grad_act = jnp.dot(grad_in, out_full.T, preferred_element_type=jnp.float32)
        gelu_pull = jax.vjp(gelu_exact, hidden)[1]
        grad_hidden = gelu_pull(grad_act)[0].astype(jnp.bfloat16)
        g_in_bias = jnp.sum(grad_hidden.astype(jnp.float32), axis=0)
        g_in = jnp.dot(normed_two.T, grad_hidden, preferred_element_type=jnp.float32)
        grad_norm_two = jnp.dot(grad_hidden, in_full.T, preferred_element_type=jnp.float32)
        scores = (
            jnp.einsum("qhd,khd->hqk", query, key_rot, preferred_element_type=jnp.float32)
            * scale_factor
        )
        probs_f = jnp.where(
            allowed[None], jnp.exp(jnp.where(allowed[None], scores - log_total, 0.0)), 0.0
        )
        grad_probs = jnp.einsum(
            "qhd,khd->hqk", grad_mixed, value, preferred_element_type=jnp.float32
        )
        row_dot = jnp.sum(probs_f * grad_probs, axis=-1, keepdims=True)
        grad_scores = (probs_f * (grad_probs - row_dot)).astype(jnp.bfloat16)
        grad_query = (
            jnp.einsum("hqk,khd->qhd", grad_scores, key_rot, preferred_element_type=jnp.float32)
            * scale_factor
        )
        grad_key = (
            jnp.einsum("hqk,qhd->khd", grad_scores, query, preferred_element_type=jnp.float32)
            * scale_factor
        )
        grad_value = jnp.einsum(
            "hqk,qhd->khd",
            probs_f.astype(jnp.bfloat16),
            grad_mixed,
            preferred_element_type=jnp.float32,
        )
        grad_pre = jnp.stack(
            [rotate(grad_query, cosines, -sines), rotate(grad_key, cosines, -sines), grad_value],
            axis=1,
        )
        grad_pre = grad_pre.reshape(slot_len, -1).astype(jnp.bfloat16)
        g_qkv_bias = jnp.sum(grad_pre.astype(jnp.float32), axis=0).reshape(3, -1)
        g_qkv = jnp.dot(normed.T, grad_pre, preferred_element_type=jnp.float32).reshape(
            model_width, 3, -1
        )
        grad_normed = jnp.dot(grad_pre, qkv_mat.T, preferred_element_type=jnp.float32)
        norm_pull_one = jax.vjp(layer_norm, acts, gains[0], shifts[0])[1]
        norm_pull_two = jax.vjp(layer_norm, acts, gains[1], shifts[1])[1]
        grad_normed, grad_norm_two = (
            lax.psum(grad_normed.astype(jnp.bfloat16), "tensor").astype(jnp.float32),
            lax.psum(grad_norm_two.astype(jnp.bfloat16), "tensor").astype(jnp.float32),
        )
        back_one = norm_pull_one(grad_normed)
        back_two = norm_pull_two(grad_norm_two)
        grad_acts = grad_in.astype(jnp.float32) + back_one[0] + back_two[0]
        acts_part = row_slice(acts)
        one_terms = norm_terms(acts_part, row_slice(grad_normed))
        two_terms = norm_terms(acts_part, row_slice(grad_norm_two))
        g_gains = jnp.stack([one_terms[0], two_terms[0]])
        g_shifts = jnp.stack([one_terms[1], two_terms[1]])
        grad_acts, weight_terms, vector_terms = (
            grad_acts,
            (g_qkv, g_attn, g_in, g_out),
            (g_qkv_bias, g_in_bias, g_out_bias, g_gains, g_shifts),
        )
        weight_terms = jax.tree.map(lambda term: jnp.where(valid, term, 0.0), weight_terms)
        vector_terms = jax.tree.map(lambda term: jnp.where(valid, term, 0.0), vector_terms)
        grad_out_bf = grad_acts.astype(jnp.bfloat16)
        grads_by_moment.append(grad_out_bf)
        if moment < micro_count:
            sent = from_behind(grad_out_bf, "section", -1)
        if weight_sums is None:
            weight_sums = tuple(weight_terms)
            vector_sums = tuple(vector_terms)
        else:
            weight_sums = tuple((total + term for total, term in zip(weight_sums, weight_terms)))
            vector_sums = tuple((total + term for total, term in zip(vector_sums, vector_terms)))
    weight_sums = (
        lax.psum_scatter(
            weight_sums[0].astype(jnp.bfloat16), "dp", scatter_dimension=0, tiled=True
        ).astype(jnp.float32),
        lax.psum_scatter(
            weight_sums[1].astype(jnp.bfloat16), "dp", scatter_dimension=1, tiled=True
        ).astype(jnp.float32),
        lax.psum_scatter(
            weight_sums[2].astype(jnp.bfloat16), "dp", scatter_dimension=0, tiled=True
        ).astype(jnp.float32),
        lax.psum_scatter(
            weight_sums[3].astype(jnp.bfloat16), "dp", scatter_dimension=1, tiled=True
        ).astype(jnp.float32),
    )
    qkv_bias_grad, in_bias_grad, out_bias_grad = lax.psum(
        (vector_sums[0], vector_sums[1], vector_sums[2]), "dp"
    )
    gains_grad, shifts_grad = lax.psum((vector_sums[3], vector_sums[4]), ("dp", "tensor"))
    out_rows = jnp.stack(
        [
            jnp.where(
                section_no == 0, outputs_by_moment[which_micro], outputs_by_moment[which_micro + 1]
            )
            for which_micro in range(micro_count)
        ]
    )
    grad_rows_all = jnp.stack(
        [
            jnp.where(
                section_no == 0, grads_by_moment[which_micro + 1], grads_by_moment[which_micro]
            )
            for which_micro in range(micro_count)
        ]
    )
    section_out = lax.dynamic_slice_in_dim(out_rows, tensor_no * out_cols, out_cols, 2)
    input_grads = lax.dynamic_slice_in_dim(grad_rows_all, tensor_no * out_cols, out_cols, 2)
    return (
        section_out[None],
        input_grads[None],
        weight_sums[0][None],
        qkv_bias_grad[None],
        weight_sums[1][None],
        weight_sums[2][None],
        in_bias_grad[None],
        weight_sums[3][None],
        out_bias_grad[None],
        gains_grad[None],
        shifts_grad[None],
    )


def solution(mesh):
    return jax.shard_map(
        body,
        mesh=mesh,
        in_specs=(
            P(None, "dp", None),
            P(None, "dp", None),
            P(None, "dp", None),
            P("section", "dp", None, "tensor"),
            P("section", None, "tensor"),
            P("section", "tensor", "dp"),
            P("section", "dp", "tensor"),
            P("section", "tensor"),
            P("section", "tensor", "dp"),
            P("section", None),
            P("section", None, None),
            P("section", None, None),
        ),
        out_specs=(
            P("section", None, "dp", "tensor"),
            P("section", None, "dp", "tensor"),
            P("section", "dp", None, "tensor"),
            P("section", None, "tensor"),
            P("section", "tensor", "dp"),
            P("section", "dp", "tensor"),
            P("section", "tensor"),
            P("section", "tensor", "dp"),
            P("section", None),
            P("section", None, None),
            P("section", None, None),
        ),
        check_vma=False,
    )
```

profile of v0, /device:TPU:0, one launch (start us, length us, event | category | flops | bytes accessed | tf_op | source)
XLA Modules:
  0.0 942.8 jit_solution(1543063323264973970)
XLA Ops:
  12.1 28.0 %all-gather = bf16[1,768,3,192]{3,1,2,0:T(8,128)(2,1)S(1)} all-gather(bf16[1,48,3,192]{3,1,2,0:T(8,128)(2,1)} %param.15), channel_id=2, replica_groups=mesh['section'=2,'dp'=16,'tensor'=4] {'dp'}, dimensions={1}, use_global_device_ids=true | all-gather | bytes 940032 | tf_op jit(solution)/shard_map/all_gather | solution.py:103
  43.3 2.0 convolution_add_fusion.5
  56.1 18.0 %all-gather.1 = bf16[1,192,768]{1,2,0:T(8,128)(2,1)S(1)} all-gather(bf16[1,192,48]{1,2,0:T(8,128)(2,1)S(1)} %copy-done.138), channel_id=3, replica_groups=mesh['section'=2,'dp'=16,'tensor'=4] {'dp'}, dimensions={2}, use_global_device_ids=true | all-gather | bytes 313344 | tf_op jit(solution)/shard_map/all_gather | solution.py:104
  74.1 2.2 fusion.161
  76.3 1.6 fusion.224
  77.9 6.4 fusion.43
  84.4 3.8 add_convert_fusion.5
  89.5 45.2 %all-reduce.10.cloned.1.call-done = bf16[512,768]{1,0:T(8,128)(2,1)} async-done(((bf16[512,768]{1,0:T(8,128)(2,1)}), bf16[512,768]{1,0:T(8,128)(2,1)}) %all-reduce.10.cloned.1.call-update) | async-done | bytes 786448 | tf_op jit(solution)/shard_map/psum | solution.py:163
  134.7 1.4 fusion.40
  136.1 6.0 collective-permute-start
  144.0 1.6 convolution_convert_fusion.8
  145.6 10.5 %collective-permute-done = bf16[512,768]{1,0:T(8,128)(2,1)} collective-permute-done((bf16[512,768]{1,0:T(8,128)(2,1)S(1)}, bf16[512,768]{1,0:T(8,128)(2,1)}, u32[]{:S(2)}, u32[]{:S(2)}) %collective-permute-start) | collective-permute-done | bytes 786464 | tf_op jit(solution)/shard_map/ppermute | solution.py:22
  156.1 1.4 fusion.327
  162.5 1.8 broadcast_select_fusion.1
  164.5 1.8 fusion.235
  172.5 1.7 convolution_convert_fusion.5
  174.3 4.5 fusion.48
  178.8 4.9 convert_reduce_fusion.8
  183.7 1.7 convolution_convert_fusion.2
  185.4 1.7 add_convert_fusion.4
  188.1 1.8 fusion.172
  189.9 1.8 fusion.173
  192.8 1.7 multiply_reduce_fusion.20
  196.7 2.2 fusion.185
  199.0 3.0 fusion.183
  201.9 51.5 %all-reduce.16.cloned.1.call-done = (bf16[512,768]{1,0:T(8,128)(2,1)}, bf16[512,768]{1,0:T(8,128)(2,1)}, bf16[512,768]{1,0:T(8,128)(2,1)}) async-done(((bf16[512,768]{1,0:T(8,128)(2,1)}, bf16[512,768]{1,0:T(8,128)(2,1)}, bf16[512,768]{1,0:T(8,128)(2,1)}), (bf16[512,768]{1,0:T(8,128)(2,1)}, bf16[512,768]{1,0:T(8,128)(2,1)}, bf16[512,768]{1,0:T(8,128)(2,1)})) %all-reduce.16.cloned.1.call-update) | async-done | bytes 2359312 | tf_op jit(solution)/shard_map/psum | solution.py:163
  253.4 2.8 select_bitcast_fusion.1
  256.2 4.9 collective-permute-start.1
  265.9 11.7 %collective-permute-done.1 = bf16[512,768]{1,0:T(8,128)(2,1)S(1)} collective-permute-done((bf16[512,768]{1,0:T(8,128)(2,1)S(1)}, bf16[512,768]{1,0:T(8,128)(2,1)S(1)}, u32[]{:S(2)}, u32[]{:S(2)}) %collective-permute-start.1) | collective-permute-done | bytes 786464 | tf_op jit(solution)/shard_map/ppermute | solution.py:22
  281.2 5.9 collective-permute-done.2
  288.3 1.7 fusion.233
  299.0 1.7 convolution_convert_fusion.4
  300.8 5.2 fusion.53
  306.0 5.0 convert_reduce_fusion.7
  311.9 1.7 convolution_convert_fusion.1
  313.7 2.6 fusion.326
  317.2 2.2 fusion.159
  321.5 40.5 %all-reduce.14.cloned.1.call-done = (bf16[512,768]{1,0:T(8,128)(2,1)}, bf16[512,768]{1,0:T(8,128)(2,1)}) async-done(((bf16[512,768]{1,0:T(8,128)(2,1)}, bf16[512,768]{1,0:T(8,128)(2,1)}), (bf16[512,768]{1,0:T(8,128)(2,1)}, bf16[512,768]{1,0:T(8,128)(2,1)})) %all-reduce.14.cloned.1.call-update) | async-done | bytes 1572880 | tf_op jit(solution)/shard_map/psum | solution.py:258
  362.0 2.6 multiply_reduce_fusion.7
  365.7 2.9 select_bitcast_fusion
  368.7 2.0 collective-permute-start.3
  371.1 1.7 add_convert_fusion.3
  372.9 3.0 fusion.181
  375.9 15.5 %collective-permute-done.3 = bf16[512,768]{1,0:T(8,128)(2,1)S(1)} collective-permute-done((bf16[512,768]{1,0:T(8,128)(2,1)S(1)}, bf16[512,768]{1,0:T(8,128)(2,1)S(1)}, u32[]{:S(2)}, u32[]{:S(2)}) %collective-permute-start.3) | collective-permute-done | bytes 786464 | tf_op jit(solution)/shard_map/ppermute | solution.py:22
  393.0 1.9 fusion.231
  406.4 4.3 add_convert_fusion.2
  411.0 3.2 convolution_convert_fusion.3
  414.2 5.8 convert_reduce_fusion.6
  420.8 1.7 convolution_convert_fusion
  423.2 4.1 fusion.197
  434.1 2.0 add_convert_fusion
  436.2 2.4 copy.129
  440.1 3.9 fusion.195
  445.7 4.3 add_convert_fusion.1
  450.0 31.2 %all-reduce.1 = (f32[1,3,192]{2,0,1:T(1,128)}, f32[1,768]{1,0:T(1,128)}, f32[1,768]{1,0:T(1,128)}) all-reduce(f32[1,3,192]{2,0,1:T(1,128)S(1)} %broadcast_in_dim.197, f32[1,768]{1,0:T(1,128)S(1)} %broadcast_in_dim.205, f32[1,768]{1,0:T(1,128)S(1)} %broadcast_in_dim.208), channel_id=1, replica_groups=mesh['section'=2,'dp'=16,'tensor'=4] {'dp'}, use_global_device_ids=true, to_apply=%region_70.71 | all-reduce | flops 2112 | bytes 16896 | tf_op jit(solution)/shard_map/psum | solution.py:300
  482.5 41.7 %reduce-scatter.7.cloned.1.call-done = bf16[48,3,192]{2,0,1:T(8,128)(2,1)} async-done(((bf16[768,3,192]{2,0,1:T(8,128)(2,1)}), bf16[48,3,192]{2,0,1:T(8,128)(2,1)}) %reduce-scatter.7.cloned.1.call-update) | async-done | bytes 55312 | tf_op jit(solution)/shard_map/reduce_scatter | solution.py:287
  524.3 1.6 bitcast_convert_fusion.2
  525.8 63.3 %all-reduce.12.cloned.1.call-done = (bf16[512,768]{1,0:T(8,128)(2,1)}, bf16[512,768]{1,0:T(8,128)(2,1)}, bf16[512,768]{1,0:T(8,128)(2,1)}) async-done(((bf16[512,768]{1,0:T(8,128)(2,1)}, bf16[512,768]{1,0:T(8,128)(2,1)}, bf16[512,768]{1,0:T(8,128)(2,1)}), (bf16[512,768]{1,0:T(8,128)(2,1)}, bf16[512,768]{1,0:T(8,128)(2,1)}, bf16[512,768]{1,0:T(8,128)(2,1)})) %all-reduce.12.cloned.1.call-update) | async-done | bytes 2359312 | tf_op jit(solution)/shard_map/psum | solution.py:163
  589.1 1.5 fusion.177
  591.7 2.0 copy.90
  595.9 2.6 fusion.330
  599.7 53.5 %reduce-scatter.13.cloned.1.call-done = bf16[48,768]{1,0:T(8,128)(2,1)} async-done(((bf16[768,768]{1,0:T(8,128)(2,1)}), bf16[48,768]{1,0:T(8,128)(2,1)}) %reduce-scatter.13.cloned.1.call-update) | async-done | bytes 73744
  656.6 277.6 %all-reduce = (f32[1,2,768]{2,1,0:T(2,128)}, f32[1,2,768]{2,1,0:T(2,128)}) all-reduce(f32[1,2,768]{2,1,0:T(2,128)S(1)} %fusion.247, f32[1,2,768]{2,1,0:T(2,128)S(1)} %fusion.250), channel_id=1, replica_groups=mesh['section'=2,'dp'=16,'tensor'=4] {'dp','tensor'}, use_global_device_ids=true, to_apply=%region_94.95 | all-reduce | flops 3072 | bytes 24576 | tf_op jit(solution)/shard_map/psum | solution.py:303
  934.2 1.6 bitcast_convert_fusion.1
  (662 shorter events, 93.8 us)
Async XLA Ops:
  7.2 70.7 %all-gather.7.cloned.1.call-start = ((), (), s32[]{:S(2)}) async-start(), calls=%async_computation.8 | async-start | bytes 1253376 | tf_op jit(solution)/shard_map/all_gather | solution.py:105
  7.9 76.4 %all-gather.9.cloned.1.call-start = ((), (), s32[]{:S(2)}) async-start(), calls=%async_computation.9 | async-start | bytes 1253376 | tf_op jit(solution)/shard_map/all_gather | solution.py:106
  8.7 126.0 %all-reduce.10.cloned.1.call-start = ((), (), s32[]{:S(2)}) async-start(), calls=%async_computation.4 | async-start | bytes 1572864 | tf_op jit(solution)/shard_map/psum | solution.py:163
  11.8 33.7 %copy-start.129 = (s32[512]{0:T(512)}, s32[512]{0:T(512)S(1)}, u32[]{:S(2)}) copy-start(s32[512]{0:T(512)S(1)} %get-tuple-element.88) | copy-start | bytes 6148
  11.8 38.3 %copy-start.130 = (s32[512]{0:T(512)}, s32[512]{0:T(512)S(1)}, u32[]{:S(2)}) copy-start(s32[512]{0:T(512)S(1)} %get-tuple-element.92) | copy-start | bytes 6148
  12.0 29.4 %copy-start.168 = (f32[1,2,768]{2,1,0:T(2,128)S(1)}, f32[1,2,768]{2,1,0:T(2,128)}, u32[]{:S(2)}) copy-start(f32[1,2,768]{2,1,0:T(2,128)} %param.23) | copy-start | bytes 18436
  12.1 30.0 %copy-start.169 = (f32[1,2,768]{2,1,0:T(2,128)S(1)}, f32[1,2,768]{2,1,0:T(2,128)}, u32[]{:S(2)}) copy-start(f32[1,2,768]{2,1,0:T(2,128)} %param.22) | copy-start | bytes 18436
  12.1 30.0 %copy-start.2 = (bf16[2,512,768]{2,1,0:T(8,128)(2,1)S(1)}, bf16[2,512,768]{2,1,0:T(8,128)(2,1)}, u32[]{:S(2)}) copy-start(bf16[2,512,768]{2,1,0:T(8,128)(2,1)} %param.12) | copy-start | bytes 4718596
  45.3 9.9 %copy-start.34 = (f32[512,576]{0,1:T(8,128)}, f32[512,576]{0,1:T(8,128)S(1)}, u32[]{:S(2)}) copy-start(f32[512,576]{0,1:T(8,128)S(1)} %convolution_add_fusion.5) | copy-start | bytes 3538948
  45.3 6.1 copy-start.188
  45.4 6.0 copy-start.59
  45.4 6.7 copy-start.58
  45.5 9.7 %copy-start.39 = (bf16[512,3,48]{0,2,1:T(8,128)(2,1)}, bf16[512,3,48]{0,2,1:T(8,128)(2,1)S(1)}, u32[]{:S(2)}) copy-start(bf16[512,3,48]{0,2,1:T(8,128)(2,1)S(1)} %slice.434) | copy-start | bytes 442372
  47.7 7.5 copy-start.141
  56.1 20.1 %copy-start.109 = (f32[3,512]{1,0:T(4,128)}, f32[3,512]{1,0:T(4,128)S(1)}, u32[]{:S(2)}) copy-start(f32[3,512]{1,0:T(4,128)S(1)} %fusion.3) | copy-start | bytes 18436
  76.3 8.1 copy-start.67
  88.2 53.9 %copy-start.146 = (s32[512]{0:T(512)S(1)}, s32[512]{0:T(512)}, u32[]{:S(2)}) copy-start(s32[512]{0:T(512)} %copy-done.145) | copy-start | bytes 6148
  88.2 53.9 %copy-start.165 = (s32[512]{0:T(512)S(1)}, s32[512]{0:T(512)}, u32[]{:S(2)}) copy-start(s32[512]{0:T(512)} %get-tuple-element.94) | copy-start | bytes 6148
  88.2 165.2 %all-reduce.16.cloned.1.call-start = ((), (), s32[]{:S(2)}) async-start(), calls=%async_computation.13 | async-start | bytes 4718592 | tf_op jit(solution)/shard_map/psum | solution.py:163
  88.3 55.7 %copy-start.126 = (f32[768]{0:T(1024)}, f32[768]{0:T(1024)S(1)}, u32[]{:S(2)}) copy-start(f32[768]{0:T(1024)S(1)} %reduce.9) | copy-start | bytes 9220
  136.1 9.5 %copy-start.25 = (bf16[512,768]{1,0:T(8,128)(2,1)}, bf16[512,768]{1,0:T(8,128)(2,1)S(1)}, u32[]{:S(2)}) copy-start(bf16[512,768]{1,0:T(8,128)(2,1)S(1)} %fusion.40) | copy-start | bytes 2359300
  136.1 20.0 %collective-permute-start = (bf16[512,768]{1,0:T(8,128)(2,1)S(1)}, bf16[512,768]{1,0:T(8,128)(2,1)}, u32[]{:S(2)}, u32[]{:S(2)}) collective-permute-start(bf16[512,768]{1,0:T(8,128)(2,1)S(1)} %fusion.40), channel_id=1, source_target_pairs={{0,64},{1,65},{2,66},{3,67},{4,68},{5,69},{6,70},{7,71},{8,72},{9,... | collective-permute-start | bytes 2359304 | tf_op jit(solution)/shard_map/ppermute | solution.py:22
  157.7 16.5 %copy-start.157 = (f32[512]{0:T(512)}, f32[512]{0:T(512)S(1)}, u32[]{:S(2)}) copy-start(f32[512]{0:T(512)S(1)} %broadcast_multiply_fusion.4) | copy-start | bytes 6148
  158.7 15.5 %copy-start.197 = (f32[512]{0:T(512)}, f32[512]{0:T(512)S(1)}, u32[]{:S(2)}) copy-start(f32[512]{0:T(512)S(1)} %add_rsqrt_fusion.1) | copy-start | bytes 6148
  159.7 10.0 %copy-start.45 = (bf16[512,3,48]{0,2,1:T(8,128)(2,1)}, bf16[512,3,48]{0,2,1:T(8,128)(2,1)S(1)}, u32[]{:S(2)}) copy-start(bf16[512,3,48]{0,2,1:T(8,128)(2,1)S(1)} %slice.432) | copy-start | bytes 442372
  159.7 9.3 copy-start.47
  160.4 8.7 copy-start.97
  160.4 8.7 copy-start.99
  160.4 9.3 copy-start.81
  160.4 9.3 copy-start.83
  164.4 5.8 copy-start.70
  178.7 6.7 copy-start.212
  187.2 174.8 %all-reduce.14.cloned.1.call-start = ((), (), s32[]{:S(2)}) async-start(), calls=%async_computation.12 | async-start | bytes 3145728 | tf_op jit(solution)/shard_map/psum | solution.py:258
  187.2 8.0 copy-start.18
  187.2 8.0 copy-start.211
  253.4 7.6 copy-start.5
  253.4 7.7 copy-start.7
  253.4 7.7 copy-start.128
  256.2 6.8 copy-start.23
  256.2 21.4 %collective-permute-start.1 = (bf16[512,768]{1,0:T(8,128)(2,1)S(1)}, bf16[512,768]{1,0:T(8,128)(2,1)S(1)}, u32[]{:S(2)}, u32[]{:S(2)}) collective-permute-start(bf16[512,768]{1,0:T(8,128)(2,1)S(1)} %get-tuple-element.138), channel_id=1, source_target_pairs={{0,64},{1,65},{2,66},{3,67},{4,68},{5,69},{6,70},{7,71},{8,72},{9,... | collective-permute-start | bytes 2359304 | tf_op jit(solution)/shard_map/ppermute | solution.py:22
  263.3 14.3 %copy-start.3 = (bf16[2,512,768]{2,1,0:T(8,128)(2,1)S(1)}, bf16[2,512,768]{2,1,0:T(8,128)(2,1)}, u32[]{:S(2)}) copy-start(bf16[2,512,768]{2,1,0:T(8,128)(2,1)} %param.12) | copy-start | bytes 4718596
  264.6 14.4 %copy-start.31 = (bf16[512,768]{1,0:T(8,128)(2,1)}, bf16[512,768]{1,0:T(8,128)(2,1)S(1)}, u32[]{:S(2)}) copy-start(bf16[512,768]{1,0:T(8,128)(2,1)S(1)} %fusion.34) | copy-start | bytes 2359300
  264.6 22.4 %collective-permute-start.2 = (bf16[512,768]{1,0:T(8,128)(2,1)S(1)}, bf16[512,768]{1,0:T(8,128)(2,1)S(1)}, u32[]{:S(2)}, u32[]{:S(2)}) collective-permute-start(bf16[512,768]{1,0:T(8,128)(2,1)S(1)} %fusion.34), channel_id=1, source_target_pairs={{64,0},{65,1},{66,2},{67,3},{68,4},{69,5},{70,6},{71,7},{72,8},{73... | collective-permute-start | bytes 2359304 | tf_op jit(solution)/shard_map/ppermute | solution.py:22
  279.2 21.6 %copy-start.160 = (f32[512]{0:T(512)}, f32[512]{0:T(512)S(1)}, u32[]{:S(2)}) copy-start(f32[512]{0:T(512)S(1)} %broadcast_multiply_fusion.3) | copy-start | bytes 6148
  280.2 20.6 %copy-start.200 = (f32[512]{0:T(512)}, f32[512]{0:T(512)S(1)}, u32[]{:S(2)}) copy-start(f32[512]{0:T(512)S(1)} %add_rsqrt_fusion) | copy-start | bytes 6148
  281.0 7.3 copy-start.36
  281.1 15.5 %copy-start.49 = (bf16[512,3,48]{0,2,1:T(8,128)(2,1)}, bf16[512,3,48]{0,2,1:T(8,128)(2,1)S(1)}, u32[]{:S(2)}) copy-start(bf16[512,3,48]{0,2,1:T(8,128)(2,1)S(1)} %slice.430) | copy-start | bytes 442372
  281.2 14.8 %copy-start.51 = (bf16[512,3,48]{0,2,1:T(8,128)(2,1)}, bf16[512,3,48]{0,2,1:T(8,128)(2,1)S(1)}, u32[]{:S(2)}) copy-start(bf16[512,3,48]{0,2,1:T(8,128)(2,1)S(1)} %slice.431) | copy-start | bytes 442372
  290.1 5.9 copy-start.105
  290.1 5.9 copy-start.107
  290.1 6.5 copy-start.101
  290.1 6.5 copy-start.103
  313.7 167.5 %reduce-scatter.9.cloned.1.call-start = ((), (), s32[]{:S(2)}) async-start(), calls=%async_computation.6 | async-start | bytes 417792 | tf_op jit(solution)/shard_map/reduce_scatter | solution.py:290
  319.4 42.5 %copy-start.135 = (f32[512]{0:T(512)S(1)}, f32[512]{0:T(512)}, u32[]{:S(2)}) copy-start(f32[512]{0:T(512)} %broadcast_multiply_fusion.1) | copy-start | bytes 6148
  368.7 22.8 %collective-permute-start.3 = (bf16[512,768]{1,0:T(8,128)(2,1)S(1)}, bf16[512,768]{1,0:T(8,128)(2,1)S(1)}, u32[]{:S(2)}, u32[]{:S(2)}) collective-permute-start(bf16[512,768]{1,0:T(8,128)(2,1)S(1)} %get-tuple-element.136), channel_id=1, source_target_pairs={{64,0},{65,1},{66,2},{67,3},{68,4},{69,5},{70,6},{71,7},{72,8},{73... | collective-permute-start | bytes 2359304 | tf_op jit(solution)/shard_map/ppermute | solution.py:22
  372.9 18.6 %copy-start.20 = (bf16[2,512,768]{2,1,0:T(8,128)(2,1)S(1)}, bf16[2,512,768]{2,1,0:T(8,128)(2,1)}, u32[]{:S(2)}) copy-start(bf16[2,512,768]{2,1,0:T(8,128)(2,1)} %param.13) | copy-start | bytes 4718596
  392.5 8.9 copy-start.9
  402.6 121.7 %reduce-scatter.7.cloned.1.call-start = ((), (), s32[]{:S(2)}) async-start(), calls=%async_computation.5 | async-start | bytes 1253376 | tf_op jit(solution)/shard_map/reduce_scatter | solution.py:287
  410.7 178.3 %all-reduce.12.cloned.1.call-start = ((), (), s32[]{:S(2)}) async-start(), calls=%async_computation.11 | async-start | bytes 4718592 | tf_op jit(solution)/shard_map/psum | solution.py:163
  414.2 6.6 copy-start.206
  422.6 230.6 %reduce-scatter.13.cloned.1.call-start = ((), (), s32[]{:S(2)}) async-start(), calls=%async_computation.10 | async-start | bytes 1253376
  438.6 495.6 %reduce-scatter.11.cloned.1.call-start = ((), (), s32[]{:S(2)}) async-start(), calls=%async_computation.7 | async-start | bytes 1253376 | tf_op jit(solution)/shard_map/reduce_scatter | solution.py:293
  445.7 143.4 %copy-start.127 = (f32[768]{0:T(1024)S(1)}, f32[768]{0:T(1024)}, u32[]{:S(2)}) copy-start(f32[768]{0:T(1024)} %copy-done.126) | copy-start | bytes 9220
  450.0 139.1 %copy-start.24 = (bf16[512,768]{1,0:T(8,128)(2,1)S(1)}, bf16[512,768]{1,0:T(8,128)(2,1)}, u32[]{:S(2)}) copy-start(bf16[512,768]{1,0:T(8,128)(2,1)} %copy-done.23) | copy-start | bytes 2359300
  (174 other events, 397.6 us)
Sparse Core Ops, SparseCore 0:
  9.7 36.2 all-gather.6
  47.7 32.9 all-gather.8
  88.3 46.2 all-reduce.9
  187.3 66.0 all-reduce.15
  313.8 48.1 all-reduce.13
  402.7 58.3 reduce-scatter.8
  463.7 60.5 reduce-scatter.6
  527.0 62.0 all-reduce.11
  591.6 61.5 reduce-scatter.12
  655.5 60.3 reduce-scatter.10
where the time goes:
time: 952 us; the launch traced here: 943 us
  blocking collectives  355 us (37%)
  waiting for transfers between devices  341 us (36%)
  matrix products  114 us (12%)
  other arithmetic  74.6 us (8%)
  local copies, waits for them, and re-layouts  26.6 us (3%)
  between operations  17.4 us (2%)
  starting transfers between devices  14.7 us (2%)
    psum x1, blocking collectives, body(): lax.psum((vector_sums[3], vector_sums[4]), ('dp', 'tensor'))  278 us
    psum x3, waiting for transfers between devices, body(): lax.psum(partial_sum.astype(jnp.bfloat16), 'tensor').astype(jnp.float32)  160 us
    unnamed x11, waiting for transfers between devices  55 us
    ppermute x4, waiting for transfers between devices, from_behind(): return lax.ppermute(shard, axis, pairs)  43.6 us
    reduce_scatter x1, waiting for transfers between devices, body(): lax.psum_scatter(weight_sums[0].astype(jnp.bfloat16), 'dp', scatter_dimen...  41.7 us
    psum x1, waiting for transfers between devices, body(): lax.psum(grad_normed.astype(jnp.bfloat16), 'tensor').astype(jnp.float32)  40.5 us
    psum x1, blocking collectives, body(): lax.psum((vector_sums[0], vector_sums[1], vector_sums[2]), 'dp')  31.2 us
    all_gather x1, blocking collectives, body(): lax.all_gather(w_qkv[0], 'dp', axis=0, tiled=True)  28 us
  transfers between devices with their start and end apart: 14, of which 10 were waited for; matrix products, arithmetic and copies ran while one was open for 13% of the time, Pallas kernels for 0%

commit v1 on v0

v1 whole, which is shorter than its diff:
```python
import functools
import math

import jax
import jax.numpy as jnp
from jax import lax
from jax.experimental import pallas as pl
from jax.experimental.pallas import tpu as pltpu
from jax.sharding import PartitionSpec as P

HD = 64
ROT = 16
BLOCK = 128
SEQS = 4
SLOT = 512
D = 768
LOCAL = 192
EPSILON = 1e-05
MASKED = -1e30
MESH = pl.DeviceIdType.MESH
BF = jnp.bfloat16
F32 = jnp.float32
VMEM_LIMIT = 56 * 2**20


def coords():
    dp = lax.axis_index("dp")
    return (
        lax.axis_index("section"),
        dp // 4,
        (dp // 2) % 2,
        dp % 2,
        lax.axis_index("tensor"),
    )


def dp_of(y, x, c):
    return y * 4 + x * 2 + c


def signal_all(targets):
    barrier = pltpu.get_barrier_semaphore()
    for target in targets:
        pl.semaphore_signal(barrier, inc=1, device_id=target, device_id_type=MESH)
    pl.semaphore_wait(barrier, len(targets))


def remote(src, dst, send, recv, target):
    return pltpu.make_async_remote_copy(
        src_ref=src,
        dst_ref=dst,
        send_sem=send,
        recv_sem=recv,
        device_id=target,
        device_id_type=MESH,
    )


def gather_kernel(shard_ref, vec_ref, w_ref, vecs_ref, send, recv, xsend, xrecv):
    s, y, x, c, _ = coords()
    me = dp_of(y, x, c)
    to_y = [{"dp": dp_of((y + k) % 4, x, c)} for k in (1, 2, 3)]
    to_x = {"dp": dp_of(y, 1 - x, c)}
    to_c = {"dp": dp_of(y, x, 1 - c)}
    to_s = {"section": 1 - s}
    signal_all(to_y + [to_x, to_c, to_s])
    w_ref[s, :, me] = shard_ref[...]
    vecs_ref[s] = vec_ref[...]

    def swap(layer, to):
        return [
            remote(w_ref.at[layer, :, me], w_ref.at[layer, :, me], xsend.at[0], xrecv.at[0], to),
            remote(vecs_ref.at[layer], vecs_ref.at[layer], xsend.at[1], xrecv.at[1], to),
        ]

    sent = []

    def push(order, layer, chunk, slot, block, to):
        number = (order * 3 + chunk) * 15 + slot
        copy = remote(
            w_ref.at[layer, chunk, block],
            w_ref.at[layer, chunk, block],
            send.at[number],
            recv.at[number],
            to,
        )
        copy.start()
        sent.append(copy)

    def arrived(order, layer, chunk, slot, block):
        number = (order * 3 + chunk) * 15 + slot
        remote(
            w_ref.at[layer, chunk, block],
            w_ref.at[layer, chunk, block],
            send.at[number],
            recv.at[number],
            to_c,
        ).wait_recv()

    def block_of(j, other):
        return dp_of((y + 4 - j) % 4, (1 - x) if other else x, c)

    def sib_block(j, other):
        return dp_of((y + 4 - j) % 4, (1 - x) if other else x, 1 - c)

    def first(order, layer):
        for chunk in range(3):
            if chunk < 2:
                for k in (1, 2, 3):
                    push(order, layer, chunk, k - 1, me, to_y[k - 1])
                push(order, layer, chunk, 3, me, to_x)
            else:
                push(order, layer, chunk, 0, me, to_x)
                for k in (1, 2, 3):
                    push(order, layer, chunk, k, me, to_y[k - 1])
            push(order, layer, chunk, 7, me, to_c)

    def second(order, layer):
        for chunk in (2, 0, 1):
            if chunk == 2:
                arrived(order, layer, chunk, 0, block_of(0, True))
                for k in (1, 2, 3):
                    push(order, layer, chunk, 3 + k, block_of(0, True), to_y[k - 1])
                push(order, layer, chunk, 8, block_of(0, True), to_c)
            else:
                for j in (1, 3, 2):
                    arrived(order, layer, chunk, j - 1, block_of(j, False))
                    push(order, layer, chunk, 3 + j, block_of(j, False), to_x)
                    push(order, layer, chunk, 7 + 2 * j, block_of(j, False), to_c)

    def third(order, layer):
        for chunk in (0, 1, 2):
            if chunk < 2:
                for j in (0, 1, 3, 2):
                    arrived(order, layer, chunk, 3 + j, block_of(j, True))
                    push(order, layer, chunk, 8 + 2 * j, block_of(j, True), to_c)
            else:
                for j in (1, 3, 2):
                    arrived(order, layer, chunk, j, block_of(j, False))
                    push(order, layer, chunk, 7 + 2 * j, block_of(j, False), to_c)
                for j in (1, 3, 2):
                    arrived(order, layer, chunk, 3 + j, block_of(j, True))
                    push(order, layer, chunk, 8 + 2 * j, block_of(j, True), to_c)

    def fourth(order, layer):
        for chunk in range(3):
            for j in range(4):
                arrived(order, layer, chunk, 7 + 2 * j, sib_block(j, False))
                arrived(order, layer, chunk, 8 + 2 * j, sib_block(j, True))

    outgoing = swap(s, to_s)
    for copy in outgoing:
        copy.start()
    first(0, s)
    second(0, s)
    for copy in swap(1 - s, to_s):
        copy.wait_recv()
    first(1, 1 - s)
    third(0, s)
    second(1, 1 - s)
    third(1, 1 - s)
    fourth(0, s)
    fourth(1, 1 - s)
    for copy in outgoing + sent:
        copy.wait_send()


def gather(shard, vec):
    dma = pltpu.SemaphoreType.DMA
    vmem = pl.BlockSpec(memory_space=pltpu.VMEM)
    return pl.pallas_call(
        gather_kernel,
        out_shape=[
            jax.ShapeDtypeStruct((2, 3, 16, 48, D), BF),
            jax.ShapeDtypeStruct((2, 8, D), F32),
        ],
        in_specs=[vmem, vmem],
        out_specs=[vmem, vmem],
        scratch_shapes=[dma((90,)), dma((90,)), dma((2,)), dma((2,))],
        compiler_params=pltpu.CompilerParams(
            collective_id=0, has_side_effects=True, vmem_limit_bytes=VMEM_LIMIT
        ),
        name="weights_gather",
    )(shard, vec)


def tensor_kernel(whole, part_ref, extra_ref, out_ref, landed, send, recv):
    t = lax.axis_index("tensor")
    to = [{"tensor": (t + k) % 4} for k in (1, 2, 3)]
    signal_all(to)
    copies = []
    for k in (1, 3, 2):
        copy = remote(
            part_ref.at[(t + k) % 4], landed.at[k - 1], send.at[k - 1], recv.at[k - 1], to[k - 1]
        )
        copy.start()
        copies.append(copy)
    for copy in copies:
        copy.wait_recv()
    rows = part_ref.shape[1]

    def add(i, _):
        at = pl.ds(pl.multiple_of(i * 32, 32), 32)
        total = extra_ref[at, :] + part_ref[t, at, :].astype(F32)
        for k in range(3):
            total = total + landed[k, at, :].astype(F32)
        if whole:
            out_ref[t, at, :] = total.astype(BF)
        else:
            out_ref[at, :] = total.astype(BF)
        return 0

    lax.fori_loop(0, rows // 32, add, 0)
    if whole:
        spread = []
        for k in (1, 3, 2):
            copy = remote(
                out_ref.at[t], out_ref.at[t], send.at[2 + k], recv.at[2 + k], to[k - 1]
            )
            copy.start()
            spread.append(copy)
        for k in (1, 3, 2):
            source = (t + 4 - k) % 4
            remote(
                out_ref.at[source], out_ref.at[source], send.at[2 + k], recv.at[2 + k], to[0]
            ).wait_recv()
        copies += spread
    for copy in copies:
        copy.wait_send()


def tensor_sum(number, whole, parts, extra):
    dma = pltpu.SemaphoreType.DMA
    vmem = pl.BlockSpec(memory_space=pltpu.VMEM)
    _, rows, cols = parts.shape
    return pl.pallas_call(
        functools.partial(tensor_kernel, whole),
        out_shape=jax.ShapeDtypeStruct((4, rows, cols) if whole else (rows, cols), BF),
        in_specs=[vmem, vmem],
        out_specs=vmem,
        scratch_shapes=[pltpu.VMEM((3, rows, cols), BF), dma((6,)), dma((6,))],
        compiler_params=pltpu.CompilerParams(
            collective_id=number, has_side_effects=True, vmem_limit_bytes=VMEM_LIMIT
        ),
        name="tensor_sum",
    )(parts, extra)


def reduce_kernel(
    g_ref,
    va_ref,
    vb_ref,
    acts_ref,
    w_out,
    va_out,
    vb_out,
    acts_out,
    sib,
    xbuf,
    ybuf,
    sbuf,
    stage,
    keep,
    vland,
    vsum,
    send,
    recv,
    vsend,
    vrecv,
    asend,
    arecv,
):
    s, y, x, c, t = coords()
    to_y = [{"dp": dp_of((y + k) % 4, x, c)} for k in (1, 2, 3)]
    to_z = [{"tensor": (t + k) % 4} for k in (1, 2, 3)]
    to_x = {"dp": dp_of(y, 1 - x, c)}
    to_c = {"dp": dp_of(y, x, 1 - c)}
    to_s = {"section": 1 - s}
    signal_all(to_y + to_z + [to_x, to_c, to_s])
    sent = []

    def start(src, dst, number, to, sems=(send, recv)):
        copy = remote(src, dst, sems[0].at[number], sems[1].at[number], to)
        copy.start()
        sent.append(copy)

    def landed(ref, number, sems=(send, recv)):
        remote(ref, ref, sems[0].at[number], sems[1].at[number], to_c).wait_recv()

    start(acts_ref.at[1 - s], acts_out.at[s], 0, to_s, (asend, arecv))
    acts_out[s] = acts_ref[s]

    for layer in (1, 0):
        for chunk in range(3):
            start(g_ref.at[layer, chunk, :, 1 - c], sib.at[layer, chunk], layer * 3 + chunk, to_c)

    def base(layer, chunk):
        return 6 + (layer * 3 + chunk) * 5

    vs = (vsend, vrecv)
    vsum[0:8] = va_ref[...]
    vland[t, 0:8] = vb_ref[...]
    for k in (1, 2, 3):
        start(vb_ref, vland.at[t, pl.ds(0, 8)], k - 1, to_z[k - 1], vs)

    for layer in (1, 0):
        for chunk in range(3):
            landed(sib.at[layer, chunk], layer * 3 + chunk)

            def add(i, _):
                sib[layer, chunk, i] = (
                    sib[layer, chunk, i].astype(F32) + g_ref[layer, chunk, i, c].astype(F32)
                ).astype(BF)
                return 0

            lax.fori_loop(0, 8, add, 0)
            if chunk < 2:
                for j in range(4):
                    yy = (y + j) % 4
                    start(
                        sib.at[layer, chunk, yy * 2 + 1 - x],
                        xbuf.at[layer, chunk, yy],
                        base(layer, chunk) + j,
                        to_x,
                    )
            else:
                for k in (1, 3, 2):
                    yy = (y + k) % 4
                    start(
                        sib.at[layer, chunk, pl.ds(yy * 2, 2)],
                        ybuf.at[layer, pl.ds(2 * (k - 1), 2)],
                        base(layer, chunk) + k - 1,
                        to_y[k - 1],
                    )

    for k in (1, 2, 3):
        landed(vland.at[(t + 4 - k) % 4, pl.ds(0, 8)], k - 1, vs)
    vsum[8:16] = vland[0, 0:8] + vland[1, 0:8] + vland[2, 0:8] + vland[3, 0:8]
    stage[0] = vsum[...]
    start(stage.at[0], vland.at[4], 3, to_c, vs)

    for layer in (1, 0):
        for chunk in range(2):
            for j in range(4):
                yy = (y + j) % 4
                landed(xbuf.at[layer, chunk, yy], base(layer, chunk) + j)
                mine = yy * 2 + x
                xbuf[layer, chunk, yy] = (
                    sib[layer, chunk, mine].astype(F32) + xbuf[layer, chunk, yy].astype(F32)
                ).astype(BF)
            for k in (1, 3, 2):
                yy = (y + k) % 4
                start(
                    xbuf.at[layer, chunk, yy],
                    ybuf.at[layer, 6 + chunk * 3 + k - 1],
                    36 + (layer * 2 + chunk) * 3 + k - 1,
                    to_y[k - 1],
                )
        for k in (1, 3, 2):
            landed(ybuf.at[layer, pl.ds(2 * (k - 1), 2)], base(layer, 2) + k - 1)
        for i in range(2):
            total = sib[layer, 2, y * 2 + i].astype(F32)
            for k in range(3):
                total = total + ybuf[layer, 2 * k + i].astype(F32)
            keep[layer, i] = total.astype(BF)
        start(keep.at[layer, 1 - x], keep.at[layer, 2], 48 + layer, to_x)

    landed(vland.at[4], 3, vs)
    vsum[...] = stage[0] + vland[4]
    stage[1] = vsum[...]
    start(stage.at[1], vland.at[5], 4, to_x, vs)

    def finish(layer):
        for chunk in range(2):
            total = xbuf[layer, chunk, y].astype(F32)
            for k in (1, 3, 2):
                landed(
                    ybuf.at[layer, 6 + chunk * 3 + k - 1], 36 + (layer * 2 + chunk) * 3 + k - 1
                )
            for k in range(3):
                total = total + ybuf[layer, 6 + chunk * 3 + k].astype(F32)
            sbuf[layer, chunk] = total.astype(BF)
        landed(keep.at[layer, 2], 48 + layer)
        sbuf[layer, 2] = (keep[layer, x].astype(F32) + keep[layer, 2].astype(F32)).astype(BF)

    finish(1 - s)
    start(sbuf.at[1 - s], sbuf.at[2], 50, to_s)

    landed(vland.at[5], 4, vs)
    vsum[...] = stage[1] + vland[5]
    stage[2] = vsum[...]
    start(stage.at[2], vland.at[6], 5, to_s, vs)

    finish(s)

    landed(vland.at[6], 5, vs)
    vsum[...] = stage[2] + vland[6]
    stage[3] = vsum[...]
    vland[7 + y] = vsum[...]
    for k in (1, 2, 3):
        start(stage.at[3], vland.at[7 + y], 5 + k, to_y[k - 1], vs)

    landed(sbuf.at[2], 50)
    for chunk in range(3):
        w_out[chunk] = sbuf[s, chunk].astype(F32) + sbuf[2, chunk].astype(F32)

    for k in (1, 2, 3):
        landed(vland.at[7 + (y + 4 - k) % 4], 5 + k, vs)
    vsum[...] = vland[7] + vland[8] + vland[9] + vland[10]
    va_out[...] = vsum[0:8]
    vb_out[...] = vsum[8:16]
    landed(acts_out.at[1 - s], 0, (asend, arecv))
    for copy in sent:
        copy.wait_send()


def reduce_all(grads, va, vb, acts):
    dma = pltpu.SemaphoreType.DMA
    vmem = pl.BlockSpec(memory_space=pltpu.VMEM)
    return pl.pallas_call(
        reduce_kernel,
        out_shape=[
            jax.ShapeDtypeStruct((3, 48, D), F32),
            jax.ShapeDtypeStruct((8, D), F32),
            jax.ShapeDtypeStruct((8, D), F32),
            jax.ShapeDtypeStruct(acts.shape, BF),
        ],
        in_specs=[vmem] * 4,
        out_specs=[vmem] * 4,
        scratch_shapes=[
            pltpu.VMEM((2, 3, 8, 48, D), BF),
            pltpu.VMEM((2, 2, 4, 48, D), BF),
            pltpu.VMEM((2, 12, 48, D), BF),
            pltpu.VMEM((3, 3, 48, D), BF),
            pltpu.VMEM((4, 16, D), F32),
            pltpu.VMEM((2, 3, 48, D), BF),
            pltpu.VMEM((11, 16, D), F32),
            pltpu.VMEM((16, D), F32),
            dma((51,)),
            dma((51,)),
            dma((9,)),
            dma((9,)),
            dma((1,)),
            dma((1,)),
        ],
        compiler_params=pltpu.CompilerParams(
            collective_id=3, has_side_effects=True, vmem_limit_bytes=VMEM_LIMIT
        ),
        name="grads_reduce",
    )(grads, va, vb, acts)


def arrange(lengths):
    blocks = (lengths + BLOCK - 1) // BLOCK
    block_ends = jnp.cumsum(blocks)
    places = jnp.arange(SLOT, dtype=jnp.int32)
    owners = jnp.sum((block_ends[None, :] <= (places // BLOCK)[:, None]).astype(jnp.int32), axis=1)
    starts = jnp.concatenate([jnp.zeros((1,), jnp.int32), block_ends]) * BLOCK
    limits = jnp.concatenate([lengths, jnp.zeros((1,), jnp.int32)])
    chosen = (owners[:, None] == jnp.arange(SEQS + 1, dtype=jnp.int32)[None, :]).astype(jnp.int32)
    offset = places - jnp.sum(chosen * starts[None, :], axis=1)
    seq_len = jnp.sum(chosen * limits[None, :], axis=1)
    allowed = (
        (owners[:, None] == owners[None, :])
        & (offset[None, :] <= offset[:, None])
        & ((offset[None, :] < seq_len[None, :]) | (places[:, None] == places[None, :]))
    )
    half_rot = ROT // 2
    inv_freq = 1.0 / 10000.0 ** (jnp.arange(half_rot, dtype=jnp.float32) * 2.0 / ROT)
    angles = offset.astype(jnp.float32)[:, None] * inv_freq[None, :]
    return (jnp.cos(angles), jnp.sin(angles), allowed)


def rotate(values, cosines, sines):
    half_rot = ROT // 2
    cos_rows = cosines[:, None, :]
    sin_rows = sines[:, None, :]
    first = values[..., :half_rot]
    second = values[..., half_rot:ROT]
    return jnp.concatenate(
        [
            first * cos_rows - second * sin_rows,
            second * cos_rows + first * sin_rows,
            values[..., ROT:],
        ],
        axis=-1,
    )


def dot(a, b):
    return jnp.dot(a, b, preferred_element_type=F32)


def dot_nt(a, b):
    return lax.dot_general(a, b, (((1,), (1,)), ((), ())), preferred_element_type=F32)


def dot_tn(a, b):
    return lax.dot_general(a, b, (((0,), (0,)), ((), ())), preferred_element_type=F32)


def gelu_exact(values):
    return jax.nn.gelu(values, approximate=False)


def normalize(acts):
    average = jnp.mean(acts, axis=-1, keepdims=True)
    centred = acts - average
    spread = jnp.mean(centred * centred, axis=-1, keepdims=True)
    rstd = lax.rsqrt(spread + EPSILON)
    return centred * rstd, rstd


def forward(acts_bf, w, vec, seq):
    cosines, sines, allowed = seq
    w_in, w_out_t, w_c = w[0], w[1], w[2]
    normal, rstd = normalize(acts_bf.astype(F32))
    normed = (normal * vec[3] + vec[5]).astype(BF)
    pre = (dot(normed, w_c[:, : 3 * LOCAL]) + vec[0, : 3 * LOCAL]).reshape(SLOT, 3, 3, HD)
    query = rotate(pre[:, 0], cosines, sines).astype(BF)
    key = rotate(pre[:, 1], cosines, sines).astype(BF)
    value = pre[:, 2].astype(BF)
    scores = jnp.einsum("qhd,khd->hqk", query, key, preferred_element_type=F32) / math.sqrt(HD)
    masked = jnp.where(allowed[None], scores, MASKED)
    top = jnp.max(masked, axis=-1, keepdims=True)
    weights = jnp.where(allowed[None], jnp.exp(masked - top), 0.0)
    probs_f = weights / jnp.sum(weights, axis=-1, keepdims=True)
    probs = probs_f.astype(BF)
    mixed = (
        jnp.einsum("hqk,khd->qhd", probs, value, preferred_element_type=F32)
        .reshape(SLOT, LOCAL)
        .astype(BF)
    )
    normed_two = (normal * vec[4] + vec[6]).astype(BF)
    hidden = dot(normed_two, w_in) + vec[1]
    activated = gelu_exact(hidden).astype(BF)
    part = dot_nt(mixed, w_c[:, 3 * LOCAL :]) + dot_nt(activated, w_out_t)
    kept = (normal, rstd, normed, query, key, value, probs_f, mixed, normed_two, hidden, activated)
    return part.astype(BF), kept


def backward(grad, kept, w, vec, seq):
    normal, rstd, normed, query, key, value, probs_f, mixed, normed_two, hidden, activated = kept
    cosines, sines, _ = seq
    w_in, w_out_t, w_c = w[0], w[1], w[2]
    g_out_bias = jnp.sum(grad.astype(F32), axis=0)
    grad_mixed = dot(grad, w_c[:, 3 * LOCAL :]).astype(BF).reshape(SLOT, 3, HD)
    g_attn = dot_tn(grad, mixed)
    g_out = dot_tn(grad, activated)
    grad_act = dot(grad, w_out_t)
    grad_hidden = jax.vjp(gelu_exact, hidden)[1](grad_act)[0].astype(BF)
    g_in_bias = jnp.sum(grad_hidden.astype(F32), axis=0)
    g_in = dot_tn(normed_two, grad_hidden)
    grad_norm_two = dot_nt(grad_hidden, w_in)
    grad_probs = jnp.einsum("qhd,khd->hqk", grad_mixed, value, preferred_element_type=F32)
    row_dot = jnp.sum(probs_f * grad_probs, axis=-1, keepdims=True)
    grad_scores = (probs_f * (grad_probs - row_dot)).astype(BF)
    scale = 1.0 / math.sqrt(HD)
    grad_query = jnp.einsum("hqk,khd->qhd", grad_scores, key, preferred_element_type=F32) * scale
    grad_key = jnp.einsum("hqk,qhd->khd", grad_scores, query, preferred_element_type=F32) * scale
    grad_value = jnp.einsum(
        "hqk,qhd->khd", probs_f.astype(BF), grad_mixed, preferred_element_type=F32
    )
    grad_pre = jnp.stack(
        [rotate(grad_query, cosines, -sines), rotate(grad_key, cosines, -sines), grad_value],
        axis=1,
    )
    grad_pre = grad_pre.reshape(SLOT, 3 * LOCAL).astype(BF)
    g_qkv_bias = jnp.sum(grad_pre.astype(F32), axis=0)
    g_qkv = dot_tn(normed, grad_pre)
    grad_normed = dot_nt(grad_pre, w_c[:, : 3 * LOCAL])
    mixture = grad_normed * vec[3] + grad_norm_two * vec[4]
    part = rstd * (
        mixture
        - jnp.mean(mixture, axis=-1, keepdims=True)
        - normal * jnp.mean(mixture * normal, axis=-1, keepdims=True)
    )
    weights = jnp.stack([g_in, g_out, jnp.concatenate([g_qkv, g_attn], axis=1)]).astype(BF)
    zero = jnp.zeros((D,), F32)
    va = jnp.stack(
        [jnp.concatenate([g_qkv_bias, jnp.zeros((LOCAL,), F32)]), g_in_bias, g_out_bias, zero]
    )
    vb = jnp.stack(
        [
            jnp.sum(grad_normed * normal, axis=0),
            jnp.sum(grad_norm_two * normal, axis=0),
            jnp.sum(grad_normed, axis=0),
            jnp.sum(grad_norm_two, axis=0),
        ]
    )
    return part.astype(BF), weights.reshape(3, 8, 2, 48, D), va, vb


def columns(values, t):
    mine = lax.dynamic_slice_in_dim(values, t * LOCAL, LOCAL, 1)
    return mine.reshape(2, 256, LOCAL).transpose(1, 0, 2).reshape(256, 2 * LOCAL)


def column_blocks(part):
    return part.reshape(2, 256, 4, LOCAL).transpose(2, 1, 0, 3).reshape(4, 256, 2 * LOCAL)


def body(
    inputs,
    cotangent,
    seq_lengths,
    w_qkv,
    b_qkv,
    w_attn_out,
    w_in,
    b_in,
    w_out,
    b_out,
    norm_gains,
    norm_biases,
):
    s = lax.axis_index("section")
    t = lax.axis_index("tensor")
    shard = jnp.stack(
        [
            w_in[0],
            w_out[0].T,
            jnp.concatenate([w_qkv[0].reshape(48, 3 * LOCAL), w_attn_out[0].T], axis=1),
        ]
    )
    vec = jnp.concatenate(
        [
            jnp.pad(b_qkv[0].reshape(1, -1), ((0, 0), (0, LOCAL))),
            b_in,
            b_out,
            norm_gains[0],
            norm_biases[0],
            jnp.zeros((1, D), F32),
        ]
    )
    weights, vecs = gather(shard, vec)
    weights = weights.reshape(2, 3, D, D)

    acts = lax.dynamic_index_in_dim(inputs, s, 0, keepdims=False)
    grad = lax.dynamic_index_in_dim(cotangent, s, 0, keepdims=False)
    lengths = lax.dynamic_index_in_dim(seq_lengths[:, 0], s, 0, keepdims=False)
    seq = arrange(lengths)

    zero_vec, one_vec = vecs[0], vecs[1]
    part, kept_zero = forward(acts, weights[0], zero_vec, seq)
    own = lax.dynamic_slice_in_dim(acts, t * 128, 128, 0).astype(F32) + zero_vec[2]
    acts_one = tensor_sum(1, True, part.reshape(4, 128, D), own).reshape(SLOT, D)
    part, kept_one = forward(acts_one, weights[1], one_vec, seq)
    bias_cols = lax.dynamic_slice_in_dim(one_vec[2], t * LOCAL, LOCAL, 0)
    extra = columns(acts_one, t).astype(F32) + jnp.tile(bias_cols, 2)
    acts_two = tensor_sum(2, False, column_blocks(part), extra)

    part, w_grads_one, va_one, vb_one = backward(grad, kept_one, weights[1], one_vec, seq)
    own = lax.dynamic_slice_in_dim(grad, t * 128, 128, 0).astype(F32)
    grad_one = tensor_sum(4, True, part.reshape(4, 128, D), own).reshape(SLOT, D)
    part, w_grads_zero, va_zero, vb_zero = backward(grad_one, kept_zero, weights[0], zero_vec, seq)
    grad_zero = tensor_sum(
        5, False, column_blocks(part), columns(grad_one, t).astype(F32)
    )
    outs = jnp.stack(
        [
            jnp.stack([columns(acts_one, t), grad_zero]),
            jnp.stack([acts_two, columns(grad_one, t)]),
        ]
    )
    w_sums, va, vb, acts_all = reduce_all(
        jnp.stack([w_grads_zero, w_grads_one]),
        jnp.concatenate([va_zero, va_one]),
        jnp.concatenate([vb_zero, vb_one]),
        outs,
    )
    acts_all = acts_all.reshape(2, 2, 256, 2, LOCAL).transpose(0, 1, 3, 2, 4)
    acts_all = acts_all.reshape(2, 2, SLOT, LOCAL)
    va = lax.dynamic_slice_in_dim(va, s * 4, 4, 0)
    vb = lax.dynamic_slice_in_dim(vb, s * 4, 4, 0)
    return (
        acts_all[:, 0][None],
        acts_all[:, 1][None],
        w_sums[2, :, : 3 * LOCAL].reshape(1, 48, 3, LOCAL),
        va[0, : 3 * LOCAL].reshape(1, 3, LOCAL),
        w_sums[2, :, 3 * LOCAL :].T[None],
        w_sums[0][None],
        va[1][None],
        w_sums[1].T[None],
        va[2][None],
        vb[0:2][None],
        vb[2:4][None],
    )


def solution(mesh):
    return jax.shard_map(
        body,
        mesh=mesh,
        in_specs=(
            P(None, "dp", None),
            P(None, "dp", None),
            P(None, "dp", None),
            P("section", "dp", None, "tensor"),
            P("section", None, "tensor"),
            P("section", "tensor", "dp"),
            P("section", "dp", "tensor"),
            P("section", "tensor"),
            P("section", "tensor", "dp"),
            P("section", None),
            P("section", None, None),
            P("section", None, None),
        ),
        out_specs=(
            P("section", None, "dp", "tensor"),
            P("section", None, "dp", "tensor"),
            P("section", "dp", None, "tensor"),
            P("section", None, "tensor"),
            P("section", "tensor", "dp"),
            P("section", "dp", "tensor"),
            P("section", "tensor"),
            P("section", "tensor", "dp"),
            P("section", None),
            P("section", None, None),
            P("section", None, None),
        ),
        check_vma=False,
    )
```

time: 952 us -> 351 us (0.37)
  blocking collectives: 355 us -> 0 us
  waiting for transfers between devices: 341 us -> 0 us
  Pallas kernels: 0 us -> 182 us
  matrix products: 114 us -> 73.7 us
  other arithmetic: 74.6 us -> 35.9 us
  local copies, waits for them, and re-layouts: 26.6 us -> 50.6 us
  between operations: 17.4 us -> 2.57 us
  starting transfers between devices: 14.7 us -> 0 us
    psum x2 -> x0, blocking collectives: 309 us -> none  [the longest x1 278 us: body(): lax.psum((vector_sums[3], vector_sums[4]), ('dp', 'tensor'))]
    psum x4 -> x0, waiting for transfers between devices: 200 us -> none  [the longest x3 160 us: body(): lax.psum(partial_sum.astype(jnp.bfloat16), 'tensor').astype(jnp.float32)]
    pallas_call x0 -> x6, Pallas kernels: none -> 182 us  [the longest x4 75.5 us: tensor_sum(): pl.pallas_call(functools.partial(tensor_kernel, whole), out_shape=jax.Sha...]
    unnamed x11 -> x0, waiting for transfers between devices: 55 us -> none
    dot_general x57 -> x34, matrix products: 114 us -> 64.9 us  [the longest x8 26.7 us: dot(): return jnp.dot(a, b, preferred_element_type=F32)]
    all_gather x2 -> x0, blocking collectives: 46 us -> none  [the longest x1 28 us: body(): lax.all_gather(w_qkv[0], 'dp', axis=0, tiled=True)]
    ppermute x4 -> x0, waiting for transfers between devices: 43.6 us -> none  [from_behind(): return lax.ppermute(shard, axis, pairs)]
    reduce_scatter x3 -> x0, waiting for transfers between devices: 41.7 us -> none  [the longest x1 41.7 us: body(): lax.psum_scatter(weight_sums[0].astype(jnp.bfloat16), 'dp', scatter_dimen...]
  transfers between devices with their start and end apart: 14 -> 0, of which waited for: 10 -> 0; matrix products, arithmetic and copies ran while one was open for 13% -> 0% of each run, Pallas kernels for 0% -> 0%
where the time goes in v1:
time: 351 us; the launch traced here: 345 us
  Pallas kernels  182 us (52%)
  matrix products  73.7 us (21%)
  local copies, waits for them, and re-layouts  50.6 us (14%)
  other arithmetic  35.9 us (10%)
    pallas_call x4, Pallas kernels, tensor_sum(): pl.pallas_call(functools.partial(tensor_kernel, whole), out_shape=jax.Sha...  75.5 us
    pallas_call x1, Pallas kernels, reduce_all(): pl.pallas_call(reduce_kernel, out_shape=[jax.ShapeDtypeStruct((3, 48, D),...  59.4 us
    pallas_call x1, Pallas kernels, gather(): pl.pallas_call(gather_kernel, out_shape=[jax.ShapeDtypeStruct((2, 3, 16,...  46.9 us
    dot_general x8, matrix products, dot(): return jnp.dot(a, b, preferred_element_type=F32)  26.7 us
    dot_general x8, matrix products, dot_tn(): lax.dot_general(a, b, (((0,), (0,)), ((), ())), preferred_element_type=F32)  14 us
    dot_general x8, matrix products, dot_nt(): lax.dot_general(a, b, (((1,), (1,)), ((), ())), preferred_element_type=F32)  13 us
    sub x2, matrix products, forward(): weights = jnp.where(allowed[None], jnp.exp(masked - top), 0.0)  8.79 us
    dot_general x5, local copies, waits for them, and re-layouts, dot_tn(): lax.dot_general(a, b, (((0,), (0,)), ((), ())), preferred_element_type=F32)  7.89 us

profile of v1, /device:TPU:0, one launch (start us, length us, event | category | flops | bytes accessed | tf_op | source)
XLA Modules:
  0.0 344.6 jit_solution(9738455888751502710)
XLA Ops:
  0.6 0.9 copy.146
  2.5 1.6 pad_maximum_fusion.3.shard_ref
  5.0 1.4 concatenate.81.vec_ref
  6.3 46.9 %weights_gather.1 = (bf16[2,3,16,48,768]{4,3,2,1,0:T(8,128)(2,1)}, f32[2,8,768]{2,1,0:T(8,128)}) custom-call(bf16[3,48,768]{2,1,0:T(8,128)(2,1)} %pad_maximum_fusion.3.shard_ref, f32[8,768]{1,0:T(8,128)} %concatenate.81.vec_ref), custom_call_target="tpu_custom_call" | custom-call | tf_op jit(solution)/shard_map/weights_gather/pallas_call | solution.py:171
  53.3 5.1 %fusion.154 = (bf16[1,1,16,48,768]{4,3,2,1,0:T(8,128)(2,1)}, bf16[1,1,16,48,768]{4,3,2,1,0:T(8,128)(2,1)}, bf16[1,1,16,48,768]{4,3,2,1,0:T(8,128)(2,1)S(1)}, bf1...) fusion(bf16[2,3,16,48,768]{4,3,2,1,0:T(8,128)(2,1)} %get-tuple-, ...), kind=kLoop, calls=%fused_computation.324 | loop fusion | bytes 14155776 | tf_op jit(solution)/shard_map/slice | solution.py:545
  58.4 1.4 slice_reduce_fusion
  59.8 1.4 convert_reduce_fusion
  61.2 2.4 fusion.32
  64.3 1.9 convolution_add_fusion.3
  66.7 1.0 fusion.67
  67.8 1.2 slice_bitcast_fusion.5
  71.7 5.0 %fusion.155 = (f32[3,512]{1,0:T(4,128)}, f32[3,512,512]{1,2,0:T(8,128)}) fusion(pred[512,512]{0,1:T(8,128)(4,1)} %fusion.67, bf16[512,3,48]{0,2,1:T(8,128)(2,1)} %slice.455, bf16[512,3,8]{0,2,1:T(8,128)(2,1)} %get-tuple-element.163, bf16[512,3,8]{0,2,1:T(8,128)(2,1)} %get-tuple-element.164, bf16[512,3,48]{0,2,1:T(8,128)(2,1)} %slice.456, ...), kind=kOutput, calls=%fused_computation.325 | convolution fusion | flops 105775616 | bytes 3807232 | tf_op jit(solution)/shard_map/sub | solution.py:526
  76.7 2.3 convolution_convert_fusion.11
  80.6 5.7 %multiply_convert_fusion.4 = (bf16[512,768]{1,0:T(8,128)(2,1)S(1)}, f32[512,768]{1,0:T(8,128)}, f32[512,768]{1,0:T(8,128)}) fusion(f32[768]{0:T(1024)S(1)} %copy-done.114, bf16[768,768]{1,0:T(8,128)(2,1)S(1)} %bitcast.343, f32[768]{0:T(1024)S(1)} %copy-done.108, f32[768]{0:T(1024)S(1)} %copy-done.110, f32[512]{0:T(512)S(1)} %copy-done.88, ...), kind=kOutput, calls=%fused_computation.89 | convolution fusion | flops 632291328 | bytes 5914628 | tf_op jit(solution)/shard_map/dot_general | solution.py:491
  86.3 1.7 add_convert_fusion.5
  88.0 1.7 convert_add_fusion.extra_ref
  89.8 28.5 %tensor_sum.4 = bf16[4,128,768]{2,1,0:T(8,128)(2,1)} custom-call(bf16[4,128,768]{2,1,0:T(8,128)(2,1)} %bitcast.359, f32[128,768]{1,0:T(8,128)} %convert_add_fusion.extra_ref), custom_call_target="tpu_custom_call" | custom-call | tf_op jit(solution)/shard_map/tensor_sum/pallas_call | solution.py:236
  118.3 1.4 convert_reduce_fusion.1
  119.7 1.5 fusion.12
  124.0 3.8 %fusion.156 = (f32[3,512]{1,0:T(4,128)}, f32[3,512,512]{1,2,0:T(8,128)}) fusion(pred[512,512]{0,1:T(8,128)(4,1)S(1)} %copy-done.41, bf16[512,3,48]{0,2,1:T(8,128)(2,1)S(1)} %slice.453, bf16[512,3,8]{0,2,1:T(8,128)(2,1)S(1)} %get-tuple-element.161, bf16[512,3,8]{0,2,1:T(8,128)(2,1)S(1)} %get-tuple-element.162, bf16[512,3,48]{0,2,1:T(8,128)(2,1)S(1)} %slice.454, ...), kind=kOutput, calls=%fused_computation.326 | convolution fusion | flops 105775616 | bytes 3807232 | tf_op jit(solution)/shard_map/sub | solution.py:526
  127.8 2.5 convolution_convert_fusion.8
  131.9 1.6 multiply_reduce_fusion.1
  136.7 1.4 fusion.9
  138.8 1.1 pad_maximum_fusion.1
  139.8 2.4 copy.160
  142.2 0.9 dynamic-slice_bitcast_fusion
  143.2 2.3 copy.158
  145.5 12.2 %multiply_convert_fusion.2 = (bf16[512,768]{1,0:T(8,128)(2,1)S(1)}, f32[512,768]{1,0:T(8,128)S(1)}, f32[512,768]{1,0:T(8,128)S(1)}) fusion(f32[768]{0:T(1024)} %get-tuple-element.90, bf16[512,768]{1,0:T(8,128)(2,1)} %bitcast.360, bf16[768,768]{1,0:T(8,128)(2,1)} %bitcast.347), kind=kOutput, calls=%fused_computation.66 | convolution fusion | flops 629932032 | bytes 5901312 | tf_op jit(solution)/shard_map/dot_general | solution.py:491
  157.7 1.8 fusion.61
  160.9 1.8 convert_reduce_fusion.3
  162.7 3.5 %fusion.149 = (f32[768]{0:T(1024)}, f32[768]{0:T(1024)}, f32[512]{0:T(512)}, f32[512]{0:T(512)}, f32[512,768]{1,0:T(8,128)}, /*index=5*/f32[768]{0:T(1024)}, f32[768]{0:T(1024)}, bf16[768,512]{0,1:T(8,128)(2,1)}) fusion(f32[512]{0:T(512)S(1)} %copy-done.84, f32[512]{0:T(512)S(1)} %copy-done.81, bf16[4,128,768]{2,1,0:T(8,128)(2,1)S(1)} %copy-done.1, ...), kind=kOutput, calls=%fused_computation.321 | convolution fusion | flops 611053568 | bytes 6714368 | tf_op jit(solution)/shard_map/dot_general | solution.py:495
  166.2 2.3 copy.157
  168.5 3.3 fusion.60
  171.9 1.4 multiply_convert_fusion.3
  174.0 23.5 %tensor_sum.5 = bf16[4,128,768]{2,1,0:T(8,128)(2,1)} custom-call(bf16[4,128,768]{2,1,0:T(8,128)(2,1)} %bitcast.334, f32[128,768]{1,0:T(8,128)} %bitcast_convert_fusion.2.extra_ref), custom_call_target="tpu_custom_call" | custom-call | tf_op jit(solution)/shard_map/tensor_sum/pallas_call | solution.py:236
  197.5 1.5 convolution_convert_fusion.7
  199.0 1.8 convolution_convert_fusion.9
  201.4 1.6 multiply_reduce_fusion
  205.6 1.1 copy-done.9
  207.6 1.1 pad_maximum_fusion
  208.7 2.5 copy.156
  211.2 1.2 copy.152
  212.4 3.3 fusion.59
  217.5 1.8 convert_reduce_fusion.5
  219.3 3.2 fusion.28
  222.6 1.2 copy.147
  223.8 2.3 fusion.58
  226.2 5.7 %maximum_maximum_fusion.g_ref = bf16[2,3,8,2,48,768]{5,4,3,2,1,0:T(8,128)(2,1)} fusion(bf16[1,1,8,2,48,768]{5,4,3,2,1,0:T(8,128)(2,1)S(1)} %bitcast.326, bf16[1,1,8,2,48,768]{5,4,3,2,1,0:T(8,128)(2,1)} %fusion.61, bf16[1,1,8,2,48,768]{5,4,3,2,1,0:T(8,128)(2,1)} %fusion.60, bf16[1,1,8,2,48,768]{5,4,3,2,1,0:T(8,128)(2,1)S(1)} %bitcast.327, ...), kind=kLoop, calls=%fused_computation.2 | loop fusion | flops 17694720 | bytes 14155776 | tf_op jit(solution)/shard_map/stack | solution.py:667
  234.6 1.2 copy.166
  237.8 1.7 add_convert_fusion
  239.5 1.4 copy.170
  241.2 1.2 copy.173.part_ref
  244.8 12.1 %tensor_sum.7 = bf16[256,384]{1,0:T(8,128)(2,1)} custom-call(bf16[4,256,384]{2,1,0:T(8,128)(2,1)} %copy.173.part_ref, f32[256,384]{1,0:T(8,128)} %broadcast_add_fusion.extra_ref), custom_call_target="tpu_custom_call" | custom-call | tf_op jit(solution)/shard_map/tensor_sum/pallas_call | solution.py:236
  256.8 1.7 maximum_bitcast_fusion.5
  258.6 1.9 fusion.31
  261.1 1.2 copy.167.part_ref
  262.3 0.9 copy.168.extra_ref
  263.2 11.5 %tensor_sum.6 = bf16[256,384]{1,0:T(8,128)(2,1)} custom-call(bf16[4,256,384]{2,1,0:T(8,128)(2,1)} %copy.167.part_ref, f32[256,384]{1,0:T(8,128)} %copy.168.extra_ref), custom_call_target="tpu_custom_call" | custom-call | tf_op jit(solution)/shard_map/tensor_sum/pallas_call | solution.py:236
  274.9 1.0 maximum_bitcast_fusion.4
  275.9 1.0 pad_maximum_fusion.2.acts_ref
  276.9 59.4 %grads_reduce.1 = (f32[3,48,768]{2,1,0:T(8,128)}, f32[8,768]{1,0:T(8,128)}, f32[8,768]{1,0:T(8,128)}, bf16[2,2,256,384]{3,2,1,0:T(8,128)(2,1)}) custom-call(bf16[2,3,8,2,48,768]{5,4,3,2,1,0:T(8,128)(2,1)} %maximum_maximum_fusion.g_ref, f32[8,768]{1,0:T(8,128)} %concatenate.96.va_ref, f32[8,768]{1,0:T(8,128)} %concatenate.97.vb_ref, ...), custom_call_target="tpu_custom_call" | custom-call | tf_op jit(solution)/shard_map/grads_reduce/pallas_call | solution.py:420
  336.3 1.4 copy.175
  337.8 0.9 slice_bitcast_fusion
  342.4 1.4 constant_dynamic-slice_fusion.2
  (364 shorter events, 34.9 us)
Async XLA Ops:
  4.9 48.3 %copy-start.60 = (f32[1,768]{1,0:T(1,128)}, f32[1,768]{1,0:T(1,128)S(1)}, u32[]{:S(2)}) copy-start(f32[1,768]{1,0:T(1,128)S(1)} %broadcast.482) | copy-start | bytes 9220
  53.3 5.1 %copy-start.42 = (f32[2,8,768]{2,1,0:T(8,128)S(1)}, f32[2,8,768]{2,1,0:T(8,128)}, u32[]{:S(2)}) copy-start(f32[2,8,768]{2,1,0:T(8,128)} %get-tuple-element.17) | copy-start | bytes 147460
  58.4 20.8 %copy-start.2 = (bf16[1,1,16,48,768]{4,3,2,1,0:T(8,128)(2,1)}, bf16[1,1,16,48,768]{4,3,2,1,0:T(8,128)(2,1)S(1)}, u32[]{:S(2)}) copy-start(bf16[1,1,16,48,768]{4,3,2,1,0:T(8,128)(2,1)S(1)} %get-tuple-element.119) | copy-start | bytes 3538948
  58.4 21.4 %copy-start.22 = (bf16[1,1,16,48,768]{4,3,2,1,0:T(8,128)(2,1)}, bf16[1,1,16,48,768]{4,3,2,1,0:T(8,128)(2,1)S(1)}, u32[]{:S(2)}) copy-start(bf16[1,1,16,48,768]{4,3,2,1,0:T(8,128)(2,1)S(1)} %get-tuple-element.120) | copy-start | bytes 3538948
  59.8 6.4 %copy-start.105 = (f32[768]{0:T(1024)}, f32[768]{0:T(1024)S(1)}, u32[]{:S(2)}) copy-start(f32[768]{0:T(1024)S(1)} %get-tuple-element.97) | copy-start | bytes 9220
  59.8 6.4 %copy-start.112 = (f32[768]{0:T(1024)}, f32[768]{0:T(1024)S(1)}, u32[]{:S(2)}) copy-start(f32[768]{0:T(1024)S(1)} %get-tuple-element.96) | copy-start | bytes 9220
  59.8 3.9 %copy-start.43 = (f32[2,8,768]{2,1,0:T(8,128)S(1)}, f32[2,8,768]{2,1,0:T(8,128)}, u32[]{:S(2)}) copy-start(f32[2,8,768]{2,1,0:T(8,128)} %get-tuple-element.17) | copy-start | bytes 147460
  59.8 4.5 %copy-start.7 = (bf16[2,512,768]{2,1,0:T(8,128)(2,1)S(1)}, bf16[2,512,768]{2,1,0:T(8,128)(2,1)}, u32[]{:S(2)}) copy-start(bf16[2,512,768]{2,1,0:T(8,128)(2,1)} %param.12) | copy-start | bytes 4718596
  61.2 5.0 %copy-start.65 = (f32[512]{0:T(512)}, f32[512]{0:T(512)S(1)}, u32[]{:S(2)}) copy-start(f32[512]{0:T(512)S(1)} %broadcast_multiply_fusion.5) | copy-start | bytes 6148
  63.6 2.6 copy-start.87
  64.3 2.0 copy-start.119
  80.6 5.7 %copy-start.24 = (bf16[1,1,16,48,768]{4,3,2,1,0:T(8,128)(2,1)S(1)}, bf16[1,1,16,48,768]{4,3,2,1,0:T(8,128)(2,1)}, u32[]{:S(2)}) copy-start(bf16[1,1,16,48,768]{4,3,2,1,0:T(8,128)(2,1)} %get-tuple-element.118) | copy-start | bytes 3538948
  89.8 32.0 %copy-start.74 = (f32[768]{0:T(1024)S(1)}, f32[768]{0:T(1024)}, u32[]{:S(2)}) copy-start(f32[768]{0:T(1024)} %get-tuple-element.94) | copy-start | bytes 9220
  89.8 32.0 %copy-start.77 = (f32[768]{0:T(1024)S(1)}, f32[768]{0:T(1024)}, u32[]{:S(2)}) copy-start(f32[768]{0:T(1024)} %get-tuple-element.93) | copy-start | bytes 9220
  89.8 32.0 %copy-start.104 = (f32[576]{0:T(1024)S(1)}, f32[576]{0:T(1024)}, u32[]{:S(2)}) copy-start(f32[576]{0:T(1024)} %get-tuple-element.194) | copy-start | bytes 6916
  118.3 3.5 %copy-start.1 = (bf16[4,128,768]{2,1,0:T(8,128)(2,1)S(1)}, bf16[4,128,768]{2,1,0:T(8,128)(2,1)}, u32[]{:S(2)}) copy-start(bf16[4,128,768]{2,1,0:T(8,128)(2,1)} %tensor_sum.4) | copy-start | bytes 2359300
  119.7 3.1 copy-start.63
  119.7 3.1 copy-start.80
  122.9 4.9 %copy-start.35 = (bf16[512,3,48]{0,2,1:T(8,128)(2,1)}, bf16[512,3,48]{0,2,1:T(8,128)(2,1)S(1)}, u32[]{:S(2)}) copy-start(bf16[512,3,48]{0,2,1:T(8,128)(2,1)S(1)} %slice.453) | copy-start | bytes 442372
  123.6 4.2 %copy-start.52 = (bf16[512,3,8]{0,2,1:T(8,128)(2,1)}, bf16[512,3,8]{0,2,1:T(8,128)(2,1)S(1)}, u32[]{:S(2)}) copy-start(bf16[512,3,8]{0,2,1:T(8,128)(2,1)S(1)} %get-tuple-element.146) | copy-start | bytes 73732
  123.6 4.2 %copy-start.54 = (bf16[512,3,8]{0,2,1:T(8,128)(2,1)}, bf16[512,3,8]{0,2,1:T(8,128)(2,1)S(1)}, u32[]{:S(2)}) copy-start(bf16[512,3,8]{0,2,1:T(8,128)(2,1)S(1)} %get-tuple-element.147) | copy-start | bytes 73732
  123.6 4.2 %copy-start.56 = (bf16[512,3,8]{0,2,1:T(8,128)(2,1)}, bf16[512,3,8]{0,2,1:T(8,128)(2,1)S(1)}, u32[]{:S(2)}) copy-start(bf16[512,3,8]{0,2,1:T(8,128)(2,1)S(1)} %get-tuple-element.161) | copy-start | bytes 73732
  123.6 4.2 %copy-start.58 = (bf16[512,3,8]{0,2,1:T(8,128)(2,1)}, bf16[512,3,8]{0,2,1:T(8,128)(2,1)S(1)}, u32[]{:S(2)}) copy-start(bf16[512,3,8]{0,2,1:T(8,128)(2,1)S(1)} %get-tuple-element.162) | copy-start | bytes 73732
  123.8 4.0 %copy-start.37 = (bf16[512,3,48]{0,2,1:T(8,128)(2,1)}, bf16[512,3,48]{0,2,1:T(8,128)(2,1)S(1)}, u32[]{:S(2)}) copy-start(bf16[512,3,48]{0,2,1:T(8,128)(2,1)S(1)} %slice.454) | copy-start | bytes 442372
  127.8 2.5 copy-start.4
  127.8 3.5 %copy-start.13 = (f32[3,512,512]{1,2,0:T(8,128)S(1)}, f32[3,512,512]{1,2,0:T(8,128)}, u32[]{:S(2)}) copy-start(f32[3,512,512]{1,2,0:T(8,128)} %get-tuple-element.182) | copy-start | bytes 9437188
  145.5 12.2 %copy-start.31 = (bf16[768,512]{1,0:T(8,128)(2,1)S(1)}, bf16[768,512]{1,0:T(8,128)(2,1)}, u32[]{:S(2)}) copy-start(bf16[768,512]{1,0:T(8,128)(2,1)} %copy.158) | copy-start | bytes 2359300
  162.6 3.6 %copy-start.124 = (bf16[512,768]{1,0:T(8,128)(2,1)}, bf16[512,768]{1,0:T(8,128)(2,1)S(1)}, u32[]{:S(2)}) copy-start(bf16[512,768]{1,0:T(8,128)(2,1)S(1)} %get-tuple-element.189) | copy-start | bytes 2359300
  168.5 3.3 copy-start.118
  168.5 3.3 copy-start.117
  168.5 3.3 copy-start.18
  168.5 3.3 copy-start.82
  168.5 3.3 copy-start.85
  173.3 24.3 %copy-start.30 = (bf16[3,64,512]{2,1,0:T(8,128)(2,1)S(1)}, bf16[3,64,512]{2,1,0:T(8,128)(2,1)}, u32[]{:S(2)}) copy-start(bf16[3,64,512]{2,1,0:T(8,128)(2,1)} %copy-done.29) | copy-start | bytes 589828
  174.0 26.8 %copy-start.12 = (f32[3,512,512]{1,2,0:T(8,128)S(1)}, f32[3,512,512]{1,2,0:T(8,128)}, u32[]{:S(2)}) copy-start(f32[3,512,512]{1,2,0:T(8,128)} %get-tuple-element.179) | copy-start | bytes 9437188
  197.5 3.3 copy-start.91
  208.7 2.5 copy-start
  212.4 3.3 copy-start.3
  212.4 4.2 %copy-start.126 = (f32[512,768]{1,0:T(8,128)S(1)}, f32[512,768]{1,0:T(8,128)}, u32[]{:S(2)}) copy-start(f32[512,768]{1,0:T(8,128)} %get-tuple-element.180) | copy-start | bytes 4718596
  219.3 3.3 copy-start.123
  223.8 2.3 copy-start.5
  223.8 2.3 copy-start.6
  226.1 5.9 %copy-start.103 = (f32[768]{0:T(1024)S(1)}, f32[768]{0:T(1024)}, u32[]{:S(2)}) copy-start(f32[768]{0:T(1024)} %get-tuple-element.106) | copy-start | bytes 9220
  226.1 6.1 %copy-start.62 = (f32[3,3,64]{2,1,0:T(4,128)S(1)}, f32[3,3,64]{2,1,0:T(4,128)}, u32[]{:S(2)}) copy-start(f32[3,3,64]{2,1,0:T(4,128)} %get-tuple-element.104) | copy-start | bytes 6916
  226.1 6.2 %copy-start.98 = (f32[768]{0:T(1024)S(1)}, f32[768]{0:T(1024)}, u32[]{:S(2)}) copy-start(f32[768]{0:T(1024)} %get-tuple-element.188) | copy-start | bytes 9220
  226.1 6.2 %copy-start.69 = (f32[768]{0:T(1024)S(1)}, f32[768]{0:T(1024)}, u32[]{:S(2)}) copy-start(f32[768]{0:T(1024)} %get-tuple-element.193) | copy-start | bytes 9220
  226.1 6.2 %copy-start.61 = (f32[1,768]{1,0:T(1,128)S(1)}, f32[1,768]{1,0:T(1,128)}, u32[]{:S(2)}) copy-start(f32[1,768]{1,0:T(1,128)} %copy-done.60) | copy-start | bytes 9220
  226.1 6.8 %copy-start.102 = (f32[768]{0:T(1024)S(1)}, f32[768]{0:T(1024)}, u32[]{:S(2)}) copy-start(f32[768]{0:T(1024)} %get-tuple-element.80) | copy-start | bytes 9220
  226.2 6.8 %copy-start.101 = (f32[768]{0:T(1024)S(1)}, f32[768]{0:T(1024)}, u32[]{:S(2)}) copy-start(f32[768]{0:T(1024)} %get-tuple-element.79) | copy-start | bytes 9220
  226.2 6.8 %copy-start.100 = (f32[768]{0:T(1024)S(1)}, f32[768]{0:T(1024)}, u32[]{:S(2)}) copy-start(f32[768]{0:T(1024)} %get-tuple-element.81) | copy-start | bytes 9220
  226.2 6.8 %copy-start.99 = (f32[768]{0:T(1024)S(1)}, f32[768]{0:T(1024)}, u32[]{:S(2)}) copy-start(f32[768]{0:T(1024)} %get-tuple-element.82) | copy-start | bytes 9220
  226.2 6.9 %copy-start.97 = (f32[768]{0:T(1024)S(1)}, f32[768]{0:T(1024)}, u32[]{:S(2)}) copy-start(f32[768]{0:T(1024)} %get-tuple-element.124) | copy-start | bytes 9220
  226.2 6.9 %copy-start.96 = (f32[768]{0:T(1024)S(1)}, f32[768]{0:T(1024)}, u32[]{:S(2)}) copy-start(f32[768]{0:T(1024)} %get-tuple-element.85) | copy-start | bytes 9220
  226.2 6.9 %copy-start.95 = (f32[768]{0:T(1024)S(1)}, f32[768]{0:T(1024)}, u32[]{:S(2)}) copy-start(f32[768]{0:T(1024)} %get-tuple-element.125) | copy-start | bytes 9220
  226.2 6.9 %copy-start.94 = (f32[768]{0:T(1024)S(1)}, f32[768]{0:T(1024)}, u32[]{:S(2)}) copy-start(f32[768]{0:T(1024)} %get-tuple-element.84) | copy-start | bytes 9220
  231.9 4.7 %copy-start.28 = (bf16[3,64,512]{2,1,0:T(8,128)(2,1)S(1)}, bf16[3,64,512]{2,1,0:T(8,128)(2,1)}, u32[]{:S(2)}) copy-start(bf16[3,64,512]{2,1,0:T(8,128)(2,1)} %copy-done.27) | copy-start | bytes 589828
  234.6 2.6 copy-start.21
  235.8 3.7 %copy-start.16 = (bf16[2,256,192]{1,2,0:T(8,128)(2,1)}, bf16[2,256,192]{1,2,0:T(8,128)(2,1)S(1)}, u32[]{:S(2)}) copy-start(bf16[2,256,192]{1,2,0:T(8,128)(2,1)S(1)} %copy.166) | copy-start | bytes 589828
  242.8 14.1 %copy-start.32 = (bf16[1,256,384]{2,1,0:T(8,128)(2,1)S(1)}, bf16[1,256,384]{2,1,0:T(8,128)(2,1)}, u32[]{:S(2)}) copy-start(bf16[1,256,384]{2,1,0:T(8,128)(2,1)} %copy.174) | copy-start | bytes 589828
  243.0 15.6 %copy-start.116 = (f32[512]{0:T(512)S(1)}, f32[512]{0:T(512)}, u32[]{:S(2)}) copy-start(f32[512]{0:T(512)} %get-tuple-element.78) | copy-start | bytes 6148
  243.0 15.6 %copy-start.115 = (f32[512]{0:T(512)S(1)}, f32[512]{0:T(512)}, u32[]{:S(2)}) copy-start(f32[512]{0:T(512)} %get-tuple-element.83) | copy-start | bytes 6148
  243.0 15.6 %copy-start.11 = (bf16[2,512,768]{2,1,0:T(8,128)(2,1)S(1)}, bf16[2,512,768]{2,1,0:T(8,128)(2,1)}, u32[]{:S(2)}) copy-start(bf16[2,512,768]{2,1,0:T(8,128)(2,1)} %param.12) | copy-start | bytes 4718596
  262.3 13.6 %copy-start.19 = (bf16[1,2,256,384]{3,2,1,0:T(8,128)(2,1)S(1)}, bf16[1,2,256,384]{3,2,1,0:T(8,128)(2,1)}, u32[]{:S(2)}) copy-start(bf16[1,2,256,384]{3,2,1,0:T(8,128)(2,1)} %maximum_bitcast_fusion.5) | copy-start | bytes 1179652
  337.8 6.0 %copy-start.93 = (f32[8,768]{1,0:T(8,128)S(1)}, f32[8,768]{1,0:T(8,128)}, u32[]{:S(2)}) copy-start(f32[8,768]{1,0:T(8,128)} %get-tuple-element.22) | copy-start | bytes 73732
  (63 other events, 81.6 us)

commit v2 on v0

v2 whole, which is shorter than its diff:
```python
import math

import jax
import jax.numpy as jnp
import numpy as np
from jax import lax
from jax.experimental import pallas as pl
from jax.experimental.pallas import tpu as pltpu
from jax.sharding import PartitionSpec as P

HD = 64
ROT = 16
BLOCK = 128
SEQS = 4
SLOT = 512
D = 768
LOCAL = 192
EPSILON = 1e-05
MASKED = -1e30
MESH = pl.DeviceIdType.MESH
BF = jnp.bfloat16
F32 = jnp.float32
VMEM_LIMIT = 58 * 2**20


def coords():
    dp = lax.axis_index("dp")
    return (
        lax.axis_index("section"),
        dp // 4,
        (dp // 2) % 2,
        dp % 2,
        lax.axis_index("tensor"),
    )


def dp_of(y, x, c):
    return y * 4 + x * 2 + c


def signal_all(targets):
    barrier = pltpu.get_barrier_semaphore()
    for target in targets:
        pl.semaphore_signal(barrier, inc=1, device_id=target, device_id_type=MESH)
    pl.semaphore_wait(barrier, len(targets))


def remote(src, dst, send, recv, target):
    return pltpu.make_async_remote_copy(
        src_ref=src,
        dst_ref=dst,
        send_sem=send,
        recv_sem=recv,
        device_id=target,
        device_id_type=MESH,
    )


def dot(a, b):
    return lax.dot_general(a, b, (((1,), (0,)), ((), ())), preferred_element_type=F32)


def dot_nt(a, b):
    return lax.dot_general(a, b, (((1,), (1,)), ((), ())), preferred_element_type=F32)


def dot_tn(a, b):
    return lax.dot_general(a, b, (((0,), (0,)), ((), ())), preferred_element_type=F32)


def gelu_parts(h):
    tail = 1.0 / (1.0 + (0.3275911 / math.sqrt(2.0)) * jnp.abs(h))
    bell = jnp.exp(h * h * -0.5)
    series = 0.5 * 1.061405429
    for term in (-1.453152027, 1.421413741, -0.284496736, 0.254829592):
        series = series * tail + 0.5 * term
    below = series * tail * bell
    phi = jnp.where(h >= 0.0, 1.0 - below, below)
    return h * phi, phi + h * bell * (1.0 / math.sqrt(2.0 * math.pi))


def col_sum(values):
    return jnp.sum(values, axis=0, keepdims=True)


class Copies:
    def __init__(self, send, recv, to_any):
        self.send, self.recv, self.to_any = send, recv, to_any
        self.numbers = {}
        self.sent = []
        self.done = set()

    def make(self, name, src, dst, to):
        number = self.numbers.setdefault(name, len(self.numbers))
        assert number < SEMS
        return remote(src, dst, self.send.at[number], self.recv.at[number], to)

    def start(self, name, src, dst, to):
        copy = self.make(name, src, dst, to)
        copy.start()
        self.late(name, copy)

    def late(self, name, copy):
        self.sent.append((self.numbers[name], copy))

    def landed(self, name, ref):
        self.make(name, ref, ref, self.to_any).wait_recv()

    def sent_off(self, name, src, dst, to):
        copy = self.make(name, src, dst, to)
        copy.wait_send()
        self.done.add(self.numbers[name])

    def finish(self):
        for number, copy in self.sent:
            if number not in self.done:
                copy.wait_send()


SEMS = 240


def mega_kernel(
    len_ref,
    freq_ref,
    inputs_ref,
    cot_ref,
    wqkv_ref,
    wattn_ref,
    win_ref,
    wout_ref,
    bqkv_ref,
    bin_ref,
    bout_ref,
    gains_ref,
    shifts_ref,
    sec_out,
    grad_out,
    w_out,
    va_out,
    vb_out,
    w,
    vecs,
    x0,
    x1,
    g1,
    g0,
    tables,
    bias,
    normal,
    rstd,
    na,
    nb,
    q,
    k,
    v,
    probs,
    mixp,
    act,
    slope,
    gm,
    gh,
    dqk,
    dv,
    gpre,
    full,
    zrow,
    zcol,
    zland,
    zland_c,
    acts,
    acts_in,
    grads,
    sib,
    xbuf,
    ybuf,
    keep,
    sbuf,
    sbuf_in,
    vec,
    vland,
    stage,
    send,
    recv,
    local,
):
    s, y, x, c, t = coords()
    me = dp_of(y, x, c)
    to_y = {j: {"dp": dp_of((y + j) % 4, x, c)} for j in (1, 2, 3)}
    to_z = {j: {"tensor": (t + j) % 4} for j in (1, 2, 3)}
    to_x = {"dp": dp_of(y, 1 - x, c)}
    to_c = {"dp": dp_of(y, x, 1 - c)}
    to_s = {"section": 1 - s}
    cp = Copies(send, recv, to_c)

    fetch_x = pltpu.make_async_copy(inputs_ref.at[s], x0, local.at[0])
    fetch_g = pltpu.make_async_copy(cot_ref.at[s], g1, local.at[1])
    fetch_x.start()
    fetch_g.start()

    def rows48(block):
        return pl.ds(pl.multiple_of(block * 48, 16), 48)

    eye = (
        lax.broadcasted_iota(jnp.int32, (48, 48), 0) == lax.broadcasted_iota(jnp.int32, (48, 48), 1)
    ).astype(BF)
    w[s, 0, rows48(me), :] = win_ref[...]
    w[s, 1, rows48(me), :] = dot_nt(eye, wout_ref[...]).astype(BF)
    w[s, 2, rows48(me), :] = jnp.concatenate(
        [wqkv_ref[...], dot_nt(eye, wattn_ref[...]).astype(BF)], axis=1
    )
    vecs[s, 0:1, :] = bqkv_ref[...]
    vecs[s, 1:2, :] = bin_ref[...]
    vecs[s, 2:3, :] = bout_ref[...]
    vecs[s, 3:5, :] = gains_ref[...]
    vecs[s, 5:7, :] = shifts_ref[...]
    vecs[s, 7:8, :] = jnp.zeros((1, D), F32)

    signal_all(list(to_y.values()) + list(to_z.values()) + [to_x, to_c, to_s])

    cp.start("swap_w", w.at[s, :, rows48(me)], w.at[s, :, rows48(me)], to_s)
    cp.start("swap_v", vecs.at[s], vecs.at[s], to_s)

    def swapped():
        cp.landed("swap_w", w.at[1 - s, :, rows48(me)])
        cp.landed("swap_v", vecs.at[1 - s])

    def block_of(j, other, core=c):
        return dp_of((y + 4 - j) % 4, (1 - x) if other else x, core)

    def push(l, ch, slot, block, to):
        ref = w.at[l, ch, rows48(block)]
        cp.start(("w", l, ch, slot), ref, ref, to)

    def arrived(l, ch, slot, block):
        cp.landed(("w", l, ch, slot), w.at[l, ch, rows48(block)])

    def gather_first(l):
        for ch in (2, 0, 1):
            if ch < 2:
                for j in (1, 3, 2):
                    push(l, ch, j - 1, me, to_y[j])
                push(l, ch, 3, me, to_x)
            else:
                push(l, ch, 0, me, to_x)
                for j in (1, 3, 2):
                    push(l, ch, j, me, to_y[j])
            push(l, ch, 7, me, to_c)

    def gather_second(l):
        for ch in (2, 0, 1):
            if ch == 2:
                arrived(l, ch, 0, block_of(0, True))
                for j in (1, 3, 2):
                    push(l, ch, 3 + j, block_of(0, True), to_y[j])
                push(l, ch, 8, block_of(0, True), to_c)
            else:
                for j in (1, 3, 2):
                    arrived(l, ch, j - 1, block_of(j, False))
                    push(l, ch, 3 + j, block_of(j, False), to_x)
                    push(l, ch, 7 + 2 * j, block_of(j, False), to_c)

    def gather_third(l):
        for ch in (2, 0, 1):
            if ch < 2:
                for j in (0, 1, 3, 2):
                    arrived(l, ch, 3 + j, block_of(j, True))
                    push(l, ch, 8 + 2 * j, block_of(j, True), to_c)
            else:
                for j in (1, 3, 2):
                    arrived(l, ch, j, block_of(j, False))
                    push(l, ch, 7 + 2 * j, block_of(j, False), to_c)
                for j in (1, 3, 2):
                    arrived(l, ch, 3 + j, block_of(j, True))
                    push(l, ch, 8 + 2 * j, block_of(j, True), to_c)

    def gather_fourth(l, chunks=(0, 1, 2)):
        for ch in chunks:
            for j in range(4):
                arrived(l, ch, 7 + 2 * j, block_of(j, False, 1 - c))
                arrived(l, ch, 8 + 2 * j, block_of(j, True, 1 - c))

    def prepare():
        lens = [len_ref[s, j] for j in range(SEQS)]
        ends, total = [], 0
        for j in range(SEQS):
            total = total + ((lens[j] + (BLOCK - 1)) >> 7)
            ends.append(total)

        def rows_of(i, _):
            at = pl.ds(pl.multiple_of(i * 128, 128), 128)
            row = i * 128 + lax.broadcasted_iota(jnp.int32, (128, SLOT), 0)
            col = lax.broadcasted_iota(jnp.int32, (128, SLOT), 1)
            block = i
            begin = jnp.int32(0)
            owner = jnp.int32(0)
            for j in range(SEQS):
                past = (ends[j] <= block).astype(jnp.int32)
                begin = jnp.maximum(begin, past * ends[j])
                owner = owner + past
            begin = begin * BLOCK
            size = jnp.int32(0)
            for j in range(SEQS):
                size = size + (owner == j).astype(jnp.int32) * lens[j]
            fine = (col >= begin) & (col <= row) & (col < begin + size) | (col == row)
            bias[at, :] = jnp.where(fine, 0.0, MASKED)
            offset = (row[:, :128] - begin).astype(F32)
            angles = offset * freq_ref[...]
            lane = lax.broadcasted_iota(jnp.int32, (128, 128), 1) & 63
            cosines, sines = jnp.cos(angles), jnp.sin(angles)
            tables[0, at, :] = jnp.where(lane < ROT, cosines, 1.0)
            tables[1, at, :] = jnp.where(lane < ROT // 2, -sines, 0.0)
            tables[2, at, :] = jnp.where((lane >= ROT // 2) & (lane < ROT), sines, 0.0)
            return 0

        lax.fori_loop(0, 4, rows_of, 0)

    def turn(values, at, sign):
        ahead = pltpu.roll(values, 384 - ROT // 2, 1)
        behind = pltpu.roll(values, ROT // 2, 1)
        parts = []
        for b in range(3):
            lanes = slice(128 * b, 128 * b + 128)
            change = ahead[:, lanes] * tables[1, at, :] + behind[:, lanes] * tables[2, at, :]
            base = values[:, lanes] * tables[0, at, :]
            parts.append(base + change if sign > 0 else base - change)
        return jnp.concatenate(parts, axis=1)

    def norms(l, x_ref):
        def rows_of(i, _):
            at = pl.ds(pl.multiple_of(i * 64, 64), 64)
            values = x_ref[at, :].astype(F32)
            centred = values - jnp.mean(values, axis=-1, keepdims=True)
            scale = lax.rsqrt(jnp.mean(centred * centred, axis=-1, keepdims=True) + EPSILON)
            unit = centred * scale
            normal[l, at, :] = unit
            rstd[l, at, :] = jnp.broadcast_to(scale, (64, 128))
            na[l, at, :] = (unit * vecs[l, 3:4, :] + vecs[l, 5:6, :]).astype(BF)
            nb[l, at, :] = (unit * vecs[l, 4:5, :] + vecs[l, 6:7, :]).astype(BF)
            return 0

        lax.fori_loop(0, SLOT // 64, rows_of, 0)

    stored = [slice(64 * j * (j + 1), 64 * (j + 1) * (j + 2)) for j in range(4)]

    def attend(l):
        def rows_of(i, _):
            at = pl.ds(pl.multiple_of(i * 256, 256), 256)
            pre = dot(na[l, at, :], w[l, 2, :, 0 : 3 * LOCAL]) + vecs[l, 0:1, 0 : 3 * LOCAL]
            turned = turn(pre[:, 0 : 2 * LOCAL], at, 1)
            for h in range(3):
                q[l, h, at, :] = (turned[:, HD * h : HD * h + HD] * (1.0 / 8.0)).astype(BF)
                k[l, h, at, :] = turned[:, LOCAL + HD * h : LOCAL + HD * h + HD].astype(BF)
                v[l, h, at, :] = pre[:, 2 * LOCAL + HD * h : 2 * LOCAL + HD * h + HD].astype(BF)
            return 0

        lax.fori_loop(0, 2, rows_of, 0)
        mixp[l, :, 0:LOCAL] = jnp.zeros((SLOT, LOCAL), BF)
        for j in range(4):
            rows = slice(128 * j, 128 * j + 128)
            seen = slice(0, 128 * j + 128)
            for h in range(3):
                scores = dot_nt(q[l, h, rows, :], k[l, h, seen, :]) + bias[rows, seen]
                weights = jnp.exp(scores - jnp.max(scores, axis=-1, keepdims=True))
                share = weights * (1.0 / jnp.sum(weights, axis=-1, keepdims=True))
                probs[l, h, :, stored[j]] = share
                out = dot(share.astype(BF), v[l, h, seen, :])
                mixp[l, rows, LOCAL + HD * h : LOCAL + HD * h + HD] = out.astype(BF)

    def feed(l):
        def rows_of(i, _):
            at = pl.ds(pl.multiple_of(i * 256, 256), 256)
            for n in range(3):
                lanes = slice(256 * n, 256 * n + 256)
                hidden = dot(nb[l, at, :], w[l, 0, :, lanes]) + vecs[l, 1:2, lanes]
                value, grade = gelu_parts(hidden)
                act[l, at, lanes] = value.astype(BF)
                slope[l, at, lanes] = grade
            return 0

        lax.fori_loop(0, 2, rows_of, 0)

    def result_rows(l, i, emit):
        rows = slice(256 * i, 256 * i + 256)
        for n in range(3):
            lanes = slice(256 * n, 256 * n + 256)
            part = dot_nt(act[l, rows, :], w[l, 1, lanes, :])
            part = part + dot_nt(mixp[l, rows, :], w[l, 2, lanes, 2 * LOCAL :])
            emit(i, lanes, part)

    def emit_row(use):
        def emit(i, lanes, part):
            zrow[use, 2 * i, :, lanes] = part[0:128].astype(BF)
            zrow[use, 2 * i + 1, :, lanes] = part[128:256].astype(BF)

        return emit

    def emit_full(i, lanes, part):
        full[256 * i : 256 * i + 256, lanes] = part.astype(BF)

    def row_push(use, i):
        for j in (1, 3, 2):
            other = (t + j) % 4

            @pl.when(other // 2 == i)
            def _():
                cp.make(
                    ("zr", use, j), zrow.at[use, other], zland.at[use, j - 1], to_z[j]
                ).start()

    def row_finish(use, extra, with_bias, out_ref):
        for j in (1, 3, 2):
            cp.landed(("zr", use, j), zland.at[use, j - 1])
        mine = pl.ds(pl.multiple_of(t * 128, 128), 128)

        def rows_of(i, _):
            at = pl.ds(pl.multiple_of(i * 32, 32), 32)
            here = pl.ds(pl.multiple_of(t * 128 + i * 32, 32), 32)
            total = extra[here, :].astype(F32) + zrow[use, t, at, :].astype(F32)
            if with_bias is not None:
                total = total + vecs[with_bias, 2:3, :]
            for j in range(3):
                total = total + zland[use, j, at, :].astype(F32)
            out_ref[here, :] = total.astype(BF)
            return 0

        lax.fori_loop(0, 4, rows_of, 0)
        for j in (1, 3, 2):
            cp.start(("za", use, j), out_ref.at[mine], out_ref.at[mine], to_z[j])
        for j in (1, 3, 2):
            name = ("zr", use, j)
            cp.late(name, cp.make(name, zrow.at[use, (t + j) % 4], zland.at[use, j - 1], to_z[j]))

    def row_wait(use, out_ref):
        for j in (1, 3, 2):
            theirs = pl.ds(pl.multiple_of(((t + 4 - j) % 4) * 128, 128), 128)
            cp.landed(("za", use, j), out_ref.at[theirs])

    def pack(ref, out):
        for b in range(4):

            @pl.when(t == b)
            def _():
                for i in range(2):
                    out[:, LOCAL * i : LOCAL * i + LOCAL] = ref[
                        256 * i : 256 * i + 256, LOCAL * b : LOCAL * b + LOCAL
                    ]

    def col_push(use):
        for b in range(4):
            for i in range(2):
                zcol[use, b, :, LOCAL * i : LOCAL * i + LOCAL] = full[
                    256 * i : 256 * i + 256, LOCAL * b : LOCAL * b + LOCAL
                ]
        for j in (1, 3, 2):
            cp.start(
                ("zc", use, j), zcol.at[use, (t + j) % 4], zland_c.at[use, j - 1], to_z[j]
            )

    def col_finish(use, extra, bias_cols, out):
        for j in (1, 3, 2):
            cp.landed(("zc", use, j), zland_c.at[use, j - 1])

        def rows_of(i, _):
            at = pl.ds(pl.multiple_of(i * 64, 64), 64)
            total = extra[at, :].astype(F32) + zcol[use, t, at, :].astype(F32)
            if bias_cols:
                total = total + stage[4, 0:1, 0 : 2 * LOCAL]
            for j in range(3):
                total = total + zland_c[use, j, at, :].astype(F32)
            out[at, :] = total.astype(BF)
            return 0

        lax.fori_loop(0, 4, rows_of, 0)

    def act_push(l, kind):
        @pl.when(s == 1 - l)
        def _():
            cp.make(("act", kind), acts.at[l, kind], acts_in.at[kind], to_s).start()

    def back_heads(l, g_ref):
        def rows_of(i, _):
            at = pl.ds(pl.multiple_of(i * 256, 256), 256)
            mixed = dot(g_ref[at, :], w[l, 2, :, 2 * LOCAL :])
            for h in range(3):
                gm[h, at, :] = mixed[:, LOCAL + HD * h : LOCAL + HD * h + HD].astype(BF)
            for n in range(3):
                lanes = slice(256 * n, 256 * n + 256)
                grad = dot(g_ref[at, :], w[l, 1, :, lanes]) * slope[l, at, lanes]
                gh[at, lanes] = grad.astype(BF)
            return 0

        lax.fori_loop(0, 2, rows_of, 0)

    def back_attend(l):
        for j in (3, 2, 1, 0):
            rows = slice(128 * j, 128 * j + 128)
            seen = slice(0, 128 * j + 128)
            for h in range(3):
                share = probs[l, h, :, stored[j]]
                grad = dot_nt(gm[h, rows, :], v[l, h, seen, :])
                dots = jnp.sum(share * grad, axis=-1, keepdims=True)
                grad = (share * (grad - dots)).astype(BF)
                lanes = slice(HD * h, HD * h + HD)
                key_lanes = slice(LOCAL + HD * h, LOCAL + HD * h + HD)
                dqk[rows, lanes] = dot(grad, k[l, h, seen, :]) * (1.0 / 8.0)
                by_key = dot_tn(grad, q[l, h, rows, :])
                by_value = dot_tn(share.astype(BF), gm[h, rows, :])
                if j == 3:
                    dqk[seen, key_lanes] = by_key
                    dv[seen, lanes] = by_value
                else:
                    dqk[seen, key_lanes] += by_key
                    dv[seen, lanes] += by_value

        def rows_of(i, _):
            at = pl.ds(pl.multiple_of(i * 128, 128), 128)
            gpre[at, 0 : 2 * LOCAL] = turn(dqk[at, :], at, -1).astype(BF)
            gpre[at, 2 * LOCAL :] = jnp.concatenate(
                [dv[at, :], jnp.zeros((128, LOCAL), F32)], axis=1
            ).astype(BF)
            return 0

        lax.fori_loop(0, 4, rows_of, 0)

    def back_norms(l, i, emit):
        rows = slice(256 * i, 256 * i + 256)
        one = dot_nt(gpre[rows, :], w[l, 2])
        two = dot_nt(gh[rows, :], w[l, 0])
        unit = normal[l, rows, :]
        sums = [col_sum(one * unit), col_sum(two * unit), col_sum(one), col_sum(two)]
        for n, value in enumerate(sums):
            row = slice(8 + 4 * l + n, 9 + 4 * l + n)
            vec[row, :] = value if i == 0 else vec[row, :] + value
        mixture = one * vecs[l, 3:4, :] + two * vecs[l, 4:5, :]
        first = jnp.mean(mixture, axis=-1, keepdims=True)
        second = jnp.mean(mixture * unit, axis=-1, keepdims=True)
        part = rstd[l, rows, 0:1] * (mixture - first - unit * second)
        emit(i, slice(0, D), part)

    def sums_of(l, g_ref):
        for n, ref in enumerate((gpre, gh, g_ref)):
            row = slice(4 * l + n, 4 * l + n + 1)
            vec[row, :] = col_sum(ref[...].astype(F32))
        vec[4 * l + 3 : 4 * l + 4, :] = jnp.zeros((1, D), F32)

    def weights_of(l, ch, g_ref):
        def rows_of(m, _):
            lanes = pl.ds(pl.multiple_of(m * 384, 128), 384)
            if ch == 0:
                value = dot_tn(nb[l, :, lanes], gh[...])
            elif ch == 1:
                value = dot_tn(g_ref[:, lanes], act[l])
            else:
                value = dot_tn(na[l, :, lanes], gpre[...])
                other = dot_tn(g_ref[:, lanes], mixp[l])
                value = jnp.concatenate(
                    [value[:, 0 : 2 * LOCAL], value[:, 2 * LOCAL :] + other], axis=1
                )
            grads[ch, pl.ds(4 * m, 4)] = value.astype(BF).reshape(4, 2, 48, D)
            return 0

        lax.fori_loop(0, 2, rows_of, 0)
        cp.start(("rc", l, ch), grads.at[ch, :, 1 - c], sib.at[l, ch], to_c)

    def weights_gone(l, ch):
        cp.sent_off(("rc", l, ch), grads.at[ch, :, 1 - c], sib.at[l, ch], to_c)

    def reduce_core(l, ch):
        cp.landed(("rc", l, ch), sib.at[l, ch])

        def add(i, _):
            sib[l, ch, i] = (sib[l, ch, i].astype(F32) + grads[ch, i, c].astype(F32)).astype(BF)
            return 0

        lax.fori_loop(0, 8, add, 0)
        if ch < 2:
            for j in (1, 3, 2, 0):
                yy = (y + j) % 4
                cp.start(("rx", l, ch, j), sib.at[l, ch, yy * 2 + 1 - x], xbuf.at[l, ch, yy], to_x)
        else:
            for j in (1, 3, 2):
                yy = (y + j) % 4
                cp.start(
                    ("ry", l, ch, j),
                    sib.at[l, ch, pl.ds(yy * 2, 2)],
                    ybuf.at[l, pl.ds(2 * (j - 1), 2)],
                    to_y[j],
                )

    def reduce_mid(l, ch):
        if ch < 2:
            for j in (1, 3, 2, 0):
                yy = (y + j) % 4
                cp.landed(("rx", l, ch, j), xbuf.at[l, ch, yy])
                mine = yy * 2 + x
                xbuf[l, ch, yy] = (
                    sib[l, ch, mine].astype(F32) + xbuf[l, ch, yy].astype(F32)
                ).astype(BF)
                if j:
                    cp.start(
                        ("ry", l, ch, j),
                        xbuf.at[l, ch, yy],
                        ybuf.at[l, 6 + ch * 3 + j - 1],
                        to_y[j],
                    )
        else:
            for j in (1, 3, 2):
                cp.landed(("ry", l, ch, j), ybuf.at[l, pl.ds(2 * (j - 1), 2)])
            for i in range(2):
                total = sib[l, 2, y * 2 + i].astype(F32)
                for j in range(3):
                    total = total + ybuf[l, 2 * j + i].astype(F32)
                keep[l, i] = total.astype(BF)
            cp.start(("rx", l, ch, 0), keep.at[l, 1 - x], keep.at[l, 2], to_x)

    def reduce_end(l, ch):
        if ch < 2:
            total = xbuf[l, ch, y].astype(F32)
            for j in (1, 3, 2):
                cp.landed(("ry", l, ch, j), ybuf.at[l, 6 + ch * 3 + j - 1])
            for j in range(3):
                total = total + ybuf[l, 6 + ch * 3 + j].astype(F32)
        else:
            cp.landed(("rx", l, ch, 0), keep.at[l, 2])
            total = keep[l, x].astype(F32) + keep[l, 2].astype(F32)
        sbuf[l, ch] = total.astype(BF)

        @pl.when(s == 1 - l)
        def _():
            cp.make(("rs", ch), sbuf.at[l, ch], sbuf_in.at[ch], to_s).start()

    @pl.when(s == 1)
    def _():
        swapped()

    gather_first(0)
    prepare()
    fetch_x.wait()
    gather_second(0)

    @pl.when(s == 0)
    def _():
        swapped()

    norms(0, x0)
    gather_third(0)
    gather_first(1)
    gather_fourth(0, (2,))
    attend(0)
    gather_second(1)
    gather_fourth(0, (0, 1))
    feed(0)
    result_rows(0, 0, emit_row(0))
    row_push(0, 0)
    result_rows(0, 1, emit_row(0))
    row_push(0, 1)
    gather_third(1)
    row_finish(0, x0, 0, x1)
    gather_fourth(1)
    fetch_g.wait()
    row_wait(0, x1)

    pack(x1, acts.at[0, 0])
    act_push(0, 0)
    norms(1, x1)
    attend(1)
    feed(1)
    result_rows(1, 0, emit_full)
    result_rows(1, 1, emit_full)
    col_push(0)

    back_heads(1, g1)
    back_attend(1)
    back_norms(1, 0, emit_row(1))
    row_push(1, 0)
    back_norms(1, 1, emit_row(1))
    row_push(1, 1)
    weights_of(1, 1, g1)
    weights_of(1, 0, g1)
    row_finish(1, g1, None, g0)
    weights_of(1, 2, g1)
    sums_of(1, g1)
    for b in range(4):

        @pl.when(t == b)
        def _():
            for i in range(2):
                stage[4, 0:1, LOCAL * i : LOCAL * i + LOCAL] = vecs[
                    1, 2:3, LOCAL * b : LOCAL * b + LOCAL
                ]

    col_finish(0, acts.at[0, 0], True, acts.at[1, 0])
    act_push(1, 0)
    reduce_core(1, 1)
    reduce_core(1, 0)
    reduce_core(1, 2)
    row_wait(1, g0)

    for ch in range(3):
        weights_gone(1, ch)
    pack(g0, acts.at[1, 1])
    act_push(1, 1)
    back_heads(0, g0)
    reduce_mid(1, 1)
    reduce_mid(1, 0)
    reduce_mid(1, 2)
    weights_of(0, 1, g0)
    weights_of(0, 0, g0)
    back_attend(0)
    for ch in (1, 0, 2):
        reduce_end(1, ch)
    back_norms(0, 0, emit_full)
    back_norms(0, 1, emit_full)
    col_push(1)
    sums_of(0, g0)
    vland[t, 0:8] = vec[8:16, :]
    for j in (1, 2, 3):
        cp.start(("vz", j), vec.at[pl.ds(8, 8)], vland.at[t, pl.ds(0, 8)], to_z[j])
    weights_of(0, 2, g0)
    reduce_core(0, 1)
    reduce_core(0, 0)
    for j in (1, 2, 3):
        cp.landed(("vz", j), vland.at[(t + 4 - j) % 4, pl.ds(0, 8)])
    stage[0, 0:8] = vec[0:8, :]
    stage[0, 8:16] = vland[0, 0:8] + vland[1, 0:8] + vland[2, 0:8] + vland[3, 0:8]
    cp.start("vc", stage.at[0], vland.at[4], to_c)
    reduce_core(0, 2)
    cp.landed("vc", vland.at[4])
    stage[1] = stage[0] + vland[4]
    cp.start("vx", stage.at[1], vland.at[5], to_x)
    reduce_mid(0, 1)
    reduce_mid(0, 0)
    cp.landed("vx", vland.at[5])
    stage[2] = stage[1] + vland[5]
    cp.start("vs", stage.at[2], vland.at[6], to_s)
    col_finish(1, acts.at[1, 1], False, acts.at[0, 1])
    act_push(0, 1)
    reduce_mid(0, 2)
    cp.landed("vs", vland.at[6])
    stage[3] = stage[2] + vland[6]
    vland[7 + y] = stage[3]
    for j in (1, 2, 3):
        cp.start(("vy", j), stage.at[3], vland.at[7 + y], to_y[j])
    for ch in (1, 0, 2):
        reduce_end(0, ch)

    def unpack(out, ref, m):
        out[m, 0:256, :] = ref[:, 0:LOCAL]
        out[m, 256:512, :] = ref[:, LOCAL : 2 * LOCAL]

    unpack(sec_out, acts.at[s, 0], s)
    unpack(grad_out, acts.at[s, 1], s)
    cp.landed(("act", 0), acts_in.at[0])
    unpack(sec_out, acts_in.at[0], 1 - s)
    cp.landed(("act", 1), acts_in.at[1])
    unpack(grad_out, acts_in.at[1], 1 - s)
    for j in (1, 2, 3):
        cp.landed(("vy", j), vland.at[7 + (y + 4 - j) % 4])
    stage[4] = vland[7] + vland[8] + vland[9] + vland[10]
    va_out[...] = stage[4, 0:8]
    vb_out[...] = stage[4, 8:16]
    for ch in (1, 0, 2):
        cp.landed(("rs", ch), sbuf_in.at[ch])
        w_out[ch] = sbuf[s, ch].astype(F32) + sbuf_in[ch].astype(F32)
        name = ("rs", ch)
        cp.late(name, cp.make(name, sbuf.at[1 - s, ch], sbuf_in.at[ch], to_s))
    for kind in range(2):
        name = ("act", kind)
        cp.late(name, cp.make(name, acts.at[1 - s, kind], acts_in.at[kind], to_s))
    cp.finish()


def mega(*arguments):
    dma = pltpu.SemaphoreType.DMA
    vmem = pl.BlockSpec(memory_space=pltpu.VMEM)
    smem = pl.BlockSpec(memory_space=pltpu.SMEM)
    anywhere = pl.BlockSpec(memory_space=pl.ANY)

    def bf(*shape):
        return pltpu.VMEM(shape, BF)

    def f32(*shape):
        return pltpu.VMEM(shape, F32)

    return pl.pallas_call(
        mega_kernel,
        out_shape=[
            jax.ShapeDtypeStruct((2, SLOT, LOCAL), BF),
            jax.ShapeDtypeStruct((2, SLOT, LOCAL), BF),
            jax.ShapeDtypeStruct((3, 48, D), F32),
            jax.ShapeDtypeStruct((8, D), F32),
            jax.ShapeDtypeStruct((8, D), F32),
        ],
        in_specs=[smem, vmem, anywhere, anywhere] + [vmem] * 9,
        out_specs=[vmem] * 5,
        scratch_shapes=[
            bf(2, 3, D, D),
            f32(2, 8, D),
            bf(SLOT, D),
            bf(SLOT, D),
            bf(SLOT, D),
            bf(SLOT, D),
            f32(3, SLOT, 128),
            f32(SLOT, SLOT),
            f32(2, SLOT, D),
            f32(2, SLOT, 128),
            bf(2, SLOT, D),
            bf(2, SLOT, D),
            bf(2, 3, SLOT, HD),
            bf(2, 3, SLOT, HD),
            bf(2, 3, SLOT, HD),
            f32(2, 3, 128, 1280),
            bf(2, SLOT, 2 * LOCAL),
            bf(2, SLOT, D),
            f32(2, SLOT, D),
            bf(3, SLOT, HD),
            bf(SLOT, D),
            f32(SLOT, 2 * LOCAL),
            f32(SLOT, LOCAL),
            bf(SLOT, D),
            bf(SLOT, D),
            bf(2, 4, 128, D),
            bf(2, 4, 256, 2 * LOCAL),
            bf(2, 3, 128, D),
            bf(2, 3, 256, 2 * LOCAL),
            bf(2, 2, 256, 2 * LOCAL),
            bf(2, 256, 2 * LOCAL),
            bf(3, 8, 2, 48, D),
            bf(2, 3, 8, 48, D),
            bf(2, 2, 4, 48, D),
            bf(2, 12, 48, D),
            bf(2, 3, 48, D),
            bf(2, 3, 48, D),
            bf(3, 48, D),
            f32(16, D),
            f32(11, 16, D),
            f32(5, 16, D),
            dma((SEMS,)),
            dma((SEMS,)),
            dma((2,)),
        ],
        compiler_params=pltpu.CompilerParams(
            collective_id=0, has_side_effects=True, vmem_limit_bytes=VMEM_LIMIT
        ),
        name="two_layers",
    )(*arguments)


def body(
    inputs,
    cotangent,
    seq_lengths,
    w_qkv,
    b_qkv,
    w_attn_out,
    w_in,
    b_in,
    w_out,
    b_out,
    norm_gains,
    norm_biases,
):
    s = lax.axis_index("section")
    powers = 1.0 / 10000.0 ** (np.arange(ROT // 2, dtype=np.float32) * 2.0 / ROT)
    freq = jnp.asarray(np.tile(powers.astype(np.float32), 128 // (ROT // 2))[None])
    qkv_bias = jnp.pad(b_qkv.reshape(1, -1), ((0, 0), (0, LOCAL)))
    sec, grad, w_sums, va, vb = mega(
        seq_lengths[:, 0],
        freq,
        inputs,
        cotangent,
        w_qkv[0].reshape(48, 3 * LOCAL),
        w_attn_out[0],
        w_in[0],
        w_out[0],
        qkv_bias,
        b_in,
        b_out,
        norm_gains[0],
        norm_biases[0],
    )
    va = lax.dynamic_slice_in_dim(va, s * 4, 4, 0)
    vb = lax.dynamic_slice_in_dim(vb, s * 4, 4, 0)
    return (
        sec[None],
        grad[None],
        w_sums[2, :, : 3 * LOCAL].reshape(1, 48, 3, LOCAL),
        va[0, : 3 * LOCAL].reshape(1, 3, LOCAL),
        w_sums[2, :, 3 * LOCAL :].T[None],
        w_sums[0][None],
        va[1][None],
        w_sums[1].T[None],
        va[2][None],
        vb[0:2][None],
        vb[2:4][None],
    )


def solution(mesh):
    return jax.shard_map(
        body,
        mesh=mesh,
        in_specs=(
            P(None, "dp", None),
            P(None, "dp", None),
            P(None, "dp", None),
            P("section", "dp", None, "tensor"),
            P("section", None, "tensor"),
            P("section", "tensor", "dp"),
            P("section", "dp", "tensor"),
            P("section", "tensor"),
            P("section", "tensor", "dp"),
            P("section", None),
            P("section", None, None),
            P("section", None, None),
        ),
        out_specs=(
            P("section", None, "dp", "tensor"),
            P("section", None, "dp", "tensor"),
            P("section", "dp", None, "tensor"),
            P("section", None, "tensor"),
            P("section", "tensor", "dp"),
            P("section", "dp", "tensor"),
            P("section", "tensor"),
            P("section", "tensor", "dp"),
            P("section", None),
            P("section", None, None),
            P("section", None, None),
        ),
        check_vma=False,
    )
```

time: 952 us -> 174 us (0.18)
  blocking collectives: 355 us -> 0 us
  waiting for transfers between devices: 341 us -> 0 us
  Pallas kernels: 0 us -> 155 us
  matrix products: 114 us -> 0 us
  other arithmetic: 74.6 us -> 0.7 us
  between operations: 17.4 us -> 0.69 us
  starting transfers between devices: 14.7 us -> 0 us
  local copies, waits for them, and re-layouts: 26.6 us -> 15.2 us
    psum x2 -> x0, blocking collectives: 309 us -> none  [the longest x1 278 us: body(): lax.psum((vector_sums[3], vector_sums[4]), ('dp', 'tensor'))]
    psum x4 -> x0, waiting for transfers between devices: 200 us -> none  [the longest x3 160 us: body(): lax.psum(partial_sum.astype(jnp.bfloat16), 'tensor').astype(jnp.float32)]
    pallas_call x0 -> x1, Pallas kernels: none -> 155 us  [mega(): pl.pallas_call(mega_kernel, out_shape=[jax.ShapeDtypeStruct((2, SLOT, LOC...]
    dot_general x57 -> x0, matrix products: 114 us -> none  [the longest x3 16.1 us: body(): jnp.dot(forward_normed_two, in_full, preferred_element_type=jnp.float32)]
    unnamed x11 -> x0, waiting for transfers between devices: 55 us -> none
    all_gather x2 -> x0, blocking collectives: 46 us -> none  [the longest x1 28 us: body(): lax.all_gather(w_qkv[0], 'dp', axis=0, tiled=True)]
    ppermute x4 -> x0, waiting for transfers between devices: 43.6 us -> none  [from_behind(): return lax.ppermute(shard, axis, pairs)]
    reduce_scatter x3 -> x0, waiting for transfers between devices: 41.7 us -> none  [the longest x1 41.7 us: body(): lax.psum_scatter(weight_sums[0].astype(jnp.bfloat16), 'dp', scatter_dimen...]
  transfers between devices with their start and end apart: 14 -> 0, of which waited for: 10 -> 0; matrix products, arithmetic and copies ran while one was open for 13% -> 0% of each run, Pallas kernels for 0% -> 0%
where the time goes in v2:
time: 174 us; the launch traced here: 171 us
  Pallas kernels  155 us (89%)
  local copies, waits for them, and re-layouts  15.2 us (9%)
    pallas_call x1, Pallas kernels, mega(): pl.pallas_call(mega_kernel, out_shape=[jax.ShapeDtypeStruct((2, SLOT, LOC...  155 us
    unnamed x10, local copies, waits for them, and re-layouts  8.8 us

profile of v2, /device:TPU:0, one launch (start us, length us, event | category | flops | bytes accessed | tf_op | source)
XLA Modules:
  0.0 171.4 jit_solution(12480532751018584091)
XLA Ops:
  0.6 0.9 copy.31
  1.6 0.7 reshape_squeeze.9.wqkv_ref
  2.3 1.5 copy.32
  3.8 1.7 copy.33
  5.5 0.7 reduce
  6.2 0.1 reshape.25
  6.3 0.6 pad.4.bqkv_ref
  6.8 154.9 %two_layers.1 = (bf16[2,512,192]{2,1,0:T(8,128)(2,1)}, bf16[2,512,192]{2,1,0:T(8,128)(2,1)}, f32[3,48,768]{2,1,0:T(8,128)}, f32[8,768]{1,0:T(8,128)}, f32[8,768]{1,0:T(8,128)}) custom-call(s32[2,4]{1,0:T(2,128)} %bitcast.31, f32[1,128]{1,0:T(1,128)} %constant.16.clone.freq_ref, bf16[2,512,768]{2,1,0:T(8,128)(2,1)} %inputs_ref.1, ...), custom_call_target="tpu_custom_call" | custom-call | tf_op jit(solution)/shard_map/two_layers/pallas_call | solution.py:786
  161.7 0.0 copy-start
  161.7 0.0 copy-start.1
  161.7 2.0 %copy.34 = bf16[1,2,512,192]{2,3,1,0:T(8,128)(2,1)} copy(bf16[1,2,512,192]{3,2,1,0:T(8,128)(2,1)} %bitcast.26) | data formatting | bytes 786432
  163.8 2.0 %copy.35 = bf16[1,2,512,192]{2,3,1,0:T(8,128)(2,1)} copy(bf16[1,2,512,192]{3,2,1,0:T(8,128)(2,1)} %bitcast.25) | data formatting | bytes 786432
  165.8 0.0 copy-done
  165.8 0.1 reshape_squeeze.10
  165.9 0.7 copy.36
  166.6 0.7 dynamic-slice_reduce_fusion
  167.3 0.7 reshape_squeeze.12
  168.0 0.7 slice_bitcast_fusion.1
  168.7 0.7 slice_bitcast_fusion
  169.4 1.4 constant_dynamic-slice_fusion.1
  170.8 0.0 copy-done.1
  170.8 0.6 dynamic-slice_bitcast_fusion
  (1 shorter events, 0.0 us)
Async XLA Ops:
  161.7 4.0 %copy-start = (f32[3,48,768]{2,1,0:T(8,128)S(1)}, f32[3,48,768]{2,1,0:T(8,128)}, u32[]{:S(2)}) copy-start(f32[3,48,768]{2,1,0:T(8,128)} %get-tuple-element.18) | copy-start | bytes 1327108
  161.7 9.1 %copy-start.1 = (f32[8,768]{1,0:T(8,128)S(1)}, f32[8,768]{1,0:T(8,128)}, u32[]{:S(2)}) copy-start(f32[8,768]{1,0:T(8,128)} %get-tuple-element.20) | copy-start | bytes 73732

commit v3 on v2

v3 whole, which is shorter than its diff:
```python
import math

import jax
import jax.numpy as jnp
import numpy as np
from jax import lax
from jax.experimental import pallas as pl
from jax.experimental.pallas import tpu as pltpu
from jax.sharding import PartitionSpec as P

HD = 64
ROT = 16
BLOCK = 128
SEQS = 4
SLOT = 512
D = 768
LOCAL = 192
EPSILON = 1e-05
MASKED = -1e30
MESH = pl.DeviceIdType.MESH
BF = jnp.bfloat16
F32 = jnp.float32
VMEM_LIMIT = 58 * 2**20


def coords():
    dp = lax.axis_index("dp")
    return (
        lax.axis_index("section"),
        dp // 4,
        (dp // 2) % 2,
        dp % 2,
        lax.axis_index("tensor"),
    )


def dp_of(y, x, c):
    return y * 4 + x * 2 + c


def signal_all(targets):
    barrier = pltpu.get_barrier_semaphore()
    for target in targets:
        pl.semaphore_signal(barrier, inc=1, device_id=target, device_id_type=MESH)
    pl.semaphore_wait(barrier, len(targets))


def remote(src, dst, send, recv, target):
    return pltpu.make_async_remote_copy(
        src_ref=src,
        dst_ref=dst,
        send_sem=send,
        recv_sem=recv,
        device_id=target,
        device_id_type=MESH,
    )


def dot(a, b):
    return lax.dot_general(a, b, (((1,), (0,)), ((), ())), preferred_element_type=F32)


def dot_nt(a, b):
    return lax.dot_general(a, b, (((1,), (1,)), ((), ())), preferred_element_type=F32)


def dot_tn(a, b):
    return lax.dot_general(a, b, (((0,), (0,)), ((), ())), preferred_element_type=F32)


def gelu_parts(h):
    tail = 1.0 / (1.0 + (0.3275911 / math.sqrt(2.0)) * jnp.abs(h))
    bell = jnp.exp(h * h * -0.5)
    series = 0.5 * 1.061405429
    for term in (-1.453152027, 1.421413741, -0.284496736, 0.254829592):
        series = series * tail + 0.5 * term
    below = series * tail * bell
    phi = jnp.where(h >= 0.0, 1.0 - below, below)
    return h * phi, phi + h * bell * (1.0 / math.sqrt(2.0 * math.pi))


def col_sum(values):
    return jnp.sum(values, axis=0, keepdims=True)


class Copies:
    def __init__(self, send, recv, to_any):
        self.send, self.recv, self.to_any = send, recv, to_any
        self.numbers = {}
        self.sent = []
        self.done = set()

    def make(self, name, src, dst, to):
        number = self.numbers.setdefault(name, len(self.numbers))
        assert number < SEMS
        return remote(src, dst, self.send.at[number], self.recv.at[number], to)

    def start(self, name, src, dst, to):
        copy = self.make(name, src, dst, to)
        copy.start()
        self.late(name, copy)

    def late(self, name, copy):
        self.sent.append((self.numbers[name], copy))

    def landed(self, name, ref):
        self.make(name, ref, ref, self.to_any).wait_recv()

    def sent_off(self, name, src, dst, to):
        copy = self.make(name, src, dst, to)
        copy.wait_send()
        self.done.add(self.numbers[name])

    def finish(self):
        for number, copy in self.sent:
            if number not in self.done:
                copy.wait_send()


SEMS = 240


def mega_kernel(
    len_ref,
    freq_ref,
    inputs_ref,
    cot_ref,
    wqkv_ref,
    wattn_ref,
    win_ref,
    wout_ref,
    bqkv_ref,
    bin_ref,
    bout_ref,
    gains_ref,
    shifts_ref,
    acts_out,
    w_out,
    vec_out,
    w,
    vecs,
    x0,
    x1,
    g1,
    g0,
    tables,
    bias,
    normal,
    rstd,
    na,
    nb,
    q,
    k,
    v,
    probs,
    mixp,
    act,
    slope,
    gm,
    gh,
    dqk,
    dv,
    gpre,
    full,
    zrow,
    zcol,
    zland,
    zland_c,
    acts,
    acts_in,
    grads,
    sib,
    xbuf,
    ybuf,
    keep,
    sbuf,
    sbuf_in,
    vec,
    vland,
    stage,
    send,
    recv,
    local,
):
    s, y, x, c, t = coords()
    me = dp_of(y, x, c)
    to_y = {j: {"dp": dp_of((y + j) % 4, x, c)} for j in (1, 2, 3)}
    to_z = {j: {"tensor": (t + j) % 4} for j in (1, 2, 3)}
    to_x = {"dp": dp_of(y, 1 - x, c)}
    to_c = {"dp": dp_of(y, x, 1 - c)}
    to_s = {"section": 1 - s}
    cp = Copies(send, recv, to_c)

    fetch_x = pltpu.make_async_copy(inputs_ref.at[s], x0, local.at[0])
    fetch_g = pltpu.make_async_copy(cot_ref.at[s], g1, local.at[1])
    fetch_x.start()
    fetch_g.start()

    def rows48(block):
        return pl.ds(pl.multiple_of(block * 48, 16), 48)

    w[s, 0, rows48(me), :] = win_ref[...]
    w[s, 1, rows48(me), :] = wout_ref[...]
    w[s, 2, rows48(me), :] = jnp.concatenate(
        [wqkv_ref[0], wqkv_ref[1], wqkv_ref[2], wattn_ref[...]], axis=1
    )
    vecs[s, 0:1, :] = jnp.concatenate(
        [bqkv_ref[0], bqkv_ref[1], bqkv_ref[2], jnp.zeros((1, LOCAL), F32)], axis=1
    )
    vecs[s, 1:2, :] = bin_ref[...]
    vecs[s, 2:3, :] = bout_ref[...]
    vecs[s, 3:5, :] = gains_ref[...]
    vecs[s, 5:7, :] = shifts_ref[...]
    vecs[s, 7:8, :] = jnp.zeros((1, D), F32)

    signal_all(list(to_y.values()) + list(to_z.values()) + [to_x, to_c, to_s])

    cp.start("swap_w", w.at[s, :, rows48(me)], w.at[s, :, rows48(me)], to_s)
    cp.start("swap_v", vecs.at[s], vecs.at[s], to_s)

    def swapped():
        cp.landed("swap_w", w.at[1 - s, :, rows48(me)])
        cp.landed("swap_v", vecs.at[1 - s])

    def block_of(j, other, core=c):
        return dp_of((y + 4 - j) % 4, (1 - x) if other else x, core)

    def push(l, ch, slot, block, to):
        ref = w.at[l, ch, rows48(block)]
        cp.start(("w", l, ch, slot), ref, ref, to)

    def arrived(l, ch, slot, block):
        cp.landed(("w", l, ch, slot), w.at[l, ch, rows48(block)])

    def gather_first(l, ch):
        if ch == 1:
            for j in (1, 3, 2):
                push(l, ch, j - 1, me, to_y[j])
            push(l, ch, 3, me, to_x)
        else:
            push(l, ch, 0, me, to_x)
            for j in (1, 3, 2):
                push(l, ch, j, me, to_y[j])
        push(l, ch, 7, me, to_c)

    def gather_second(l, ch):
        if ch == 1:
            for j in (1, 3, 2):
                arrived(l, ch, j - 1, block_of(j, False))
                push(l, ch, 3 + j, block_of(j, False), to_x)
                push(l, ch, 7 + 2 * j, block_of(j, False), to_c)
        else:
            arrived(l, ch, 0, block_of(0, True))
            for j in (1, 3, 2):
                push(l, ch, 3 + j, block_of(0, True), to_y[j])
            push(l, ch, 8, block_of(0, True), to_c)

    def gather_third(l, ch):
        if ch == 1:
            for j in (0, 1, 3, 2):
                arrived(l, ch, 3 + j, block_of(j, True))
                push(l, ch, 8 + 2 * j, block_of(j, True), to_c)
        else:
            for j in (1, 3, 2):
                arrived(l, ch, j, block_of(j, False))
                push(l, ch, 7 + 2 * j, block_of(j, False), to_c)
            for j in (1, 3, 2):
                arrived(l, ch, 3 + j, block_of(j, True))
                push(l, ch, 8 + 2 * j, block_of(j, True), to_c)

    def gather_fourth(l, ch):
        for j in range(4):
            arrived(l, ch, 7 + 2 * j, block_of(j, False, 1 - c))
            arrived(l, ch, 8 + 2 * j, block_of(j, True, 1 - c))

    def prepare():
        lens = [len_ref[s, j] for j in range(SEQS)]
        ends, total = [], 0
        for j in range(SEQS):
            total = total + ((lens[j] + (BLOCK - 1)) >> 7)
            ends.append(total)

        def rows_of(i, _):
            at = pl.ds(pl.multiple_of(i * 128, 128), 128)
            row = i * 128 + lax.broadcasted_iota(jnp.int32, (128, SLOT), 0)
            col = lax.broadcasted_iota(jnp.int32, (128, SLOT), 1)
            block = i
            begin = jnp.int32(0)
            owner = jnp.int32(0)
            for j in range(SEQS):
                past = (ends[j] <= block).astype(jnp.int32)
                begin = jnp.maximum(begin, past * ends[j])
                owner = owner + past
            begin = begin * BLOCK
            size = jnp.int32(0)
            for j in range(SEQS):
                size = size + (owner == j).astype(jnp.int32) * lens[j]
            fine = (col >= begin) & (col <= row) & (col < begin + size) | (col == row)
            bias[at, :] = jnp.where(fine, 0.0, MASKED)
            offset = (row[:, :128] - begin).astype(F32)
            angles = offset * freq_ref[...]
            lane = lax.broadcasted_iota(jnp.int32, (128, 128), 1) & 63
            cosines, sines = jnp.cos(angles), jnp.sin(angles)
            tables[0, at, :] = jnp.where(lane < ROT, cosines, 1.0)
            tables[1, at, :] = jnp.where(lane < ROT // 2, -sines, 0.0)
            tables[2, at, :] = jnp.where((lane >= ROT // 2) & (lane < ROT), sines, 0.0)
            return 0

        lax.fori_loop(0, 4, rows_of, 0)

    def turn(values, at, sign):
        ahead = pltpu.roll(values, 384 - ROT // 2, 1)
        behind = pltpu.roll(values, ROT // 2, 1)
        parts = []
        for b in range(3):
            lanes = slice(128 * b, 128 * b + 128)
            change = ahead[:, lanes] * tables[1, at, :] + behind[:, lanes] * tables[2, at, :]
            base = values[:, lanes] * tables[0, at, :]
            parts.append(base + change if sign > 0 else base - change)
        return jnp.concatenate(parts, axis=1)

    def norms(l, x_ref, half):
        def rows_of(i, _):
            at = pl.ds(pl.multiple_of(256 * half + i * 64, 64), 64)
            values = x_ref[at, :].astype(F32)
            centred = values - jnp.mean(values, axis=-1, keepdims=True)
            scale = lax.rsqrt(jnp.mean(centred * centred, axis=-1, keepdims=True) + EPSILON)
            unit = centred * scale
            normal[l, at, :] = unit
            rstd[l, at, :] = jnp.broadcast_to(scale, (64, 128))
            na[l, at, :] = (unit * vecs[l, 3:4, :] + vecs[l, 5:6, :]).astype(BF)
            nb[l, at, :] = (unit * vecs[l, 4:5, :] + vecs[l, 6:7, :]).astype(BF)
            return 0

        lax.fori_loop(0, 4, rows_of, 0)

    stored = [slice(64 * j * (j + 1), 64 * (j + 1) * (j + 2)) for j in range(4)]

    def project(l, half):
        at = slice(256 * half, 256 * half + 256)
        pre = dot(na[l, at, :], w[l, 2, :, 0 : 3 * LOCAL]) + vecs[l, 0:1, 0 : 3 * LOCAL]
        turned = turn(pre[:, 0 : 2 * LOCAL], at, 1)
        for h in range(3):
            q[l, h, at, :] = (turned[:, HD * h : HD * h + HD] * (1.0 / 8.0)).astype(BF)
            k[l, h, at, :] = turned[:, LOCAL + HD * h : LOCAL + HD * h + HD].astype(BF)
            v[l, h, at, :] = pre[:, 2 * LOCAL + HD * h : 2 * LOCAL + HD * h + HD].astype(BF)
        mixp[l, at, 0:LOCAL] = jnp.zeros((256, LOCAL), BF)

    def attend(l, j):
        rows = slice(128 * j, 128 * j + 128)
        seen = slice(0, 128 * j + 128)
        for h in range(3):
            scores = dot_nt(q[l, h, rows, :], k[l, h, seen, :]) + bias[rows, seen]
            weights = jnp.exp(scores - jnp.max(scores, axis=-1, keepdims=True))
            share = weights * (1.0 / jnp.sum(weights, axis=-1, keepdims=True))
            probs[l, h, :, stored[j]] = share
            out = dot(share.astype(BF), v[l, h, seen, :])
            mixp[l, rows, LOCAL + HD * h : LOCAL + HD * h + HD] = out.astype(BF)

    def feed(l, half):
        at = slice(256 * half, 256 * half + 256)
        for n in range(3):
            lanes = slice(256 * n, 256 * n + 256)
            hidden = dot(nb[l, at, :], w[l, 0, :, lanes]) + vecs[l, 1:2, lanes]
            value, grade = gelu_parts(hidden)
            act[l, at, lanes] = value.astype(BF)
            slope[l, at, lanes] = grade

    def result_rows(l, i, emit):
        rows = slice(256 * i, 256 * i + 256)
        for n in range(3):
            lanes = slice(256 * n, 256 * n + 256)
            part = dot_nt(act[l, rows, :], w[l, 1, lanes, :])
            part = part + dot_nt(mixp[l, rows, :], w[l, 2, lanes, 2 * LOCAL :])
            emit(i, lanes, part)

    def emit_row(use):
        def emit(i, lanes, part):
            for b in range(4):
                zrow[use, i, b, :, lanes] = part[64 * b : 64 * b + 64].astype(BF)

        return emit

    def emit_full(i, lanes, part):
        full[256 * i : 256 * i + 256, lanes] = part.astype(BF)

    def shared(i, b):
        return pl.ds(pl.multiple_of(256 * i + b * 64, 64), 64)

    def row_push(use, i):
        for j in (1, 3, 2):
            cp.start(
                ("zr", use, i, j), zrow.at[use, i, (t + j) % 4], zland.at[use, i, j - 1], to_z[j]
            )

    def row_finish(use, i, extra, with_bias, out_ref):
        for j in (1, 3, 2):
            cp.landed(("zr", use, i, j), zland.at[use, i, j - 1])
        here = shared(i, t)
        total = extra[here, :].astype(F32) + zrow[use, i, t].astype(F32)
        if with_bias is not None:
            total = total + vecs[with_bias, 2:3, :]
        for j in range(3):
            total = total + zland[use, i, j].astype(F32)
        out_ref[here, :] = total.astype(BF)
        for j in (1, 3, 2):
            cp.start(("za", use, i, j), out_ref.at[here], out_ref.at[here], to_z[j])

    def row_wait(use, i, out_ref):
        for j in (1, 3, 2):
            cp.landed(("za", use, i, j), out_ref.at[shared(i, (t + 4 - j) % 4)])

    def chosen(b):
        row = lax.broadcasted_iota(jnp.int32, (LOCAL, D), 0)
        return lax.broadcasted_iota(jnp.int32, (LOCAL, D), 1) == row + b * LOCAL

    def pack(ref, out):
        out[...] = dot_nt(chosen(t).astype(BF), ref[...]).astype(BF)

    def result_cols(l, use):
        for b in range(4):
            rows = slice(LOCAL * b, LOCAL * b + LOCAL)
            part = dot_nt(w[l, 1, rows, :], act[l])
            part = part + dot_nt(w[l, 2, rows, 2 * LOCAL :], mixp[l])
            zcol[use, b] = part.astype(BF)

    def half_of(i):
        return slice(256 * i, 256 * i + 256)

    def turn_cols(use, i):
        for b in range(4):
            zcol[use, b, :, half_of(i)] = dot_nt(
                chosen(b).astype(BF), full[half_of(i), :]
            ).astype(BF)

    def col_push(use, i):
        for j in (1, 3, 2):
            cp.start(
                ("zc", use, i, j),
                zcol.at[use, (t + j) % 4, :, half_of(i)],
                zland_c.at[use, j - 1, :, half_of(i)],
                to_z[j],
            )

    def col_finish(use, i, extra, with_bias, l, kind):
        lanes = half_of(i)
        for j in (1, 3, 2):
            cp.landed(("zc", use, i, j), zland_c.at[use, j - 1, :, lanes])
        total = extra[:, lanes].astype(F32) + zcol[use, t, :, lanes].astype(F32)
        if with_bias is not None:
            total = total + jnp.sum(
                jnp.where(chosen(t), vecs[with_bias, 2:3, :], 0.0), axis=1, keepdims=True
            )
        for j in range(3):
            total = total + zland_c[use, j, :, lanes].astype(F32)
        acts[l, kind, :, lanes] = total.astype(BF)
        act_push(l, kind, i)

    def act_copy(l, kind, i):
        ref = acts.at[l, kind, :, half_of(i)]
        return cp.make(("act", kind, i), ref, acts_in.at[kind, :, half_of(i)], to_s)

    def act_push(l, kind, i):
        @pl.when(s == 1 - l)
        def _():
            act_copy(l, kind, i).start()

    def back_heads(l, g_ref, half):
        at = slice(256 * half, 256 * half + 256)
        mixed = dot(g_ref[at, :], w[l, 2, :, 2 * LOCAL :])
        for h in range(3):
            gm[h, at, :] = mixed[:, LOCAL + HD * h : LOCAL + HD * h + HD].astype(BF)
        for n in range(3):
            lanes = slice(256 * n, 256 * n + 256)
            grad = dot(g_ref[at, :], w[l, 1, :, lanes]) * slope[l, at, lanes]
            gh[at, lanes] = grad.astype(BF)

    def back_attend(l, j):
        rows = slice(128 * j, 128 * j + 128)
        seen = slice(0, 128 * j + 128)
        for h in range(3):
            share = probs[l, h, :, stored[j]]
            grad = dot_nt(gm[h, rows, :], v[l, h, seen, :])
            dots = jnp.sum(share * grad, axis=-1, keepdims=True)
            grad = (share * (grad - dots)).astype(BF)
            lanes = slice(HD * h, HD * h + HD)
            key_lanes = slice(LOCAL + HD * h, LOCAL + HD * h + HD)
            dqk[rows, lanes] = dot(grad, k[l, h, seen, :]) * (1.0 / 8.0)
            by_key = dot_tn(grad, q[l, h, rows, :])
            by_value = dot_tn(share.astype(BF), gm[h, rows, :])
            if j == 3:
                dqk[seen, key_lanes] = by_key
                dv[seen, lanes] = by_value
            else:
                dqk[seen, key_lanes] += by_key
                dv[seen, lanes] += by_value

    def back_turn():
        def rows_of(i, _):
            at = pl.ds(pl.multiple_of(i * 128, 128), 128)
            gpre[at, 0 : 2 * LOCAL] = turn(dqk[at, :], at, -1).astype(BF)
            gpre[at, 2 * LOCAL :] = jnp.concatenate(
                [dv[at, :], jnp.zeros((128, LOCAL), F32)], axis=1
            ).astype(BF)
            return 0

        lax.fori_loop(0, 4, rows_of, 0)

    def back_norms(l, i, emit):
        rows = slice(256 * i, 256 * i + 256)
        one = dot_nt(gpre[rows, :], w[l, 2])
        two = dot_nt(gh[rows, :], w[l, 0])
        unit = normal[l, rows, :]
        sums = [col_sum(one * unit), col_sum(two * unit), col_sum(one), col_sum(two)]
        for n, value in enumerate(sums):
            row = slice(8 + 4 * l + n, 9 + 4 * l + n)
            vec[row, :] = value if i == 0 else vec[row, :] + value
        mixture = one * vecs[l, 3:4, :] + two * vecs[l, 4:5, :]
        first = jnp.mean(mixture, axis=-1, keepdims=True)
        second = jnp.mean(mixture * unit, axis=-1, keepdims=True)
        part = rstd[l, rows, 0:1] * (mixture - first - unit * second)
        emit(i, slice(0, D), part)

    def sums_of(l, g_ref):
        for n, ref in enumerate((gpre, gh, g_ref)):
            row = slice(4 * l + n, 4 * l + n + 1)
            vec[row, :] = col_sum(ref[...].astype(F32))
        vec[4 * l + 3 : 4 * l + 4, :] = jnp.zeros((1, D), F32)

    def weights_of(l, ch, g_ref):
        def rows_of(m, _):
            lanes = pl.ds(pl.multiple_of(m * 384, 128), 384)
            if ch == 0:
                value = dot_tn(nb[l, :, lanes], gh[...])
            elif ch == 1:
                value = dot_tn(g_ref[:, lanes], act[l])
            else:
                value = dot_tn(na[l, :, lanes], gpre[...])
                other = dot_tn(g_ref[:, lanes], mixp[l])
                value = jnp.concatenate(
                    [value[:, 0 : 2 * LOCAL], value[:, 2 * LOCAL :] + other], axis=1
                )
            grads[ch, pl.ds(4 * m, 4)] = value.astype(BF).reshape(4, 2, 48, D)
            return 0

        lax.fori_loop(0, 2, rows_of, 0)
        cp.start(("rc", l, ch), grads.at[ch, :, 1 - c], sib.at[l, ch], to_c)

    def weights_gone(l, ch):
        cp.sent_off(("rc", l, ch), grads.at[ch, :, 1 - c], sib.at[l, ch], to_c)

    def reduce_core(l, ch):
        cp.landed(("rc", l, ch), sib.at[l, ch])

        def add(i, _):
            sib[l, ch, i] = (sib[l, ch, i].astype(F32) + grads[ch, i, c].astype(F32)).astype(BF)
            return 0

        lax.fori_loop(0, 8, add, 0)
        if ch == 1:
            for j in (1, 3, 2, 0):
                yy = (y + j) % 4
                cp.start(("rx", l, ch, j), sib.at[l, ch, yy * 2 + 1 - x], xbuf.at[l, yy], to_x)
        else:
            for j in (1, 3, 2):
                yy = (y + j) % 4
                cp.start(
                    ("ry", l, ch, j),
                    sib.at[l, ch, pl.ds(yy * 2, 2)],
                    ybuf.at[l, pl.ds(3 * ch + 2 * (j - 1), 2)],
                    to_y[j],
                )

    def reduce_mid(l, ch):
        if ch == 1:
            for j in (1, 3, 2, 0):
                yy = (y + j) % 4
                cp.landed(("rx", l, ch, j), xbuf.at[l, yy])
                mine = yy * 2 + x
                xbuf[l, yy] = (sib[l, ch, mine].astype(F32) + xbuf[l, yy].astype(F32)).astype(BF)
                if j:
                    cp.start(("ry", l, ch, j), xbuf.at[l, yy], ybuf.at[l, 11 + j], to_y[j])
        else:
            for j in (1, 3, 2):
                cp.landed(("ry", l, ch, j), ybuf.at[l, pl.ds(3 * ch + 2 * (j - 1), 2)])
            for i in range(2):
                total = sib[l, ch, y * 2 + i].astype(F32)
                for j in range(3):
                    total = total + ybuf[l, 3 * ch + 2 * j + i].astype(F32)
                keep[l, ch // 2, i] = total.astype(BF)
            cp.start(("rx", l, ch, 0), keep.at[l, ch // 2, 1 - x], keep.at[l, ch // 2, 2], to_x)

    def reduce_end(l, ch):
        if ch == 1:
            total = xbuf[l, y].astype(F32)
            for j in (1, 3, 2):
                cp.landed(("ry", l, ch, j), ybuf.at[l, 11 + j])
            for j in (1, 2, 3):
                total = total + ybuf[l, 11 + j].astype(F32)
        else:
            cp.landed(("rx", l, ch, 0), keep.at[l, ch // 2, 2])
            total = keep[l, ch // 2, x].astype(F32) + keep[l, ch // 2, 2].astype(F32)
        sbuf[l, ch] = total.astype(BF)

        @pl.when(s == 1 - l)
        def _():
            cp.make(("rs", ch), sbuf.at[l, ch], sbuf_in.at[ch], to_s).start()

    def vec_z():
        vland[t, 0:8] = vec[8:16, :]
        for j in (1, 2, 3):
            cp.start(("vz", j), vec.at[pl.ds(8, 8)], vland.at[t, pl.ds(0, 8)], to_z[j])

    def vec_c():
        for j in (1, 2, 3):
            cp.landed(("vz", j), vland.at[(t + 4 - j) % 4, pl.ds(0, 8)])
        stage[0, 0:8] = vec[0:8, :]
        stage[0, 8:16] = vland[0, 0:8] + vland[1, 0:8] + vland[2, 0:8] + vland[3, 0:8]
        cp.start("vc", stage.at[0], vland.at[4], to_c)

    def vec_x():
        cp.landed("vc", vland.at[4])
        stage[1] = stage[0] + vland[4]
        cp.start("vx", stage.at[1], vland.at[5], to_x)

    def vec_s():
        cp.landed("vx", vland.at[5])
        stage[2] = stage[1] + vland[5]
        cp.start("vs", stage.at[2], vland.at[6], to_s)

    def vec_y():
        cp.landed("vs", vland.at[6])
        stage[3] = stage[2] + vland[6]
        vland[7 + y] = stage[3]
        for j in (1, 2, 3):
            cp.start(("vy", j), stage.at[3], vland.at[7 + y], to_y[j])

    @pl.when(s == 1)
    def _():
        swapped()

    gather_first(0, 2)
    prepare()
    gather_second(0, 2)
    gather_first(0, 0)
    gather_first(0, 1)
    fetch_x.wait()
    norms(0, x0, 0)
    gather_second(0, 0)
    norms(0, x0, 1)
    gather_third(0, 2)
    gather_second(0, 1)

    @pl.when(s == 0)
    def _():
        swapped()

    gather_fourth(0, 2)
    project(0, 0)
    project(0, 1)
    attend(0, 0)
    attend(0, 1)
    gather_third(0, 0)
    gather_third(0, 1)
    gather_first(1, 2)
    gather_first(1, 0)
    gather_first(1, 1)
    attend(0, 2)
    attend(0, 3)
    gather_fourth(0, 0)
    feed(0, 0)
    gather_fourth(0, 1)
    result_rows(0, 0, emit_row(0))
    row_push(0, 0)
    gather_second(1, 2)
    gather_second(1, 0)
    feed(0, 1)
    result_rows(0, 1, emit_row(0))
    row_push(0, 1)
    gather_second(1, 1)
    row_finish(0, 0, x0, 0, x1)
    gather_third(1, 2)
    gather_third(1, 0)
    row_finish(0, 1, x0, 0, x1)
    gather_third(1, 1)
    gather_fourth(1, 2)
    row_wait(0, 0, x1)

    norms(1, x1, 0)
    project(1, 0)
    attend(1, 0)
    attend(1, 1)
    row_wait(0, 1, x1)
    norms(1, x1, 1)
    project(1, 1)
    attend(1, 2)
    attend(1, 3)
    gather_fourth(1, 0)
    feed(1, 0)
    feed(1, 1)
    gather_fourth(1, 1)
    result_cols(1, 0)
    col_push(0, 0)
    col_push(0, 1)
    pack(x1, acts.at[0, 0])
    act_push(0, 0, 0)
    act_push(0, 0, 1)

    fetch_g.wait()
    back_heads(1, g1, 0)
    back_heads(1, g1, 1)
    for j in (3, 2, 1, 0):
        back_attend(1, j)
    back_turn()
    back_norms(1, 0, emit_row(1))
    row_push(1, 0)
    back_norms(1, 1, emit_row(1))
    row_push(1, 1)
    weights_of(1, 1, g1)
    weights_of(1, 0, g1)
    row_finish(1, 0, g1, None, g0)
    weights_of(1, 2, g1)
    reduce_core(1, 1)
    row_finish(1, 1, g1, None, g0)
    reduce_core(1, 0)
    sums_of(1, g1)
    reduce_core(1, 2)
    for i in range(2):
        col_finish(0, i, acts.at[0, 0], 1, 1, 0)
    for ch in range(3):
        weights_gone(1, ch)

    row_wait(1, 0, g0)
    back_heads(0, g0, 0)
    row_wait(1, 1, g0)
    back_heads(0, g0, 1)
    weights_of(0, 1, g0)
    weights_of(0, 0, g0)
    reduce_mid(1, 1)
    reduce_mid(1, 0)
    back_attend(0, 3)
    reduce_mid(1, 2)
    reduce_core(0, 1)
    reduce_core(0, 0)
    back_attend(0, 2)
    reduce_end(1, 1)
    reduce_end(1, 0)
    reduce_end(1, 2)
    back_attend(0, 1)
    back_attend(0, 0)
    back_turn()
    back_norms(0, 0, emit_full)
    turn_cols(1, 0)
    col_push(1, 0)
    back_norms(0, 1, emit_full)
    turn_cols(1, 1)
    col_push(1, 1)
    pack(g0, acts.at[1, 1])
    act_push(1, 1, 0)
    act_push(1, 1, 1)
    weights_of(0, 2, g0)
    sums_of(0, g0)
    vec_z()
    reduce_mid(0, 1)
    reduce_core(0, 2)
    vec_c()
    reduce_mid(0, 0)
    vec_x()
    col_finish(1, 0, acts.at[1, 1], None, 0, 1)
    vec_s()
    reduce_end(0, 1)
    reduce_end(0, 0)
    reduce_mid(0, 2)
    col_finish(1, 1, acts.at[1, 1], None, 0, 1)
    vec_y()
    reduce_end(0, 2)

    acts_out[0, s] = acts[s, 0]
    acts_out[1, s] = acts[s, 1]
    for kind in range(2):
        for i in range(2):
            cp.landed(("act", kind, i), acts_in.at[kind, :, half_of(i)])
        acts_out[kind, 1 - s] = acts_in[kind]
    for j in (1, 2, 3):
        cp.landed(("vy", j), vland.at[7 + (y + 4 - j) % 4])
    stage[4] = vland[7] + vland[8] + vland[9] + vland[10]
    vec_out[0:4] = jnp.where(s == 0, stage[4, 0:4], stage[4, 4:8])
    vec_out[4:8] = jnp.where(s == 0, stage[4, 8:12], stage[4, 12:16])
    for ch in (1, 0, 2):
        cp.landed(("rs", ch), sbuf_in.at[ch])
        w_out[ch] = sbuf[s, ch].astype(F32) + sbuf_in[ch].astype(F32)
        name = ("rs", ch)
        cp.late(name, cp.make(name, sbuf.at[1 - s, ch], sbuf_in.at[ch], to_s))
    for kind in range(2):
        for i in range(2):
            cp.late(("act", kind, i), act_copy(1 - s, kind, i))
    cp.finish()


def mega(*arguments):
    dma = pltpu.SemaphoreType.DMA
    vmem = pl.BlockSpec(memory_space=pltpu.VMEM)
    smem = pl.BlockSpec(memory_space=pltpu.SMEM)
    anywhere = pl.BlockSpec(memory_space=pl.ANY)

    def bf(*shape):
        return pltpu.VMEM(shape, BF)

    def f32(*shape):
        return pltpu.VMEM(shape, F32)

    return pl.pallas_call(
        mega_kernel,
        out_shape=[
            jax.ShapeDtypeStruct((2, 2, LOCAL, SLOT), BF),
            jax.ShapeDtypeStruct((3, 48, D), F32),
            jax.ShapeDtypeStruct((8, D), F32),
        ],
        in_specs=[smem, vmem, anywhere, anywhere] + [vmem] * 9,
        out_specs=[vmem] * 3,
        scratch_shapes=[
            bf(2, 3, D, D),
            f32(2, 8, D),
            bf(SLOT, D),
            bf(SLOT, D),
            bf(SLOT, D),
            bf(SLOT, D),
            f32(3, SLOT, 128),
            f32(SLOT, SLOT),
            f32(2, SLOT, D),
            f32(2, SLOT, 128),
            bf(2, SLOT, D),
            bf(2, SLOT, D),
            bf(2, 3, SLOT, HD),
            bf(2, 3, SLOT, HD),
            bf(2, 3, SLOT, HD),
            f32(2, 3, 128, 1280),
            bf(2, SLOT, 2 * LOCAL),
            bf(2, SLOT, D),
            f32(2, SLOT, D),
            bf(3, SLOT, HD),
            bf(SLOT, D),
            f32(SLOT, 2 * LOCAL),
            f32(SLOT, LOCAL),
            bf(SLOT, D),
            bf(SLOT, D),
            bf(2, 2, 4, 64, D),
            bf(2, 4, LOCAL, SLOT),
            bf(2, 2, 3, 64, D),
            bf(2, 3, LOCAL, SLOT),
            bf(2, 2, LOCAL, SLOT),
            bf(2, LOCAL, SLOT),
            bf(3, 8, 2, 48, D),
            bf(2, 3, 8, 48, D),
            bf(2, 4, 48, D),
            bf(2, 15, 48, D),
            bf(2, 2, 3, 48, D),
            bf(2, 3, 48, D),
            bf(3, 48, D),
            f32(16, D),
            f32(11, 16, D),
            f32(5, 16, D),
            dma((SEMS,)),
            dma((SEMS,)),
            dma((2,)),
        ],
        compiler_params=pltpu.CompilerParams(
            collective_id=0, has_side_effects=True, vmem_limit_bytes=VMEM_LIMIT
        ),
        name="two_layers",
    )(*arguments)


def hand_out_kernel(acts, sums, vec, sec, grad, wqkv, bqkv, wattn, win, bin_, wout, bout, gains, shifts):
    sec[...] = acts[0]
    grad[...] = acts[1]
    for n in range(3):
        lanes = slice(LOCAL * n, LOCAL * n + LOCAL)
        wqkv[n] = sums[2, :, lanes]
        bqkv[n] = vec[0:1, lanes]
    wattn[...] = sums[2, :, 3 * LOCAL :]
    win[...] = sums[0]
    wout[...] = sums[1]
    bin_[...] = vec[1:2, :]
    bout[...] = vec[2:3, :]
    gains[...] = vec[4:6, :]
    shifts[...] = vec[6:8, :]


def hand_out(acts, sums, vec):
    vmem = pl.BlockSpec(memory_space=pltpu.VMEM)
    shapes = [(3, 48, LOCAL), (3, 1, LOCAL), (48, LOCAL), (48, D), (1, D), (48, D), (1, D)]
    return pl.pallas_call(
        hand_out_kernel,
        out_shape=[jax.ShapeDtypeStruct((2, LOCAL, SLOT), BF)] * 2
        + [jax.ShapeDtypeStruct(shape, F32) for shape in shapes + [(2, D), (2, D)]],
        in_specs=[vmem] * 3,
        out_specs=[vmem] * 11,
        name="hand_out",
    )(acts, sums, vec)


def body(
    inputs,
    cotangent,
    seq_lengths,
    w_qkv,
    b_qkv,
    w_attn_out,
    w_in,
    b_in,
    w_out,
    b_out,
    norm_gains,
    norm_biases,
):
    powers = 1.0 / 10000.0 ** (np.arange(ROT // 2, dtype=np.float32) * 2.0 / ROT)
    freq = jnp.asarray(np.tile(powers.astype(np.float32), 128 // (ROT // 2))[None])
    acts, sums, vec = mega(
        seq_lengths[:, 0],
        freq,
        inputs,
        cotangent,
        w_qkv[0].transpose(1, 0, 2),
        w_attn_out[0].T,
        w_in[0],
        w_out[0].T,
        b_qkv.transpose(1, 0, 2),
        b_in,
        b_out,
        norm_gains[0],
        norm_biases[0],
    )
    sec, grad, wqkv, bqkv, wattn, win, bin_, wout, bout, gains, shifts = hand_out(acts, sums, vec)
    return (
        sec.transpose(0, 2, 1)[None],
        grad.transpose(0, 2, 1)[None],
        wqkv.transpose(1, 0, 2)[None],
        bqkv.transpose(1, 0, 2),
        wattn.T[None],
        win[None],
        bin_,
        wout.T[None],
        bout,
        gains[None],
        shifts[None],
    )


def solution(mesh):
    return jax.shard_map(
        body,
        mesh=mesh,
        in_specs=(
            P(None, "dp", None),
            P(None, "dp", None),
            P(None, "dp", None),
            P("section", "dp", None, "tensor"),
            P("section", None, "tensor"),
            P("section", "tensor", "dp"),
            P("section", "dp", "tensor"),
            P("section", "tensor"),
            P("section", "tensor", "dp"),
            P("section", None),
            P("section", None, None),
            P("section", None, None),
        ),
        out_specs=(
            P("section", None, "dp", "tensor"),
            P("section", None, "dp", "tensor"),
            P("section", "dp", None, "tensor"),
            P("section", None, "tensor"),
            P("section", "tensor", "dp"),
            P("section", "dp", "tensor"),
            P("section", "tensor"),
            P("section", "tensor", "dp"),
            P("section", None),
            P("section", None, None),
            P("section", None, None),
        ),
        check_vma=False,
    )
```

time: 174 us -> 144 us (0.83); the launches traced: 171 us -> 144 us
  local copies, waits for them, and re-layouts: 15.2 us -> 0 us
  Pallas kernels: 155 us -> 143 us
    pallas_call x1 -> x2, Pallas kernels: 155 us -> 143 us  [the longest x1 140 us: mega(): pl.pallas_call(mega_kernel, out_shape=[jax.ShapeDtypeStruct((2, 2, LOCAL,...]
    unnamed x10 -> x0, local copies, waits for them, and re-layouts: 8.8 us -> none
    slice x3 -> x0, local copies, waits for them, and re-layouts: 2.15 us -> none  [the longest x1 1.4 us: body(): va[2][None]]
    broadcast_in_dim x3 -> x0, local copies, waits for them, and re-layouts: 2.03 us -> none  [the longest x1 0.73 us: body(): w_sums[1].T[None]]
where the time goes in v3:
time: 144 us
  Pallas kernels  143 us (99%)
    pallas_call x1, Pallas kernels, mega(): pl.pallas_call(mega_kernel, out_shape=[jax.ShapeDtypeStruct((2, 2, LOCAL,...  140 us

profile of v3, /device:TPU:0, one launch (start us, length us, event | category | flops | bytes accessed | tf_op | source)
XLA Modules:
  0.0 143.7 jit_solution(5764900616929032531)
XLA Ops:
  0.6 140.5 %two_layers.1 = (bf16[2,2,192,512]{3,2,1,0:T(8,128)(2,1)}, f32[3,48,768]{2,1,0:T(8,128)}, f32[8,768]{1,0:T(8,128)}) custom-call(s32[2,4]{1,0:T(2,128)} %bitcast.40, f32[1,128]{1,0:T(1,128)} %constant.2.clone.freq_ref, bf16[2,512,768]{2,1,0:T(8,128)(2,1)} %inputs_ref.1, bf16[2,512,768]{2,1,0:T(8,128)(2,1)} %cot_ref.1, bf16[3,48,192]{2,1,0:T(8,128)(2,1)} %bitcast.33, ...), custom_call_target="tpu_custom_call" | custom-call | tf_op jit(solution)/shard_map/two_layers/pallas_call | solution.py:812
  141.2 2.4 %hand_out.1 = (bf16[2,192,512]{2,1,0:T(8,128)(2,1)}, bf16[2,192,512]{2,1,0:T(8,128)(2,1)}, f32[3,48,192]{2,1,0:T(8,128)}, f32[3,1,192]{2,1,0:T(1,128)}, f32[48,1...) custom-call(bf16[2,2,192,512]{3,2,1,0:T(8,128)(2,1)} %get-tuple-elem, ...), custom_call_target="tpu_custom_call" | custom-call | tf_op jit(solution)/shard_map/hand_out/pallas_call | solution.py:893

commit v4 on v3

--- a/solution.py
+++ b/solution.py
@@ -117,7 +117,9 @@
                 copy.wait_send()
 
 
-SEMS = 240
+SEMS = 288
+GATHER = ((2, slice(0, 384), True), (2, slice(384, D), True), (0, slice(0, D), True), (1, slice(0, D), False))
+REDUCE = ((1, slice(0, D), True), (0, slice(0, D), False), (2, slice(0, 384), False), (2, slice(384, D), True))
 
 
 def mega_kernel(
@@ -215,63 +217,97 @@
 
     signal_all(list(to_y.values()) + list(to_z.values()) + [to_x, to_c, to_s])
 
-    cp.start("swap_w", w.at[s, :, rows48(me)], w.at[s, :, rows48(me)], to_s)
-    cp.start("swap_v", vecs.at[s], vecs.at[s], to_s)
-
-    def swapped():
-        cp.landed("swap_w", w.at[1 - s, :, rows48(me)])
-        cp.landed("swap_v", vecs.at[1 - s])
+    def swap(l):
+        names = [("swap", ch) for ch in (2, 0, 1)]
+        refs = [w.at[l, ch, rows48(me)] for ch in (2, 0, 1)]
+        return [
+            (name, cp.make(name, ref, ref, to_s))
+            for name, ref in zip(["swap"] + names, [vecs.at[l]] + refs)
+        ]
+
+    def swap_start(l):
+        @pl.when(s == l)
+        def _():
+            for _, copy in swap(l):
+                copy.start()
+
+    def swap_wait(l, which):
+        @pl.when(s == 1 - l)
+        def _():
+            if which is None:
+                cp.landed("swap", vecs.at[l])
+            else:
+                cp.landed(("swap", which), w.at[l, which, rows48(me)])
 
     def block_of(j, other, core=c):
         return dp_of((y + 4 - j) % 4, (1 - x) if other else x, core)
 
-    def push(l, ch, slot, block, to):
-        ref = w.at[l, ch, rows48(block)]
-        cp.start(("w", l, ch, slot), ref, ref, to)
-
-    def arrived(l, ch, slot, block):
-        cp.landed(("w", l, ch, slot), w.at[l, ch, rows48(block)])
-
-    def gather_first(l, ch):
-        if ch == 1:
-            for j in (1, 3, 2):
-                push(l, ch, j - 1, me, to_y[j])
-            push(l, ch, 3, me, to_x)
+    turnwise = 1 + 2 * c
+    to_relay = {"dp": dp_of((y + turnwise) % 4, x, c)}
+
+    def part_ref(l, p, block):
+        ch, lanes, _ = GATHER[p]
+        return w.at[l, ch, rows48(block), lanes]
+
+    def push(l, p, slot, block, to):
+        ref = part_ref(l, p, block)
+        cp.start(("w", l, p, slot), ref, ref, to)
+
+    def arrived(l, p, slot, block):
+        cp.landed(("w", l, p, slot), part_ref(l, p, block))
+
+    def gather_first(l, p):
+        if GATHER[p][2]:
+            push(l, p, 0, me, to_x)
+            for j in (1, 3):
+                push(l, p, j, me, to_y[j])
         else:
-            push(l, ch, 0, me, to_x)
-            for j in (1, 3, 2):
-                push(l, ch, j, me, to_y[j])
-        push(l, ch, 7, me, to_c)
-
-    def gather_second(l, ch):
-        if ch == 1:
-            for j in (1, 3, 2):
-                arrived(l, ch, j - 1, block_of(j, False))
-                push(l, ch, 3 + j, block_of(j, False), to_x)
-                push(l, ch, 7 + 2 * j, block_of(j, False), to_c)
+            for j in (1, 3):
+                push(l, p, j - 1, me, to_y[j])
+            push(l, p, 3, me, to_x)
+        push(l, p, 7, me, to_c)
+
+    def gather_second(l, p):
+        if GATHER[p][2]:
+            arrived(l, p, 0, block_of(0, True))
+            for j in (1, 3):
+                push(l, p, 3 + j, block_of(0, True), to_y[j])
+            push(l, p, 8, block_of(0, True), to_c)
         else:
-            arrived(l, ch, 0, block_of(0, True))
-            for j in (1, 3, 2):
-                push(l, ch, 3 + j, block_of(0, True), to_y[j])
-            push(l, ch, 8, block_of(0, True), to_c)
-
-    def gather_third(l, ch):
-        if ch == 1:
-            for j in (0, 1, 3, 2):
-                arrived(l, ch, 3 + j, block_of(j, True))
-                push(l, ch, 8 + 2 * j, block_of(j, True), to_c)
+            for j in (1, 3):
+                arrived(l, p, j - 1, block_of(j, False))
+            push(l, p, 1, block_of(turnwise, False), to_relay)
+            for j in (1, 3):
+                push(l, p, 3 + j, block_of(j, False), to_x)
+                push(l, p, 7 + 2 * j, block_of(j, False), to_c)
+
+    def gather_third(l, p):
+        if GATHER[p][2]:
+            for slot, other in ((0, False), (3, True)):
+                for j in (1, 3):
+                    arrived(l, p, slot + j, block_of(j, other))
+                push(l, p, slot + 2, block_of(turnwise, other), to_relay)
+                for j in (1, 3):
+                    push(l, p, 7 + 2 * j + other, block_of(j, other), to_c)
         else:
-            for j in (1, 3, 2):
-                arrived(l, ch, j, block_of(j, False))
-                push(l, ch, 7 + 2 * j, block_of(j, False), to_c)
-            for j in (1, 3, 2):
-                arrived(l, ch, 3 + j, block_of(j, True))
-                push(l, ch, 8 + 2 * j, block_of(j, True), to_c)
-
-    def gather_fourth(l, ch):
+            arrived(l, p, 1, block_of(2, False))
+            push(l, p, 5, block_of(2, False), to_x)
+            push(l, p, 11, block_of(2, False), to_c)
+            for j in (0, 1, 3):
+                arrived(l, p, 3 + j, block_of(j, True))
+                push(l, p, 8 + 2 * j, block_of(j, True), to_c)
+
+    def gather_fourth(l, p):
+        if GATHER[p][2]:
+            arrived(l, p, 2, block_of(2, False))
+            push(l, p, 11, block_of(2, False), to_c)
+        arrived(l, p, 5, block_of(2, True))
+        push(l, p, 12, block_of(2, True), to_c)
+
+    def gather_last(l, p):
         for j in range(4):
-            arrived(l, ch, 7 + 2 * j, block_of(j, False, 1 - c))
-            arrived(l, ch, 8 + 2 * j, block_of(j, True, 1 - c))
+            arrived(l, p, 7 + 2 * j, block_of(j, False, 1 - c))
+            arrived(l, p, 8 + 2 * j, block_of(j, True, 1 - c))
 
     def prepare():
         lens = [len_ref[s, j] for j in range(SEQS)]
@@ -319,9 +355,9 @@
             parts.append(base + change if sign > 0 else base - change)
         return jnp.concatenate(parts, axis=1)
 
-    def norms(l, x_ref, half):
+    def norms(l, x_ref, j):
         def rows_of(i, _):
-            at = pl.ds(pl.multiple_of(256 * half + i * 64, 64), 64)
+            at = pl.ds(pl.multiple_of(128 * j + i * 64, 64), 64)
             values = x_ref[at, :].astype(F32)
             centred = values - jnp.mean(values, axis=-1, keepdims=True)
             scale = lax.rsqrt(jnp.mean(centred * centred, axis=-1, keepdims=True) + EPSILON)
@@ -332,33 +368,35 @@
             nb[l, at, :] = (unit * vecs[l, 4:5, :] + vecs[l, 6:7, :]).astype(BF)
             return 0
 
-        lax.fori_loop(0, 4, rows_of, 0)
+        lax.fori_loop(0, 2, rows_of, 0)
 
     stored = [slice(64 * j * (j + 1), 64 * (j + 1) * (j + 2)) for j in range(4)]
 
-    def project(l, half):
-        at = slice(256 * half, 256 * half + 256)
+    def project(l, first, size):
+        at = slice(first, first + size)
         pre = dot(na[l, at, :], w[l, 2, :, 0 : 3 * LOCAL]) + vecs[l, 0:1, 0 : 3 * LOCAL]
         turned = turn(pre[:, 0 : 2 * LOCAL], at, 1)
         for h in range(3):
             q[l, h, at, :] = (turned[:, HD * h : HD * h + HD] * (1.0 / 8.0)).astype(BF)
             k[l, h, at, :] = turned[:, LOCAL + HD * h : LOCAL + HD * h + HD].astype(BF)
             v[l, h, at, :] = pre[:, 2 * LOCAL + HD * h : 2 * LOCAL + HD * h + HD].astype(BF)
-        mixp[l, at, 0:LOCAL] = jnp.zeros((256, LOCAL), BF)
+        mixp[l, at, 0:LOCAL] = jnp.zeros((size, LOCAL), BF)
 
     def attend(l, j):
         rows = slice(128 * j, 128 * j + 128)
         seen = slice(0, 128 * j + 128)
+        scores = [
+            dot_nt(q[l, h, rows, :], k[l, h, seen, :]) + bias[rows, seen] for h in range(3)
+        ]
+        weights = [jnp.exp(one - jnp.max(one, axis=-1, keepdims=True)) for one in scores]
+        shares = [one * (1.0 / jnp.sum(one, axis=-1, keepdims=True)) for one in weights]
         for h in range(3):
-            scores = dot_nt(q[l, h, rows, :], k[l, h, seen, :]) + bias[rows, seen]
-            weights = jnp.exp(scores - jnp.max(scores, axis=-1, keepdims=True))
-            share = weights * (1.0 / jnp.sum(weights, axis=-1, keepdims=True))
-            probs[l, h, :, stored[j]] = share
-            out = dot(share.astype(BF), v[l, h, seen, :])
-            mixp[l, rows, LOCAL + HD * h : LOCAL + HD * h + HD] = out.astype(BF)
-
-    def feed(l, half):
-        at = slice(256 * half, 256 * half + 256)
+            probs[l, h, :, stored[j]] = shares[h]
+        outs = [dot(shares[h].astype(BF), v[l, h, seen, :]) for h in range(3)]
+        mixp[l, rows, LOCAL:] = jnp.concatenate(outs, axis=1).astype(BF)
+
+    def feed(l, i):
+        at = slice(256 * i, 256 * i + 256)
         for n in range(3):
             lanes = slice(256 * n, 256 * n + 256)
             hidden = dot(nb[l, at, :], w[l, 0, :, lanes]) + vecs[l, 1:2, lanes]
@@ -376,8 +414,8 @@
 
     def emit_row(use):
         def emit(i, lanes, part):
-            for b in range(4):
-                zrow[use, i, b, :, lanes] = part[64 * b : 64 * b + 64].astype(BF)
+            for b in range(8):
+                zrow[use, 2 * i + b // 4, b % 4, :, lanes] = part[32 * b : 32 * b + 32].astype(BF)
 
         return emit
 
@@ -385,7 +423,7 @@
         full[256 * i : 256 * i + 256, lanes] = part.astype(BF)
 
     def shared(i, b):
-        return pl.ds(pl.multiple_of(256 * i + b * 64, 64), 64)
+        return pl.ds(pl.multiple_of(128 * i + b * 32, 32), 32)
 
     def row_push(use, i):
         for j in (1, 3, 2):
@@ -424,26 +462,25 @@
             part = part + dot_nt(w[l, 2, rows, 2 * LOCAL :], mixp[l])
             zcol[use, b] = part.astype(BF)
 
-    def half_of(i):
-        return slice(256 * i, 256 * i + 256)
+    def part_of(i):
+        return slice(128 * i, 128 * i + 128)
 
     def turn_cols(use, i):
+        rows = slice(256 * i, 256 * i + 256)
         for b in range(4):
-            zcol[use, b, :, half_of(i)] = dot_nt(
-                chosen(b).astype(BF), full[half_of(i), :]
-            ).astype(BF)
+            zcol[use, b, :, rows] = dot_nt(chosen(b).astype(BF), full[rows, :]).astype(BF)
 
     def col_push(use, i):
         for j in (1, 3, 2):
             cp.start(
                 ("zc", use, i, j),
-                zcol.at[use, (t + j) % 4, :, half_of(i)],
-                zland_c.at[use, j - 1, :, half_of(i)],
+                zcol.at[use, (t + j) % 4, :, part_of(i)],
+                zland_c.at[use, j - 1, :, part_of(i)],
                 to_z[j],
             )
 
     def col_finish(use, i, extra, with_bias, l, kind):
-        lanes = half_of(i)
+        lanes = part_of(i)
         for j in (1, 3, 2):
             cp.landed(("zc", use, i, j), zland_c.at[use, j - 1, :, lanes])
         total = extra[:, lanes].astype(F32) + zcol[use, t, :, lanes].astype(F32)
@@ -457,16 +494,16 @@
         act_push(l, kind, i)
 
     def act_copy(l, kind, i):
-        ref = acts.at[l, kind, :, half_of(i)]
-        return cp.make(("act", kind, i), ref, acts_in.at[kind, :, half_of(i)], to_s)
+        ref = acts.at[l, kind, :, part_of(i)]
+        return cp.make(("act", kind, i), ref, acts_in.at[kind, :, part_of(i)], to_s)
 
     def act_push(l, kind, i):
         @pl.when(s == 1 - l)
         def _():
             act_copy(l, kind, i).start()
 
-    def back_heads(l, g_ref, half):
-        at = slice(256 * half, 256 * half + 256)
+    def back_heads(l, g_ref, i):
+        at = slice(256 * i, 256 * i + 256)
         mixed = dot(g_ref[at, :], w[l, 2, :, 2 * LOCAL :])
         for h in range(3):
             gm[h, at, :] = mixed[:, LOCAL + HD * h : LOCAL + HD * h + HD].astype(BF)
@@ -478,33 +515,29 @@
     def back_attend(l, j):
         rows = slice(128 * j, 128 * j + 128)
         seen = slice(0, 128 * j + 128)
-        for h in range(3):
-            share = probs[l, h, :, stored[j]]
-            grad = dot_nt(gm[h, rows, :], v[l, h, seen, :])
-            dots = jnp.sum(share * grad, axis=-1, keepdims=True)
-            grad = (share * (grad - dots)).astype(BF)
-            lanes = slice(HD * h, HD * h + HD)
-            key_lanes = slice(LOCAL + HD * h, LOCAL + HD * h + HD)
-            dqk[rows, lanes] = dot(grad, k[l, h, seen, :]) * (1.0 / 8.0)
-            by_key = dot_tn(grad, q[l, h, rows, :])
-            by_value = dot_tn(share.astype(BF), gm[h, rows, :])
-            if j == 3:
-                dqk[seen, key_lanes] = by_key
-                dv[seen, lanes] = by_value
-            else:
-                dqk[seen, key_lanes] += by_key
-                dv[seen, lanes] += by_value
-
-    def back_turn():
-        def rows_of(i, _):
-            at = pl.ds(pl.multiple_of(i * 128, 128), 128)
-            gpre[at, 0 : 2 * LOCAL] = turn(dqk[at, :], at, -1).astype(BF)
-            gpre[at, 2 * LOCAL :] = jnp.concatenate(
-                [dv[at, :], jnp.zeros((128, LOCAL), F32)], axis=1
-            ).astype(BF)
-            return 0
-
-        lax.fori_loop(0, 4, rows_of, 0)
+        shares = [probs[l, h, :, stored[j]] for h in range(3)]
+        grads_of = [dot_nt(gm[h, rows, :], v[l, h, seen, :]) for h in range(3)]
+        dots = [jnp.sum(shares[h] * grads_of[h], axis=-1, keepdims=True) for h in range(3)]
+        grads_of = [(shares[h] * (grads_of[h] - dots[h])).astype(BF) for h in range(3)]
+        by_query = [dot(grads_of[h], k[l, h, seen, :]) for h in range(3)]
+        dqk[rows, 0:LOCAL] = jnp.concatenate(by_query, axis=1) * (1.0 / 8.0)
+        by_key = [dot_tn(grads_of[h], q[l, h, rows, :]) for h in range(3)]
+        by_value = [dot_tn(shares[h].astype(BF), gm[h, rows, :]) for h in range(3)]
+        by_key = jnp.concatenate(by_key, axis=1)
+        by_value = jnp.concatenate(by_value, axis=1)
+        if j == 3:
+            dqk[seen, LOCAL:] = by_key
+            dv[seen, :] = by_value
+        else:
+            dqk[seen, LOCAL:] += by_key
+            dv[seen, :] += by_value
+
+    def back_turn(j):
+        at = slice(128 * j, 128 * j + 128)
+        gpre[at, 0 : 2 * LOCAL] = turn(dqk[at, :], at, -1).astype(BF)
+        gpre[at, 2 * LOCAL :] = jnp.concatenate(
+            [dv[at, :], jnp.zeros((128, LOCAL), F32)], axis=1
+        ).astype(BF)
 
     def back_norms(l, i, emit):
         rows = slice(256 * i, 256 * i + 256)
@@ -514,7 +547,7 @@
         sums = [col_sum(one * unit), col_sum(two * unit), col_sum(one), col_sum(two)]
         for n, value in enumerate(sums):
             row = slice(8 + 4 * l + n, 9 + 4 * l + n)
-            vec[row, :] = value if i == 0 else vec[row, :] + value
+            vec[row, :] = value if i == 1 else vec[row, :] + value
         mixture = one * vecs[l, 3:4, :] + two * vecs[l, 4:5, :]
         first = jnp.mean(mixture, axis=-1, keepdims=True)
         second = jnp.mean(mixture * unit, axis=-1, keepdims=True)
@@ -557,54 +590,86 @@
             return 0
 
         lax.fori_loop(0, 8, add, 0)
-        if ch == 1:
+        for p in range(4):
+            if REDUCE[p][0] == ch:
+                reduce_start(l, p)
+
+    def reduce_start(l, p):
+        ch, lanes, x_first = REDUCE[p]
+        if x_first:
             for j in (1, 3, 2, 0):
                 yy = (y + j) % 4
-                cp.start(("rx", l, ch, j), sib.at[l, ch, yy * 2 + 1 - x], xbuf.at[l, yy], to_x)
+                cp.start(
+                    ("rx", l, p, j),
+                    sib.at[l, ch, yy * 2 + 1 - x, :, lanes],
+                    xbuf.at[l, ch - 1, yy, :, lanes],
+                    to_x,
+                )
         else:
             for j in (1, 3, 2):
                 yy = (y + j) % 4
                 cp.start(
-                    ("ry", l, ch, j),
-                    sib.at[l, ch, pl.ds(yy * 2, 2)],
-                    ybuf.at[l, pl.ds(3 * ch + 2 * (j - 1), 2)],
+                    ("ry", l, p, j),
+                    sib.at[l, ch, pl.ds(yy * 2, 2), :, lanes],
+                    ybuf.at[l, pl.ds(3 * ch + 2 * (j - 1), 2), :, lanes],
                     to_y[j],
                 )
 
-    def reduce_mid(l, ch):
-        if ch == 1:
+    def slot_of(p, j):
+        return 11 + j if REDUCE[p][0] == 1 else 5 + j
+
+    def reduce_mid(l, p):
+        ch, lanes, x_first = REDUCE[p]
+        if x_first:
             for j in (1, 3, 2, 0):
                 yy = (y + j) % 4
-                cp.landed(("rx", l, ch, j), xbuf.at[l, yy])
-                mine = yy * 2 + x
-                xbuf[l, yy] = (sib[l, ch, mine].astype(F32) + xbuf[l, yy].astype(F32)).astype(BF)
+                ref = xbuf.at[l, ch - 1, yy, :, lanes]
+                cp.landed(("rx", l, p, j), ref)
+                mine = sib[l, ch, yy * 2 + x, :, lanes].astype(F32)
+                xbuf[l, ch - 1, yy, :, lanes] = (
+                    mine + xbuf[l, ch - 1, yy, :, lanes].astype(F32)
+                ).astype(BF)
                 if j:
-                    cp.start(("ry", l, ch, j), xbuf.at[l, yy], ybuf.at[l, 11 + j], to_y[j])
+                    to = ybuf.at[l, slot_of(p, j), :, lanes]
+                    cp.start(("ry", l, p, j), ref, to, to_y[j])
         else:
             for j in (1, 3, 2):
-                cp.landed(("ry", l, ch, j), ybuf.at[l, pl.ds(3 * ch + 2 * (j - 1), 2)])
+                cp.landed(
+                    ("ry", l, p, j), ybuf.at[l, pl.ds(3 * ch + 2 * (j - 1), 2), :, lanes]
+                )
             for i in range(2):
-                total = sib[l, ch, y * 2 + i].astype(F32)
+                total = sib[l, ch, y * 2 + i, :, lanes].astype(F32)
                 for j in range(3):
-                    total = total + ybuf[l, 3 * ch + 2 * j + i].astype(F32)
-                keep[l, ch // 2, i] = total.astype(BF)
-            cp.start(("rx", l, ch, 0), keep.at[l, ch // 2, 1 - x], keep.at[l, ch // 2, 2], to_x)
-
-    def reduce_end(l, ch):
-        if ch == 1:
-            total = xbuf[l, y].astype(F32)
+                    total = total + ybuf[l, 3 * ch + 2 * j + i, :, lanes].astype(F32)
+                keep[l, ch // 2, i, :, lanes] = total.astype(BF)
+            cp.start(
+                ("rx", l, p, 0),
+                keep.at[l, ch // 2, 1 - x, :, lanes],
+                keep.at[l, ch // 2, 2, :, lanes],
+                to_x,
+            )
+
+    def sums_copy(l, p):
+        ch, lanes, _ = REDUCE[p]
+        return cp.make(("rs", p), sbuf.at[l, ch, :, lanes], sbuf_in.at[ch, :, lanes], to_s)
+
+    def reduce_end(l, p):
+        ch, lanes, x_first = REDUCE[p]
+        if x_first:
+            total = xbuf[l, ch - 1, y, :, lanes].astype(F32)
             for j in (1, 3, 2):
-                cp.landed(("ry", l, ch, j), ybuf.at[l, 11 + j])
+                cp.landed(("ry", l, p, j), ybuf.at[l, slot_of(p, j), :, lanes])
             for j in (1, 2, 3):
-                total = total + ybuf[l, 11 + j].astype(F32)
+                total = total + ybuf[l, slot_of(p, j), :, lanes].astype(F32)
         else:
-            cp.landed(("rx", l, ch, 0), keep.at[l, ch // 2, 2])
-            total = keep[l, ch // 2, x].astype(F32) + keep[l, ch // 2, 2].astype(F32)
-        sbuf[l, ch] = total.astype(BF)
+            cp.landed(("rx", l, p, 0), keep.at[l, ch // 2, 2, :, lanes])
+            total = keep[l, ch // 2, x, :, lanes].astype(F32)
+            total = total + keep[l, ch // 2, 2, :, lanes].astype(F32)
+        sbuf[l, ch, :, lanes] = total.astype(BF)
 
         @pl.when(s == 1 - l)
         def _():
-            cp.make(("rs", ch), sbuf.at[l, ch], sbuf_in.at[ch], to_s).start()
+            sums_copy(l, p).start()
 
     def vec_z():
         vland[t, 0:8] = vec[8:16, :]
@@ -635,164 +700,192 @@
         for j in (1, 2, 3):
             cp.start(("vy", j), stage.at[3], vland.at[7 + y], to_y[j])
 
-    @pl.when(s == 1)
-    def _():
-        swapped()
-
-    gather_first(0, 2)
-    prepare()
-    gather_second(0, 2)
+    swap_start(0)
+    swap_wait(0, 2)
     gather_first(0, 0)
     gather_first(0, 1)
+    prepare()
+    gather_second(0, 0)
+    gather_second(0, 1)
+    swap_wait(0, 0)
+    gather_first(0, 2)
+    swap_wait(0, 1)
+    gather_first(0, 3)
+    swap_wait(0, None)
+    swap_start(1)
     fetch_x.wait()
     norms(0, x0, 0)
-    gather_second(0, 0)
     norms(0, x0, 1)
-    gather_third(0, 2)
-    gather_second(0, 1)
-
-    @pl.when(s == 0)
-    def _():
-        swapped()
-
-    gather_fourth(0, 2)
-    project(0, 0)
-    project(0, 1)
-    attend(0, 0)
-    attend(0, 1)
     gather_third(0, 0)
     gather_third(0, 1)
-    gather_first(1, 2)
+    norms(0, x0, 2)
+    norms(0, x0, 3)
+    gather_second(0, 2)
+    gather_second(0, 3)
+    gather_fourth(0, 0)
+    gather_fourth(0, 1)
+    gather_last(0, 0)
+    gather_last(0, 1)
+    project(0, 0, 256)
+    project(0, 256, 256)
+    attend(0, 0)
+    gather_third(0, 2)
+    gather_third(0, 3)
+    swap_wait(1, 2)
     gather_first(1, 0)
     gather_first(1, 1)
+    swap_wait(1, 0)
+    gather_first(1, 2)
+    swap_wait(1, 1)
+    gather_first(1, 3)
+    swap_wait(1, None)
+    attend(0, 1)
+    gather_fourth(0, 2)
+    gather_fourth(0, 3)
     attend(0, 2)
+    gather_second(1, 0)
+    gather_second(1, 1)
     attend(0, 3)
-    gather_fourth(0, 0)
+    gather_second(1, 2)
+    gather_second(1, 3)
+    gather_last(0, 2)
     feed(0, 0)
-    gather_fourth(0, 1)
+    gather_last(0, 3)
     result_rows(0, 0, emit_row(0))
     row_push(0, 0)
-    gather_second(1, 2)
-    gather_second(1, 0)
+    row_push(0, 1)
+    gather_third(1, 0)
+    gather_third(1, 1)
     feed(0, 1)
     result_rows(0, 1, emit_row(0))
-    row_push(0, 1)
-    gather_second(1, 1)
+    row_push(0, 2)
+    row_push(0, 3)
     row_finish(0, 0, x0, 0, x1)
+    row_finish(0, 1, x0, 0, x1)
     gather_third(1, 2)
-    gather_third(1, 0)
-    row_finish(0, 1, x0, 0, x1)
-    gather_third(1, 1)
-    gather_fourth(1, 2)
-    row_wait(0, 0, x1)
-
-    norms(1, x1, 0)
-    project(1, 0)
-    attend(1, 0)
-    attend(1, 1)
-    row_wait(0, 1, x1)
-    norms(1, x1, 1)
-    project(1, 1)
-    attend(1, 2)
-    attend(1, 3)
-    gather_fourth(1, 0)
-    feed(1, 0)
-    feed(1, 1)
-    gather_fourth(1, 1)
-    result_cols(1, 0)
-    col_push(0, 0)
-    col_push(0, 1)
-    pack(x1, acts.at[0, 0])
-    act_push(0, 0, 0)
-    act_push(0, 0, 1)
+    row_finish(0, 2, x0, 0, x1)
+    gather_third(1, 3)
+    row_finish(0, 3, x0, 0, x1)
+    for p in range(4):
+        gather_fourth(1, p)
+    gather_last(1, 0)
+    gather_last(1, 1)
+
+    for i in range(2):
+        row_wait(0, 2 * i, x1)
+        norms(1, x1, 2 * i)
+        row_wait(0, 2 * i + 1, x1)
+        norms(1, x1, 2 * i + 1)
+        project(1, 256 * i, 256)
+        attend(1, 2 * i)
+        attend(1, 2 * i + 1)
+        if i == 0:
+            gather_last(1, 2)
+        feed(1, i)
+    gather_last(1, 3)
 
     fetch_g.wait()
+    back_heads(1, g1, 1)
     back_heads(1, g1, 0)
-    back_heads(1, g1, 1)
-    for j in (3, 2, 1, 0):
-        back_attend(1, j)
-    back_turn()
-    back_norms(1, 0, emit_row(1))
-    row_push(1, 0)
-    back_norms(1, 1, emit_row(1))
-    row_push(1, 1)
+    for i in (1, 0):
+        back_attend(1, 2 * i + 1)
+        back_attend(1, 2 * i)
+        back_turn(2 * i + 1)
+        back_turn(2 * i)
+        back_norms(1, i, emit_row(1))
+        row_push(1, 2 * i + 1)
+        row_push(1, 2 * i)
+    row_finish(1, 3, g1, None, g0)
     weights_of(1, 1, g1)
+    row_finish(1, 2, g1, None, g0)
     weights_of(1, 0, g1)
+    row_finish(1, 1, g1, None, g0)
+    weights_of(1, 2, g1)
     row_finish(1, 0, g1, None, g0)
-    weights_of(1, 2, g1)
     reduce_core(1, 1)
-    row_finish(1, 1, g1, None, g0)
     reduce_core(1, 0)
     sums_of(1, g1)
     reduce_core(1, 2)
-    for i in range(2):
-        col_finish(0, i, acts.at[0, 0], 1, 1, 0)
+    result_cols(1, 0)
+    for i in range(4):
+        col_push(0, i)
+    pack(x1, acts.at[0, 0])
+    for i in range(4):
+        act_push(0, 0, i)
     for ch in range(3):
         weights_gone(1, ch)
 
-    row_wait(1, 0, g0)
-    back_heads(0, g0, 0)
-    row_wait(1, 1, g0)
-    back_heads(0, g0, 1)
-    weights_of(0, 1, g0)
-    weights_of(0, 0, g0)
-    reduce_mid(1, 1)
-    reduce_mid(1, 0)
-    back_attend(0, 3)
-    reduce_mid(1, 2)
-    reduce_core(0, 1)
-    reduce_core(0, 0)
-    back_attend(0, 2)
-    reduce_end(1, 1)
-    reduce_end(1, 0)
-    reduce_end(1, 2)
-    back_attend(0, 1)
-    back_attend(0, 0)
-    back_turn()
-    back_norms(0, 0, emit_full)
-    turn_cols(1, 0)
-    col_push(1, 0)
-    back_norms(0, 1, emit_full)
-    turn_cols(1, 1)
-    col_push(1, 1)
-    pack(g0, acts.at[1, 1])
-    act_push(1, 1, 0)
-    act_push(1, 1, 1)
+    for i in (1, 0):
+        row_wait(1, 2 * i + 1, g0)
+        row_wait(1, 2 * i, g0)
+        back_heads(0, g0, i)
+        if i == 0:
+            weights_of(0, 1, g0)
+            weights_of(0, 0, g0)
+            reduce_mid(1, 1)
+            reduce_mid(1, 2)
+            reduce_mid(1, 3)
+            reduce_core(0, 1)
+            pack(g0, acts.at[1, 1])
+            for n in range(4):
+                act_push(1, 1, n)
+        back_attend(0, 2 * i + 1)
+        if i == 1:
+            reduce_mid(1, 0)
+        else:
+            reduce_core(0, 0)
+        back_attend(0, 2 * i)
+        if i == 1:
+            for n in range(4):
+                col_finish(0, n, acts.at[0, 0], 1, 1, 0)
+        back_turn(2 * i + 1)
+        back_turn(2 * i)
+        back_norms(0, i, emit_full)
+        turn_cols(1, i)
+        col_push(1, 2 * i + 1)
+        col_push(1, 2 * i)
     weights_of(0, 2, g0)
+    for p in range(4):
+        reduce_end(1, p)
     sums_of(0, g0)
     vec_z()
-    reduce_mid(0, 1)
     reduce_core(0, 2)
     vec_c()
     reduce_mid(0, 0)
+    reduce_mid(0, 1)
     vec_x()
+    col_finish(1, 3, acts.at[1, 1], None, 0, 1)
+    col_finish(1, 2, acts.at[1, 1], None, 0, 1)
+    vec_s()
+    reduce_mid(0, 3)
+    reduce_end(0, 1)
+    reduce_mid(0, 2)
+    reduce_end(0, 0)
+    col_finish(1, 1, acts.at[1, 1], None, 0, 1)
     col_finish(1, 0, acts.at[1, 1], None, 0, 1)
-    vec_s()
-    reduce_end(0, 1)
-    reduce_end(0, 0)
-    reduce_mid(0, 2)
-    col_finish(1, 1, acts.at[1, 1], None, 0, 1)
     vec_y()
+    reduce_end(0, 3)
     reduce_end(0, 2)
 
     acts_out[0, s] = acts[s, 0]
     acts_out[1, s] = acts[s, 1]
     for kind in range(2):
-        for i in range(2):
-            cp.landed(("act", kind, i), acts_in.at[kind, :, half_of(i)])
+        for i in range(4):
+            cp.landed(("act", kind, i), acts_in.at[kind, :, part_of(i)])
         acts_out[kind, 1 - s] = acts_in[kind]
     for j in (1, 2, 3):
         cp.landed(("vy", j), vland.at[7 + (y + 4 - j) % 4])
     stage[4] = vland[7] + vland[8] + vland[9] + vland[10]
     vec_out[0:4] = jnp.where(s == 0, stage[4, 0:4], stage[4, 4:8])
     vec_out[4:8] = jnp.where(s == 0, stage[4, 8:12], stage[4, 12:16])
-    for ch in (1, 0, 2):
-        cp.landed(("rs", ch), sbuf_in.at[ch])
-        w_out[ch] = sbuf[s, ch].astype(F32) + sbuf_in[ch].astype(F32)
-        name = ("rs", ch)
-        cp.late(name, cp.make(name, sbuf.at[1 - s, ch], sbuf_in.at[ch], to_s))
+    for p, (ch, lanes, _) in enumerate(REDUCE):
+        cp.landed(("rs", p), sbuf_in.at[ch, :, lanes])
+        w_out[ch, :, lanes] = sbuf[s, ch, :, lanes].astype(F32) + sbuf_in[ch, :, lanes].astype(F32)
+        cp.late(("rs", p), sums_copy(1 - s, p))
+    for name, copy in swap(s):
+        cp.late(name, copy)
     for kind in range(2):
-        for i in range(2):
+        for i in range(4):
             cp.late(("act", kind, i), act_copy(1 - s, kind, i))
     cp.finish()
 
@@ -844,15 +937,15 @@
             f32(SLOT, LOCAL),
             bf(SLOT, D),
             bf(SLOT, D),
-            bf(2, 2, 4, 64, D),
+            bf(2, 4, 4, 32, D),
             bf(2, 4, LOCAL, SLOT),
-            bf(2, 2, 3, 64, D),
+            bf(2, 4, 3, 32, D),
             bf(2, 3, LOCAL, SLOT),
             bf(2, 2, LOCAL, SLOT),
             bf(2, LOCAL, SLOT),
             bf(3, 8, 2, 48, D),
             bf(2, 3, 8, 48, D),
-            bf(2, 4, 48, D),
+            bf(2, 2, 4, 48, D),
             bf(2, 15, 48, D),
             bf(2, 2, 3, 48, D),
             bf(2, 3, 48, D),

time: 144 us -> 138 us (0.958)
  Pallas kernels: 143 us -> 137 us
    pallas_call x1, Pallas kernels: 140 us -> 134 us  [mega(): pl.pallas_call(mega_kernel, out_shape=[jax.ShapeDtypeStruct((2, 2, LOCAL,...]
where the time goes in v4:
time: 138 us
  Pallas kernels  137 us (99%)
    pallas_call x1, Pallas kernels, mega(): pl.pallas_call(mega_kernel, out_shape=[jax.ShapeDtypeStruct((2, 2, LOCAL,...  134 us

profile of v4, /device:TPU:0, one launch (start us, length us, event | category | flops | bytes accessed | tf_op | source)
XLA Modules:
  0.0 137.6 jit_solution(6036740669713697064)
XLA Ops:
  0.6 134.4 %two_layers.1 = (bf16[2,2,192,512]{3,2,1,0:T(8,128)(2,1)}, f32[3,48,768]{2,1,0:T(8,128)}, f32[8,768]{1,0:T(8,128)}) custom-call(s32[2,4]{1,0:T(2,128)} %bitcast.40, f32[1,128]{1,0:T(1,128)} %constant.2.clone.freq_ref, bf16[2,512,768]{2,1,0:T(8,128)(2,1)} %inputs_ref.1, bf16[2,512,768]{2,1,0:T(8,128)(2,1)} %cot_ref.1, bf16[3,48,192]{2,1,0:T(8,128)(2,1)} %bitcast.33, ...), custom_call_target="tpu_custom_call" | custom-call | tf_op jit(solution)/shard_map/two_layers/pallas_call | solution.py:905
  135.1 2.4 %hand_out.1 = (bf16[2,192,512]{2,1,0:T(8,128)(2,1)}, bf16[2,192,512]{2,1,0:T(8,128)(2,1)}, f32[3,48,192]{2,1,0:T(8,128)}, f32[3,1,192]{2,1,0:T(1,128)}, f32[48,1...) custom-call(bf16[2,2,192,512]{3,2,1,0:T(8,128)(2,1)} %get-tuple-elem, ...), custom_call_target="tpu_custom_call" | custom-call | tf_op jit(solution)/shard_map/hand_out/pallas_call | solution.py:986

commit v5 on v4

--- a/solution.py
+++ b/solution.py
@@ -382,18 +382,28 @@
             v[l, h, at, :] = pre[:, 2 * LOCAL + HD * h : 2 * LOCAL + HD * h + HD].astype(BF)
         mixp[l, at, 0:LOCAL] = jnp.zeros((size, LOCAL), BF)
 
-    def attend(l, j):
-        rows = slice(128 * j, 128 * j + 128)
-        seen = slice(0, 128 * j + 128)
+    def attend(l, *blocks):
+        work = [
+            (j, h, slice(128 * j, 128 * j + 128), slice(0, 128 * j + 128))
+            for j in blocks
+            for h in range(3)
+        ]
         scores = [
-            dot_nt(q[l, h, rows, :], k[l, h, seen, :]) + bias[rows, seen] for h in range(3)
+            dot_nt(q[l, h, rows, :], k[l, h, seen, :]) + bias[rows, seen]
+            for _, h, rows, seen in work
         ]
         weights = [jnp.exp(one - jnp.max(one, axis=-1, keepdims=True)) for one in scores]
         shares = [one * (1.0 / jnp.sum(one, axis=-1, keepdims=True)) for one in weights]
-        for h in range(3):
-            probs[l, h, :, stored[j]] = shares[h]
-        outs = [dot(shares[h].astype(BF), v[l, h, seen, :]) for h in range(3)]
-        mixp[l, rows, LOCAL:] = jnp.concatenate(outs, axis=1).astype(BF)
+        for (j, h, _, _), share in zip(work, shares):
+            probs[l, h, :, stored[j]] = share
+        outs = [
+            dot(share.astype(BF), v[l, h, seen, :])
+            for (_, h, _, seen), share in zip(work, shares)
+        ]
+        for n, j in enumerate(blocks):
+            mixp[l, 128 * j : 128 * j + 128, LOCAL:] = jnp.concatenate(
+                outs[3 * n : 3 * n + 3], axis=1
+            ).astype(BF)
 
     def feed(l, i):
         at = slice(256 * i, 256 * i + 256)
@@ -777,8 +787,7 @@
         row_wait(0, 2 * i + 1, x1)
         norms(1, x1, 2 * i + 1)
         project(1, 256 * i, 256)
-        attend(1, 2 * i)
-        attend(1, 2 * i + 1)
+        attend(1, 2 * i, 2 * i + 1)
         if i == 0:
             gather_last(1, 2)
         feed(1, i)

time: 138 us -> 138 us (level)
  no operation moved by 1% of the time
where the time goes in v5:
time: 138 us; the launch traced here: 137 us
  Pallas kernels  137 us (99%)
    pallas_call x1, Pallas kernels, mega(): pl.pallas_call(mega_kernel, out_shape=[jax.ShapeDtypeStruct((2, 2, LOCAL,...  134 us

profile of v5, /device:TPU:0, one launch (start us, length us, event | category | flops | bytes accessed | tf_op | source)
XLA Modules:
  0.0 137.4 jit_solution(17722182401904051061)
XLA Ops:
  0.6 134.2 %two_layers.1 = (bf16[2,2,192,512]{3,2,1,0:T(8,128)(2,1)}, f32[3,48,768]{2,1,0:T(8,128)}, f32[8,768]{1,0:T(8,128)}) custom-call(s32[2,4]{1,0:T(2,128)} %bitcast.40, f32[1,128]{1,0:T(1,128)} %constant.2.clone.freq_ref, bf16[2,512,768]{2,1,0:T(8,128)(2,1)} %inputs_ref.1, bf16[2,512,768]{2,1,0:T(8,128)(2,1)} %cot_ref.1, bf16[3,48,192]{2,1,0:T(8,128)(2,1)} %bitcast.33, ...), custom_call_target="tpu_custom_call" | custom-call | tf_op jit(solution)/shard_map/two_layers/pallas_call | solution.py:914
  134.9 2.4 %hand_out.1 = (bf16[2,192,512]{2,1,0:T(8,128)(2,1)}, bf16[2,192,512]{2,1,0:T(8,128)(2,1)}, f32[3,48,192]{2,1,0:T(8,128)}, f32[3,1,192]{2,1,0:T(1,128)}, f32[48,1...) custom-call(bf16[2,2,192,512]{3,2,1,0:T(8,128)(2,1)} %get-tuple-elem, ...), custom_call_target="tpu_custom_call" | custom-call | tf_op jit(solution)/shard_map/hand_out/pallas_call | solution.py:995
